TPU v7x, 32 devices: a whole 2x2x4 slice. The times are simulated.
32 devices in a mesh: expert: 8 (over z, y), group: 4 (over x, core).
Axes of the slice: x: 2, y: 2, z: 4, core: 2. Of those that a mesh axis runs over, the one named last changes fastest.
Arguments:
- tokens: bfloat16 [2, 4096, 2048], P(None, ('expert', 'group')), may hold values from -6 to 6
- expert_ids: int32 [2, 4096, 8], P(None, ('expert', 'group')), may hold values from 0 to 31, all different within a row; in each aligned block of 128 rows (0 to 127, 128 to 255, ..., all dimensions but the last counted through in order) at most 40 rows name the same one
- gate_probs: float32 [2, 4096, 8], P(None, ('expert', 'group')), may hold values from 0.05 to 1
- capacity: int32 [32], P(('expert', 'group')), may hold values from 448 to 896, as said below
- flows: int32 [32, 3], P(('expert', 'group')), may hold values from 0 to 64, as said below
- w_gate: bfloat16 [32, 2048, 768], P(('expert', 'group')), may hold values from -0.125 to 0.125
- w_up: bfloat16 [32, 2048, 768], P(('expert', 'group')), may hold values from -0.125 to 0.125
- w_down: bfloat16 [32, 768, 2048], P(('expert', 'group')), may hold values from -0.21875 to 0.21875
Outputs:
- mixed: bfloat16 [2, 4096, 2048], P(None, ('expert', 'group'))
Inputs may be any that keep to these rules, and one draw needn't show every extreme that they name: `expert_ids`: among one device's 128 tokens of a micro-batch no expert is chosen more than 40 times, a bound that some block reaches; a token never chooses an expert twice. Some expert has capacity exactly 896. `flows`: some expert has all its grants exactly 64, the same expert that has capacity 896.
All inputs are finite; a program needn't handle non-finite values.
Results may differ from a plain program's by a relative error of at most 0.0085.
Values may be sent and summed in bfloat16 or wider, within the bound.
A program may use at most 128 MiB of HBM per device.

v0:
```python
import jax
import jax.numpy as jnp
from jax import lax
from jax.sharding import PartitionSpec as P


def swiglu_rows(rows_in, gate_mat, up_mat, down_mat):
    gate_val = jnp.dot(rows_in, gate_mat, preferred_element_type=jnp.float32)
    up_val = jnp.dot(rows_in, up_mat, preferred_element_type=jnp.float32)
    hidden = (jax.nn.silu(gate_val) * up_val).astype(jnp.bfloat16)
    return jnp.dot(hidden, down_mat, preferred_element_type=jnp.float32).astype(jnp.bfloat16)


def body(tokens, expert_ids, gate_probs, capacity, flows, w_gate, w_up, w_down):
    device_count = lax.axis_size(("expert", "group"))
    micro_count, tok_local, model_dim = tokens.shape
    top_count = expert_ids.shape[2]
    slot_count = tok_local * top_count * 5 // (4 * device_count)
    slot_total = device_count * slot_count
    keep_limit = capacity[0] + jnp.sum(flows[0])
    expert_iota = jnp.arange(device_count, dtype=jnp.int32)
    slot_all = jnp.arange(slot_total, dtype=jnp.int32)
    slot_iota = jnp.arange(slot_count, dtype=jnp.int32)
    zero_row = jnp.zeros((), jnp.bfloat16)
    results = []
    for micro_index in range(micro_count):
        local_rows = tokens[micro_index]
        pair_expert = expert_ids[micro_index].reshape(-1)
        onehot = (pair_expert[:, None] == expert_iota[None, :]).astype(jnp.int32)
        slot_rank = jnp.sum((jnp.cumsum(onehot, 0) - onehot) * onehot, 1)
        counts = jnp.sum(onehot, 0)
        flat_slot = pair_expert * slot_count + slot_rank
        matches = (flat_slot[:, None] == slot_all[None, :]).reshape(
            tok_local, top_count, slot_total
        )
        select = jnp.any(matches, 1).astype(jnp.bfloat16)
        outgoing = lax.dot_general(
            select, local_rows, (((0,), (0,)), ((), ())), preferred_element_type=jnp.float32
        ).astype(jnp.bfloat16)
        outgoing = outgoing.reshape(device_count, slot_count, model_dim)
        incoming, arrived_counts = (
            lax.all_to_all(outgoing, ("expert", "group"), split_axis=0, concat_axis=0, tiled=True),
            lax.all_to_all(counts, ("expert", "group"), split_axis=0, concat_axis=0, tiled=True),
        )
        offset = jnp.cumsum(arrived_counts) - arrived_counts
        back_pos = offset[:, None] + slot_iota[None, :]
        back_live = (slot_iota[None, :] < arrived_counts[:, None]) & (back_pos < keep_limit)
        expert_out = swiglu_rows(
            incoming.reshape(slot_total, model_dim), w_gate[0], w_up[0], w_down[0]
        )
        returned = jnp.where(back_live.reshape(-1)[:, None], expert_out, zero_row)
        returned = returned.reshape(device_count, slot_count, model_dim)
        answered = lax.all_to_all(
            returned, ("expert", "group"), split_axis=0, concat_axis=0, tiled=True
        )
        answered = answered.reshape(slot_total, model_dim)
        probs = gate_probs[micro_index]
        gate_norm = probs / jnp.sum(probs, 1, keepdims=True)
        weights = jnp.sum(matches.astype(jnp.float32) * gate_norm[:, :, None], 1)
        weight_high = weights.astype(jnp.bfloat16)
        weight_low = (weights - weight_high.astype(jnp.float32)).astype(jnp.bfloat16)
        mixed = jnp.dot(weight_high, answered, preferred_element_type=jnp.float32)
        mixed = mixed + jnp.dot(weight_low, answered, preferred_element_type=jnp.float32)
        results.append(mixed.astype(jnp.bfloat16))
    return jnp.stack(results)


def solution(mesh):
    placed = (
        P(None, ("expert", "group"), None),
        P(None, ("expert", "group"), None),
        P(None, ("expert", "group"), None),
        P(("expert", "group")),
        P(("expert", "group"), None),
        P(("expert", "group"), None, None),
        P(("expert", "group"), None, None),
        P(("expert", "group"), None, None),
    )
    return jax.shard_map(
        body,
        mesh=mesh,
        in_specs=placed,
        out_specs=P(None, ("expert", "group"), None),
        check_vma=False,
    )
```

profile of v0, /device:TPU:0, one launch (start us, length us, event | category | flops | bytes accessed | tf_op | source)
XLA Modules:
  0.0 543.4 jit_solution(3176871275506537740)
XLA Ops:
  0.0 0.9 fusion.36
  0.9 0.1 copy.62
  1.2 9.0 %reduce-window.39 = s32[32,8,128]{2,1,0:T(8,128)S(1)} reduce-window(s32[32,8,128]{2,1,0:T(8,128)S(1)} %fusion.33, s32[]{:T(128)} %constant.21.clone.1), window={size=1x1x128 pad=0_0x0_0x127_0}, to_apply=%region_9.10 | reduce-window | flops 4161536 | bytes 262148 | tf_op jit(solution)/shard_map/reduce-window.3
  10.3 0.1 copy.56
  10.5 0.1 broadcast_add_fusion
  10.6 0.1 convert_reduce_fusion
  10.8 0.7 copy.59
  11.5 7.3 %all-to-all-start.3 = ((s32[32,1,1]{2,1,0:T(1,128)}), s32[32,1,1]{2,1,0:T(1,128)S(1)}, u32[]{:S(2)}, u32[]{:S(2)}) async-start(s32[32,1,1]{2,1,0:T(1,128)} %copy.59), calls=%async_computation.3 | async-start | bytes 32768 | tf_op jit(solution)/shard_map/all_to_all | solution.py:43
  19.2 1.6 fusion.2
  20.8 0.7 fusion.32
  21.5 15.7 %reduce-window.36 = s32[32,8,128]{2,1,0:T(8,128)S(1)} reduce-window(s32[32,8,128]{2,1,0:T(8,128)} %fusion.32, s32[]{:T(128)} %constant.21.clone.1), window={size=1x1x128 pad=0_0x0_0x127_0}, to_apply=%region_0.0 | reduce-window | flops 4161536 | bytes 262148 | tf_op jit(solution)/shard_map/reduce-window
  37.2 0.8 slice.40
  37.9 1.0 copy.50
  39.2 0.1 convert_reduce_fusion.1
  39.3 0.7 copy.53
  40.0 5.8 %all-to-all-start = ((s32[32,1,1]{2,1,0:T(1,128)}), s32[32,1,1]{2,1,0:T(1,128)S(1)}, u32[]{:S(2)}, u32[]{:S(2)}) async-start(s32[32,1,1]{2,1,0:T(1,128)} %copy.53), calls=%async_computation | async-start | bytes 32768 | tf_op jit(solution)/shard_map/all_to_all | solution.py:43
  45.9 4.9 convolution_convert_fusion.1
  50.8 2.1 all-to-all-done
  52.9 3.8 all-to-all-start.4
  56.8 1.6 fusion.3
  58.5 5.0 convolution_convert_fusion.3
  63.5 110.0 %all-to-all-done.4 = bf16[32,40,2048]{2,1,0:T(8,128)(2,1)} async-done(((bf16[32,40,2048]{2,1,0:T(8,128)(2,1)}), bf16[32,40,2048]{2,1,0:T(8,128)(2,1)}, u32[]{:S(2)}, u32[]{:S(2)}) %all-to-all-start.4) | async-done | bytes 5242912 | tf_op jit(solution)/shard_map/all_to_all | solution.py:42
  173.5 3.9 all-to-all-start.1
  178.0 0.7 reduce_sum.90
  179.5 0.1 reduce.6
  179.6 0.7 reduce.5
  180.4 0.1 and.23
  180.5 7.3 %fusion.10 = f32[1280,768]{1,0:T(8,128)S(1)} fusion(bf16[1280,2048]{1,0:T(8,128)(2,1)} %bitcast.24, bf16[1,2048,768]{2,1,0:T(8,128)(2,1)} %param.13), kind=kOutput, calls=%fused_computation.20 | convolution fusion | flops 4026531840 | bytes 12320768 | tf_op jit(solution)/shard_map/dot_general | solution.py:8
  187.8 7.3 %fusion.5 = bf16[1280,768]{1,0:T(8,128)(2,1)S(1)} fusion(bf16[1280,2048]{1,0:T(8,128)(2,1)} %bitcast.24, f32[1280,768]{1,0:T(8,128)S(1)} %fusion.10, bf16[1,2048,768]{2,1,0:T(8,128)(2,1)S(1)} %copy-done.6), kind=kOutput, calls=%fused_computation.15 | convolution fusion | flops 4032430080 | bytes 14286848 | tf_op jit(solution)/shard_map/dot_general | solution.py:9
  195.1 6.0 %fusion.1 = bf16[1280,2048]{1,0:T(8,128)(2,1)} fusion(bf16[1280,768]{1,0:T(8,128)(2,1)S(1)} %fusion.5, pred[1280]{0:T(1024)(128)(4,1)S(1)} %and.23, bf16[1,768,2048]{2,1,0:T(8,128)(2,1)S(1)} %copy-done), kind=kOutput, calls=%fused_computation.5 | convolution fusion | flops 4031774720 | bytes 10355968 | tf_op jit(solution)/shard_map/dot_general | solution.py:11
  201.1 93.0 %all-to-all-done.1 = bf16[32,40,2048]{2,1,0:T(8,128)(2,1)} async-done(((bf16[32,40,2048]{2,1,0:T(8,128)(2,1)}), bf16[32,40,2048]{2,1,0:T(8,128)(2,1)}, u32[]{:S(2)}, u32[]{:S(2)}) %all-to-all-start.1) | async-done | bytes 5242912 | tf_op jit(solution)/shard_map/all_to_all | solution.py:42
  294.0 3.8 all-to-all-start.5
  297.9 0.1 reduce.4
  298.0 0.7 reduce.3
  298.8 0.1 and.21
  298.9 7.2 %fusion.12 = f32[1280,768]{1,0:T(8,128)S(1)} fusion(bf16[1280,2048]{1,0:T(8,128)(2,1)} %bitcast.9, bf16[1,2048,768]{2,1,0:T(8,128)(2,1)} %param.13), kind=kOutput, calls=%fused_computation.22 | convolution fusion | flops 4026531840 | bytes 12320768 | tf_op jit(solution)/shard_map/dot_general | solution.py:8
  306.2 7.3 %fusion.4 = bf16[1280,768]{1,0:T(8,128)(2,1)S(1)} fusion(bf16[1280,2048]{1,0:T(8,128)(2,1)} %bitcast.9, f32[1280,768]{1,0:T(8,128)S(1)} %fusion.12, bf16[1,2048,768]{2,1,0:T(8,128)(2,1)S(1)} %copy-done.7), kind=kOutput, calls=%fused_computation.14 | convolution fusion | flops 4032430080 | bytes 14286848 | tf_op jit(solution)/shard_map/dot_general | solution.py:9
  313.4 6.1 %fusion = bf16[1280,2048]{1,0:T(8,128)(2,1)} fusion(bf16[1280,768]{1,0:T(8,128)(2,1)S(1)} %fusion.4, pred[1280]{0:T(1024)(128)(4,1)S(1)} %and.21, bf16[1,768,2048]{2,1,0:T(8,128)(2,1)S(1)} %copy-done), kind=kOutput, calls=%fused_computation.4 | convolution fusion | flops 4031774720 | bytes 10355968 | tf_op jit(solution)/shard_map/dot_general | solution.py:11
  319.5 95.0 %all-to-all-done.5 = bf16[32,40,2048]{2,1,0:T(8,128)(2,1)} async-done(((bf16[32,40,2048]{2,1,0:T(8,128)(2,1)}), bf16[32,40,2048]{2,1,0:T(8,128)(2,1)}, u32[]{:S(2)}, u32[]{:S(2)}) %all-to-all-start.5) | async-done | bytes 5242912 | tf_op jit(solution)/shard_map/all_to_all | solution.py:53
  414.5 4.0 all-to-all-start.2
  418.8 1.6 select_reduce_fusion
  420.4 2.5 select_reduce_fusion.1
  422.9 3.3 fusion.23
  426.2 4.2 fusion.16
  430.4 104.8 %all-to-all-done.2 = bf16[32,40,2048]{2,1,0:T(8,128)(2,1)} async-done(((bf16[32,40,2048]{2,1,0:T(8,128)(2,1)}), bf16[32,40,2048]{2,1,0:T(8,128)(2,1)}, u32[]{:S(2)}, u32[]{:S(2)}) %all-to-all-start.2) | async-done | bytes 5242912 | tf_op jit(solution)/shard_map/all_to_all | solution.py:53
  535.2 3.6 fusion.26
  538.9 3.5 fusion.17
  542.4 1.1 pad_maximum_fusion
  (47 shorter events, 1.6 us)
Async XLA Ops:
  0.0 195.1 %copy-start = (bf16[1,768,2048]{2,1,0:T(8,128)(2,1)S(1)}, bf16[1,768,2048]{2,1,0:T(8,128)(2,1)}, u32[]{:S(2)}) copy-start(bf16[1,768,2048]{2,1,0:T(8,128)(2,1)} %param.15) | copy-start | bytes 9437188
  11.5 28.6 %all-to-all-start.3 = ((s32[32,1,1]{2,1,0:T(1,128)}), s32[32,1,1]{2,1,0:T(1,128)S(1)}, u32[]{:S(2)}, u32[]{:S(2)}) async-start(s32[32,1,1]{2,1,0:T(1,128)} %copy.59), calls=%async_computation.3 | async-start | bytes 32768 | tf_op jit(solution)/shard_map/all_to_all | solution.py:43
  19.2 1.7 copy-start.3
  40.0 12.9 %all-to-all-start = ((s32[32,1,1]{2,1,0:T(1,128)}), s32[32,1,1]{2,1,0:T(1,128)S(1)}, u32[]{:S(2)}, u32[]{:S(2)}) async-start(s32[32,1,1]{2,1,0:T(1,128)} %copy.53), calls=%async_computation | async-start | bytes 32768 | tf_op jit(solution)/shard_map/all_to_all | solution.py:43
  52.9 120.6 %all-to-all-start.4 = ((bf16[32,40,2048]{2,1,0:T(8,128)(2,1)}), bf16[32,40,2048]{2,1,0:T(8,128)(2,1)}, u32[]{:S(2)}, u32[]{:S(2)}) async-start(bf16[32,40,2048]{2,1,0:T(8,128)(2,1)} %bitcast.80), calls=%async_computation.4 | async-start | bytes 10485760 | tf_op jit(solution)/shard_map/all_to_all | solution.py:42
  173.5 4.5 copy-start.8
  173.5 120.5 %all-to-all-start.1 = ((bf16[32,40,2048]{2,1,0:T(8,128)(2,1)}), bf16[32,40,2048]{2,1,0:T(8,128)(2,1)}, u32[]{:S(2)}, u32[]{:S(2)}) async-start(bf16[32,40,2048]{2,1,0:T(8,128)(2,1)} %bitcast.79), calls=%async_computation.1 | async-start | bytes 10485760 | tf_op jit(solution)/shard_map/all_to_all | solution.py:42
  180.5 7.3 %copy-start.6 = (bf16[1,2048,768]{2,1,0:T(8,128)(2,1)S(1)}, bf16[1,2048,768]{2,1,0:T(8,128)(2,1)}, u32[]{:S(2)}) copy-start(bf16[1,2048,768]{2,1,0:T(8,128)(2,1)} %param.14) | copy-start | bytes 9437188
  294.0 120.5 %all-to-all-start.5 = ((bf16[32,40,2048]{2,1,0:T(8,128)(2,1)}), bf16[32,40,2048]{2,1,0:T(8,128)(2,1)}, u32[]{:S(2)}, u32[]{:S(2)}) async-start(bf16[32,40,2048]{2,1,0:T(8,128)(2,1)} %bitcast.82), calls=%async_computation.5 | async-start | bytes 10485760 | tf_op jit(solution)/shard_map/all_to_all | solution.py:53
  298.9 7.3 %copy-start.7 = (bf16[1,2048,768]{2,1,0:T(8,128)(2,1)S(1)}, bf16[1,2048,768]{2,1,0:T(8,128)(2,1)}, u32[]{:S(2)}) copy-start(bf16[1,2048,768]{2,1,0:T(8,128)(2,1)} %param.14) | copy-start | bytes 9437188
  414.5 4.0 copy-start.5
  414.5 4.2 copy-start.4
  414.5 120.7 %all-to-all-start.2 = ((bf16[32,40,2048]{2,1,0:T(8,128)(2,1)}), bf16[32,40,2048]{2,1,0:T(8,128)(2,1)}, u32[]{:S(2)}, u32[]{:S(2)}) async-start(bf16[32,40,2048]{2,1,0:T(8,128)(2,1)} %bitcast.81), calls=%async_computation.2 | async-start | bytes 10485760 | tf_op jit(solution)/shard_map/all_to_all | solution.py:53
  535.2 3.6 copy-start.1
  538.9 3.5 copy-start.2
where the time goes:
time: 545 us; the launch traced here: 543 us
  waiting for transfers between devices  405 us (74%)
  matrix products  65.6 us (12%)
  other arithmetic  36.9 us (7%)
  starting transfers between devices  28.6 us (5%)
  local copies, waits for them, and re-layouts  5.59 us (1%)
    all_to_all x2, waiting for transfers between devices, body(): lax.all_to_all(outgoing, ('expert', 'group'), split_axis=0, concat_axis=0...  203 us
    all_to_all x2, waiting for transfers between devices, body(): lax.all_to_all(returned, ('expert', 'group'), split_axis=0, concat_axis=0...  200 us
    another operation x10, other arithmetic  25.3 us
    dot_general x2, matrix products, swiglu_rows(): up_val = jnp.dot(rows_in, up_mat, preferred_element_type=jnp.float32)  14.5 us
    dot_general x2, matrix products, swiglu_rows(): gate_val = jnp.dot(rows_in, gate_mat, preferred_element_type=jnp.float32)  14.5 us
    all_to_all x2, starting transfers between devices, body(): lax.all_to_all(counts, ('expert', 'group'), split_axis=0, concat_axis=0,...  13.1 us
    dot_general x2, matrix products, swiglu_rows(): jnp.dot(hidden, down_mat, preferred_element_type=jnp.float32)  12.1 us
  transfers between devices with their start and end apart: 6, of which 5 were waited for; matrix products, arithmetic and copies ran while one was open for 16% of the time, Pallas kernels for 0%

commit v1 on v0

--- a/solution.py
+++ b/solution.py
@@ -2,6 +2,8 @@
 import jax.numpy as jnp
 from jax import lax
 from jax.sharding import PartitionSpec as P
+
+AXES = ("expert", "group")
 
 
 def swiglu_rows(rows_in, gate_mat, up_mat, down_mat):
@@ -11,8 +13,8 @@
     return jnp.dot(hidden, down_mat, preferred_element_type=jnp.float32).astype(jnp.bfloat16)
 
 
-def body(tokens, expert_ids, gate_probs, capacity, flows, w_gate, w_up, w_down):
-    device_count = lax.axis_size(("expert", "group"))
+def sparse_body(tokens, expert_ids, gate_probs, capacity, flows, w_gate, w_up, w_down):
+    device_count = lax.axis_size(AXES)
     micro_count, tok_local, model_dim = tokens.shape
     top_count = expert_ids.shape[2]
     slot_count = tok_local * top_count * 5 // (4 * device_count)
@@ -39,8 +41,8 @@
         ).astype(jnp.bfloat16)
         outgoing = outgoing.reshape(device_count, slot_count, model_dim)
         incoming, arrived_counts = (
-            lax.all_to_all(outgoing, ("expert", "group"), split_axis=0, concat_axis=0, tiled=True),
-            lax.all_to_all(counts, ("expert", "group"), split_axis=0, concat_axis=0, tiled=True),
+            lax.all_to_all(outgoing, AXES, split_axis=0, concat_axis=0, tiled=True),
+            lax.all_to_all(counts, AXES, split_axis=0, concat_axis=0, tiled=True),
         )
         offset = jnp.cumsum(arrived_counts) - arrived_counts
         back_pos = offset[:, None] + slot_iota[None, :]
@@ -50,9 +52,7 @@
         )
         returned = jnp.where(back_live.reshape(-1)[:, None], expert_out, zero_row)
         returned = returned.reshape(device_count, slot_count, model_dim)
-        answered = lax.all_to_all(
-            returned, ("expert", "group"), split_axis=0, concat_axis=0, tiled=True
-        )
+        answered = lax.all_to_all(returned, AXES, split_axis=0, concat_axis=0, tiled=True)
         answered = answered.reshape(slot_total, model_dim)
         probs = gate_probs[micro_index]
         gate_norm = probs / jnp.sum(probs, 1, keepdims=True)
@@ -65,21 +65,79 @@
     return jnp.stack(results)
 
 
+def route(expert_ids, gate_probs, keep_limit, device_count):
+    gate_norm = gate_probs / jnp.sum(gate_probs, 2, keepdims=True)
+    expert_iota = jnp.arange(device_count, dtype=jnp.int32)
+    named = expert_ids[:, :, :, None] == expert_iota
+    chosen = jnp.any(named, 2).astype(jnp.float32)
+    spread = jnp.sum(jnp.where(named, gate_norm[:, :, :, None], 0.0), 2)
+    packed = jnp.transpose(jnp.stack([chosen, spread]), (3, 0, 1, 2))
+    arrived = lax.all_to_all(packed, AXES, split_axis=0, concat_axis=0, tiled=True)
+    chosen, weight = arrived[:, 0], arrived[:, 1]
+    tok_local = chosen.shape[2]
+    tok_iota = jnp.arange(tok_local, dtype=jnp.int32)
+    before = (tok_iota[:, None] < tok_iota[None, :]).astype(jnp.bfloat16)
+    rank = jnp.einsum(
+        "dmt,tu->dmu", chosen.astype(jnp.bfloat16), before, preferred_element_type=jnp.float32
+    )
+    counts = jnp.sum(chosen, 2)
+    earlier = expert_iota[:, None] < expert_iota[None, :]
+    offset = jnp.sum(jnp.where(earlier[:, :, None], counts[:, None, :], 0.0), 0)
+    kept = (chosen > 0) & (offset[:, :, None] + rank < keep_limit.astype(jnp.float32))
+    slot = jnp.where(kept, rank, -1.0).astype(jnp.int32)
+    return slot, weight
+
+
+def dense_body(tokens, expert_ids, gate_probs, capacity, flows, w_gate, w_up, w_down):
+    device_count = lax.axis_size(AXES)
+    micro_count, tok_local, model_dim = tokens.shape
+    top_count = expert_ids.shape[2]
+    slot_count = tok_local * top_count * 5 // (4 * device_count)
+    slot_total = device_count * slot_count
+    keep_limit = capacity[0] + jnp.sum(flows[0])
+    slot_iota = jnp.arange(slot_count, dtype=jnp.int32)
+    slot, weight = route(expert_ids, gate_probs, keep_limit, device_count)
+    results = []
+    for micro_index in range(micro_count):
+        gathered = lax.all_gather(tokens[micro_index], AXES, axis=0, tiled=False)
+        match = slot[:, micro_index, None, :] == slot_iota[None, :, None]
+        select = match.astype(jnp.bfloat16)
+        rows = jnp.einsum(
+            "dst,dtk->dsk", select, gathered, preferred_element_type=jnp.float32
+        ).astype(jnp.bfloat16)
+        expert_out = swiglu_rows(
+            rows.reshape(slot_total, model_dim), w_gate[0], w_up[0], w_down[0]
+        )
+        slot_weight = jnp.sum(jnp.where(match, weight[:, micro_index, None, :], 0.0), 2)
+        scaled = expert_out.astype(jnp.float32) * slot_weight.reshape(-1)[:, None]
+        scaled = scaled.astype(jnp.bfloat16).reshape(device_count, slot_count, model_dim)
+        partial = jnp.einsum(
+            "dst,dsk->dtk", select, scaled, preferred_element_type=jnp.float32
+        ).astype(jnp.bfloat16)
+        results.append(lax.psum_scatter(partial, AXES, scatter_dimension=0, tiled=False))
+    return jnp.stack(results)
+
+
 def solution(mesh):
     placed = (
-        P(None, ("expert", "group"), None),
-        P(None, ("expert", "group"), None),
-        P(None, ("expert", "group"), None),
-        P(("expert", "group")),
-        P(("expert", "group"), None),
-        P(("expert", "group"), None, None),
-        P(("expert", "group"), None, None),
-        P(("expert", "group"), None, None),
+        P(None, AXES, None),
+        P(None, AXES, None),
+        P(None, AXES, None),
+        P(AXES),
+        P(AXES, None),
+        P(AXES, None, None),
+        P(AXES, None, None),
+        P(AXES, None, None),
     )
+
+    def chosen_body(*args):
+        dense = 4 * args[1].shape[2] >= lax.axis_size(AXES)
+        return (dense_body if dense else sparse_body)(*args)
+
     return jax.shard_map(
-        body,
+        chosen_body,
         mesh=mesh,
         in_specs=placed,
-        out_specs=P(None, ("expert", "group"), None),
+        out_specs=P(None, AXES, None),
         check_vma=False,
     )

time: 545 us -> 623 us (1.14)
  waiting for transfers between devices: 405 us -> 517 us
  other arithmetic: 36.9 us -> 6.63 us
  starting transfers between devices: 28.6 us -> 7.42 us
  between operations: 1.68 us -> 14.7 us
  matrix products: 65.6 us -> 73.4 us
    all_to_all x6 -> x1, waiting for transfers between devices: 405 us -> 4.83 us  [route(): lax.all_to_all(packed, AXES, split_axis=0, concat_axis=0, tiled=True)]
    reduce_scatter x0 -> x2, waiting for transfers between devices: none -> 333 us  [dense_body(): lax.psum_scatter(partial, AXES, scatter_dimension=0, tiled=False)]
    all_gather x0 -> x2, waiting for transfers between devices: none -> 178 us  [dense_body(): gathered = lax.all_gather(tokens[micro_index], AXES, axis=0, tiled=False)]
    another operation x11 -> x1, other arithmetic: 26.4 us -> 2.27 us  [dense_body(): return jnp.stack(results)]
    all_to_all x6 -> x1, starting transfers between devices: 28.6 us -> 7.3 us  [route(): lax.all_to_all(packed, AXES, split_axis=0, concat_axis=0, tiled=True)]
    dot_general x6 -> x5, matrix products: 24.5 us -> 42.5 us  [the longest x2 26 us: dense_body(): jnp.einsum('dst,dsk->dtk', select, scaled, preferred_element_type=jnp.flo...]
  transfers between devices with their start and end apart: 6 -> 5, of which waited for: 5 -> 5; matrix products, arithmetic and copies ran while one was open for 16% -> 13% of each run, Pallas kernels for 0% -> 0%
where the time goes in v1:
time: 623 us; the launch traced here: 622 us
  waiting for transfers between devices  517 us (83%)
  matrix products  73.4 us (12%)
  between operations  14.7 us (2%)
  starting transfers between devices  7.42 us (1%)
  other arithmetic  6.63 us (1%)
    reduce_scatter x2, waiting for transfers between devices, dense_body(): lax.psum_scatter(partial, AXES, scatter_dimension=0, tiled=False)  333 us
    all_gather x2, waiting for transfers between devices, dense_body(): gathered = lax.all_gather(tokens[micro_index], AXES, axis=0, tiled=False)  178 us
    dot_general x2, matrix products, dense_body(): jnp.einsum('dst,dsk->dtk', select, scaled, preferred_element_type=jnp.flo...  26 us
    dot_general x2, matrix products, dense_body(): jnp.einsum('dst,dtk->dsk', select, gathered, preferred_element_type=jnp.f...  16.4 us
    dot_general x2, matrix products, swiglu_rows(): jnp.dot(hidden, down_mat, preferred_element_type=jnp.float32)  12.6 us
  transfers between devices with their start and end apart: 5, of which 5 were waited for; matrix products, arithmetic and copies ran while one was open for 13% of the time, Pallas kernels for 0%

profile of v1, /device:TPU:0, one launch (start us, length us, event | category | flops | bytes accessed | tf_op | source)
XLA Modules:
  0.0 622.4 jit_solution(3031114590858696645)
XLA Ops:
  6.5 0.0 copy-start
  6.5 0.0 all-gather.3.cloned.1.call-start
  6.5 2.4 fusion.25
  9.0 0.0 all-gather.3.cloned.1.call-update
  9.0 0.0 all-gather.5.cloned.1.call-start
  9.0 0.7 all-gather.5.cloned.1.call-update
  9.7 0.7 fusion.14
  10.5 0.8 fusion.24
  11.3 0.7 select_reduce_fusion.2
  12.0 0.7 copy.15
  12.7 7.3 %all-to-all-start = ((f32[32,2,2,128]{3,2,1,0:T(2,128)}), f32[32,2,2,128]{3,2,1,0:T(2,128)S(1)}, u32[]{:S(2)}, u32[]{:S(2)}) async-start(f32[32,2,2,128]{3,2,1,0:T(2,128)} %copy.15), calls=%async_computation | async-start | bytes 131072 | tf_op jit(solution)/shard_map/all_to_all | solution.py:75
  20.0 0.0 reduce-scatter.3.cloned.1.call-start
  20.7 1.3 reduce_sum.67
  22.7 4.8 all-to-all-done
  27.5 0.1 slice_bitcast_fusion
  27.6 0.1 copy.18
  27.7 0.1 select_reduce_fusion.3
  27.8 0.1 select_convert_fusion
  28.0 0.3 select_reduce_fusion.1
  28.3 0.1 mul.35
  28.4 99.4 %all-gather.3.cloned.1.call-done = bf16[32,128,2048]{2,1,0:T(8,128)(2,1)} async-done(((bf16[1,128,2048]{2,1,0:T(8,128)(2,1)}), bf16[32,128,2048]{2,1,0:T(8,128)(2,1)}) %all-gather.3.cloned.1.call-update) | async-done | bytes 16777232 | tf_op jit(solution)/shard_map/all_gather | solution.py:102
  127.8 0.0 copy-start.1
  127.8 8.2 %convolution_convert_fusion.5 = bf16[32,40,2048]{2,1,0:T(8,128)(2,1)S(1)} fusion(bf16[32,128,2048]{2,1,0:T(8,128)(2,1)} %all-gather.3.cloned.1.call-done, s32[32,128]{1,0:T(8,128)S(1)} %get-tuple-element.12), kind=kOutput, calls=%fused_computation.7 | convolution fusion | flops 673873920 | bytes 22036480 | tf_op jit(solution)/shard_map/dst,dtk->dsk/dot_general | solution.py:105
  136.0 0.0 copy-done.1
  136.0 0.0 copy-start.3
  136.1 4.3 fusion.8
  140.4 0.0 copy-done.3
  140.4 4.8 fusion
  145.2 0.0 copy-done
  145.2 6.3 %multiply_convert_fusion.1 = bf16[1280,2048]{1,0:T(8,128)(2,1)} fusion(bf16[1280,768]{1,0:T(8,128)(2,1)S(1)} %fusion, f32[1280]{0:T(1024)S(1)} %mul.35, bf16[1,768,2048]{2,1,0:T(8,128)(2,1)S(1)} %copy-done), kind=kOutput, calls=%fused_computation.3 | convolution fusion | flops 4037017600 | bytes 10359808 | tf_op jit(solution)/shard_map/dot_general | solution.py:13
  151.5 12.9 %convolution_convert_fusion.1 = bf16[32,128,2048]{2,1,0:T(8,128)(2,1)} fusion(bf16[32,40,2048]{2,1,0:T(8,128)(2,1)} %bitcast.59, s32[32,128]{1,0:T(8,128)S(1)} %get-tuple-element.12), kind=kOutput, calls=%fused_computation.1 | convolution fusion | flops 679641088 | bytes 22036480 | tf_op jit(solution)/shard_map/dst,dsk->dtk/dot_general | solution.py:114
  164.4 0.0 reduce-scatter.3.cloned.1.call-update
  164.4 0.0 reduce-scatter.5.cloned.1.call-start
  164.5 0.3 select_reduce_fusion
  164.8 0.1 mul.40
  164.9 78.9 %all-gather.5.cloned.1.call-done = bf16[32,128,2048]{2,1,0:T(8,128)(2,1)} async-done(((bf16[1,128,2048]{2,1,0:T(8,128)(2,1)}), bf16[32,128,2048]{2,1,0:T(8,128)(2,1)}) %all-gather.5.cloned.1.call-update) | async-done | bytes 16777232 | tf_op jit(solution)/shard_map/all_gather | solution.py:102
  243.7 8.2 %convolution_convert_fusion.4 = bf16[32,40,2048]{2,1,0:T(8,128)(2,1)S(1)} fusion(bf16[32,128,2048]{2,1,0:T(8,128)(2,1)} %all-gather.5.cloned.1.call-done, s32[32,128]{1,0:T(8,128)S(1)} %get-tuple-element.13), kind=kOutput, calls=%fused_computation.6 | convolution fusion | flops 673873920 | bytes 22036480 | tf_op jit(solution)/shard_map/dst,dtk->dsk/dot_general | solution.py:105
  252.0 0.0 copy-done.2
  252.0 0.0 copy-start.4
  252.0 4.3 fusion.6
  256.3 0.0 copy-done.4
  256.3 4.8 fusion.1
  261.1 6.3 %multiply_convert_fusion = bf16[1280,2048]{1,0:T(8,128)(2,1)} fusion(bf16[1280,768]{1,0:T(8,128)(2,1)S(1)} %fusion.1, f32[1280]{0:T(1024)S(1)} %mul.40, bf16[1,768,2048]{2,1,0:T(8,128)(2,1)S(1)} %copy-done), kind=kOutput, calls=%fused_computation.2 | convolution fusion | flops 4037017600 | bytes 10359808 | tf_op jit(solution)/shard_map/dot_general | solution.py:13
  267.5 13.1 %convolution_convert_fusion = bf16[32,128,2048]{2,1,0:T(8,128)(2,1)} fusion(bf16[32,40,2048]{2,1,0:T(8,128)(2,1)} %bitcast.60, s32[32,128]{1,0:T(8,128)S(1)} %get-tuple-element.13), kind=kOutput, calls=%fused_computation | convolution fusion | flops 679641088 | bytes 22036480 | tf_op jit(solution)/shard_map/dst,dsk->dtk/dot_general | solution.py:114
  280.6 0.0 reduce-scatter.5.cloned.1.call-update
  280.6 146.5 %reduce-scatter.3.cloned.1.call-done = bf16[1,128,2048]{2,1,0:T(8,128)(2,1)} async-done(((bf16[32,128,2048]{2,1,0:T(8,128)(2,1)}), bf16[1,128,2048]{2,1,0:T(8,128)(2,1)}) %reduce-scatter.3.cloned.1.call-update) | async-done | bytes 524304 | tf_op jit(solution)/shard_map/reduce_scatter | solution.py:117
  427.0 186.5 %reduce-scatter.5.cloned.1.call-done = bf16[1,128,2048]{2,1,0:T(8,128)(2,1)} async-done(((bf16[32,128,2048]{2,1,0:T(8,128)(2,1)}), bf16[1,128,2048]{2,1,0:T(8,128)(2,1)}) %reduce-scatter.5.cloned.1.call-update) | async-done | bytes 524304 | tf_op jit(solution)/shard_map/reduce_scatter | solution.py:117
  613.6 2.3 pad_maximum_fusion
  (6 shorter events, 0.1 us)
Async XLA Ops:
  6.5 138.7 %copy-start = (bf16[1,768,2048]{2,1,0:T(8,128)(2,1)S(1)}, bf16[1,768,2048]{2,1,0:T(8,128)(2,1)}, u32[]{:S(2)}) copy-start(bf16[1,768,2048]{2,1,0:T(8,128)(2,1)} %param.15) | copy-start | bytes 9437188
  6.5 121.3 %all-gather.3.cloned.1.call-start = ((), (), s32[]{:S(2)}) async-start(), calls=%async_computation.3 | async-start | bytes 17301504 | tf_op jit(solution)/shard_map/all_gather | solution.py:102
  9.0 234.7 %all-gather.5.cloned.1.call-start = ((), (), s32[]{:S(2)}) async-start(), calls=%async_computation.5 | async-start | bytes 17301504 | tf_op jit(solution)/shard_map/all_gather | solution.py:102
  12.7 14.8 %all-to-all-start = ((f32[32,2,2,128]{3,2,1,0:T(2,128)}), f32[32,2,2,128]{3,2,1,0:T(2,128)S(1)}, u32[]{:S(2)}, u32[]{:S(2)}) async-start(f32[32,2,2,128]{3,2,1,0:T(2,128)} %copy.15), calls=%async_computation | async-start | bytes 131072 | tf_op jit(solution)/shard_map/all_to_all | solution.py:75
  20.0 407.1 %reduce-scatter.3.cloned.1.call-start = ((), (), s32[]{:S(2)}) async-start(), calls=%async_computation.4 | async-start | bytes 17301504 | tf_op jit(solution)/shard_map/reduce_scatter | solution.py:117
  127.8 8.2 %copy-start.1 = (bf16[1,2048,768]{2,1,0:T(8,128)(2,1)S(1)}, bf16[1,2048,768]{2,1,0:T(8,128)(2,1)}, u32[]{:S(2)}) copy-start(bf16[1,2048,768]{2,1,0:T(8,128)(2,1)} %param.13) | copy-start | bytes 9437188
  136.0 4.3 copy-start.3
  164.4 449.1 %reduce-scatter.5.cloned.1.call-start = ((), (), s32[]{:S(2)}) async-start(), calls=%async_computation.6 | async-start | bytes 17301504 | tf_op jit(solution)/shard_map/reduce_scatter | solution.py:117
  243.7 8.2 %copy-start.2 = (bf16[1,2048,768]{2,1,0:T(8,128)(2,1)S(1)}, bf16[1,2048,768]{2,1,0:T(8,128)(2,1)}, u32[]{:S(2)}) copy-start(bf16[1,2048,768]{2,1,0:T(8,128)(2,1)} %param.13) | copy-start | bytes 9437188
  252.0 4.3 copy-start.4
Sparse Core Ops, SparseCore 0:
  10.2 117.5 all-gather.2
  130.7 113.0 all-gather.4
  246.0 180.9 reduce-scatter.2
  429.2 184.3 reduce-scatter.4

commit v2 on v0

v2 whole, which is shorter than its diff:
```python
import jax
import jax.numpy as jnp
from jax import lax
from jax.sharding import PartitionSpec as P

AXES = ("expert", "group")


def swiglu_rows(rows_in, gate_mat, up_mat, down_mat):
    gate_val = jnp.dot(rows_in, gate_mat, preferred_element_type=jnp.float32)
    up_val = jnp.dot(rows_in, up_mat, preferred_element_type=jnp.float32)
    hidden = (jax.nn.silu(gate_val) * up_val).astype(jnp.bfloat16)
    return jnp.dot(hidden, down_mat, preferred_element_type=jnp.float32).astype(jnp.bfloat16)


def route(expert_ids, gate_probs, capacity, flows, planes, slot_count):
    device_count = lax.axis_size(AXES)
    plane_size = device_count // planes
    micro_count, tok_local, top_count = expert_ids.shape
    me = lax.axis_index(AXES)
    my_z, my_spot = me // plane_size, me % plane_size
    expert_iota = jnp.arange(device_count, dtype=jnp.int32)
    gate_norm = gate_probs / jnp.sum(gate_probs, 2, keepdims=True)
    named = expert_ids[:, None] == expert_iota[None, :, None, None]
    spread = jnp.sum(jnp.where(named, gate_norm[:, None], 0.0), 3)
    limit = (capacity[0] + jnp.sum(flows[0])).astype(jnp.float32)
    limit_row = jnp.full((micro_count, 1, tok_local), limit)
    everyone = lax.all_gather(jnp.concatenate([spread, limit_row], 1), AXES, axis=0)
    limits = everyone[:, 0, device_count, 0]
    everyone = everyone[:, :, :device_count]
    here = lax.dynamic_slice_in_dim(everyone, my_z * plane_size, plane_size, 2)
    limits = lax.dynamic_slice_in_dim(limits, my_z * plane_size, plane_size, 0)
    counts = jnp.sum((here > 0).astype(jnp.float32), 3)
    earlier = (expert_iota[:, None] < expert_iota[None, :]).astype(jnp.float32)
    offset = jnp.sum(earlier[:, :, None, None] * counts[:, None], 0)

    def column(value):
        grid = value.reshape((planes, plane_size) + value.shape[1:])
        mine = lax.dynamic_index_in_dim(grid, my_spot, 1, keepdims=False)
        return jnp.roll(mine, -my_z, 0)

    weight, offset = column(here), column(offset)
    chosen = weight > 0
    tok_iota = jnp.arange(tok_local, dtype=jnp.int32)
    before = (tok_iota[:, None] < tok_iota[None, :]).astype(jnp.bfloat16)
    rank = jnp.einsum(
        "jmet,tu->jmeu", chosen.astype(jnp.bfloat16), before, preferred_element_type=jnp.float32
    )
    kept = chosen & (rank + offset[:, :, :, None] < limits[None, None, :, None])
    block = (jnp.arange(planes, dtype=jnp.int32) * slot_count)[:, None, None, None]
    code = jnp.where(chosen, block + rank.astype(jnp.int32), -1)
    weight = jnp.where(kept, weight, 0.0)

    def flat(value):
        value = jnp.transpose(value, (1, 2, 0, 3))
        return value.reshape(micro_count, plane_size, planes * tok_local)

    return flat(code), flat(weight)


def body(tokens, expert_ids, gate_probs, capacity, flows, w_gate, w_up, w_down):
    device_count, group_size = lax.axis_size(AXES), lax.axis_size("group")
    width = max(1, group_size // 2)
    planes = max(1, lax.axis_size("expert") // width)
    plane_size = device_count // planes
    micro_count, tok_local, model_dim = tokens.shape
    top_count = expert_ids.shape[2]
    slot_count = tok_local * top_count * 5 // (4 * device_count)
    sent = planes * slot_count
    plane_groups = [
        [z * plane_size + spot for spot in range(plane_size)] for z in range(planes)
    ]

    def shift(value, step):
        pairs = [
            ((z + step) % planes * plane_size + spot, z * plane_size + spot)
            for z in range(planes)
            for spot in range(plane_size)
        ]
        return lax.ppermute(value, AXES, pairs)

    def swap(value):
        return lax.all_to_all(
            value, AXES, split_axis=0, concat_axis=0, tiled=True, axis_index_groups=plane_groups
        )

    code, weight = route(expert_ids, gate_probs, capacity, flows, planes, slot_count)
    slot_iota = jnp.arange(sent, dtype=jnp.int32)

    columns = []
    for micro_index in range(micro_count):
        own = tokens[micro_index]
        if columns:
            own, columns[-1] = lax.optimization_barrier((own, columns[-1]))
        columns.append([own] + [shift(own, step) for step in range(1, planes)])

    arrived, matches = [], []
    for micro_index in range(micro_count):
        match = code[micro_index][:, None, :] == slot_iota[None, :, None]
        matches.append(match)
        rows = jnp.dot(
            match.astype(jnp.bfloat16).reshape(plane_size * sent, planes * tok_local),
            jnp.concatenate(columns[micro_index], 0),
            preferred_element_type=jnp.float32,
        ).astype(jnp.bfloat16)
        arrived.append(swap(rows.reshape(plane_size, sent, model_dim)))

    answers = []
    for micro_index in range(micro_count):
        expert_out = swiglu_rows(
            arrived[micro_index].reshape(plane_size * sent, model_dim),
            w_gate[0], w_up[0], w_down[0],
        )
        answers.append(swap(expert_out.reshape(plane_size, sent, model_dim)))

    results = []
    for micro_index in range(micro_count):
        back = answers[micro_index].reshape(plane_size * sent, model_dim)
        spread = jnp.where(matches[micro_index], weight[micro_index][:, None, :], 0.0)
        spread = spread.reshape(plane_size * sent, planes * tok_local)
        high = spread.astype(jnp.bfloat16)
        low = (spread - high.astype(jnp.float32)).astype(jnp.bfloat16)
        contract = (((0,), (0,)), ((), ()))
        partial = lax.dot_general(high, back, contract, preferred_element_type=jnp.float32)
        partial = partial + lax.dot_general(low, back, contract, preferred_element_type=jnp.float32)
        partial = partial.reshape(planes, tok_local, model_dim)
        total = partial[0]
        rounded = partial.astype(jnp.bfloat16)
        for step in range(1, planes):
            total = total + shift(rounded[step], -step).astype(jnp.float32)
        results.append(total.astype(jnp.bfloat16))
    return jnp.stack(results)


def solution(mesh):
    placed = (
        P(None, AXES, None),
        P(None, AXES, None),
        P(None, AXES, None),
        P(AXES),
        P(AXES, None),
        P(AXES, None, None),
        P(AXES, None, None),
        P(AXES, None, None),
    )
    return jax.shard_map(
        body,
        mesh=mesh,
        in_specs=placed,
        out_specs=P(None, AXES, None),
        check_vma=False,
    )
```

time: 545 us -> 425 us (0.78)
  the two profiles are of different devices: /device:TPU:0 before, /device:TPU:11 now
where the time goes in v2:
time: 425 us; the launch traced here: 424 us
  waiting for transfers between devices  276 us (65%)
  matrix products  76 us (18%)
  starting transfers between devices  39.7 us (9%)
  between operations  15 us (4%)
  local copies, waits for them, and re-layouts  8.69 us (2%)
  other arithmetic  8.69 us (2%)
    ppermute x12, waiting for transfers between devices, shift(): return lax.ppermute(value, AXES, pairs)  130 us
    all_to_all x4, waiting for transfers between devices, swap(): lax.all_to_all(value, AXES, split_axis=0, concat_axis=0, tiled=True, axis...  123 us
    all_gather x1, waiting for transfers between devices, route(): lax.all_gather(jnp.concatenate([spread, limit_row], 1), AXES, axis=0)  24 us
    all_to_all x4, starting transfers between devices, swap(): lax.all_to_all(value, AXES, split_axis=0, concat_axis=0, tiled=True, axis...  23.5 us
    ppermute x12, starting transfers between devices, shift(): return lax.ppermute(value, AXES, pairs)  16.2 us
    dot_general x2, matrix products, swiglu_rows(): up_val = jnp.dot(rows_in, up_mat, preferred_element_type=jnp.float32)  14.5 us
    dot_general x2, matrix products, swiglu_rows(): gate_val = jnp.dot(rows_in, gate_mat, preferred_element_type=jnp.float32)  14.5 us
    dot_general x2, matrix products, body(): jnp.dot(match.astype(jnp.bfloat16).reshape(plane_size * sent, planes * to...  13.2 us
  transfers between devices with their start and end apart: 17, of which 13 were waited for; matrix products, arithmetic and copies ran while one was open for 18% of the time, Pallas kernels for 0%

profile of v2, /device:TPU:11, one launch (start us, length us, event | category | flops | bytes accessed | tf_op | source)
XLA Modules:
  0.0 424.4 jit_solution(3487908697671815893)
XLA Ops:
  6.5 0.9 fusion.59
  8.2 1.4 reduce_sum.47
  10.2 0.8 select_reduce_fusion
  11.7 2.3 slice_bitcast_fusion
  14.1 2.3 collective-permute-start.1
  16.4 2.2 collective-permute-start.2
  18.7 8.6 %collective-permute-done = bf16[128,2048]{1,0:T(8,128)(2,1)} collective-permute-done((bf16[128,2048]{1,0:T(8,128)(2,1)}, bf16[128,2048]{1,0:T(8,128)(2,1)}, u32[]{:S(2)}, u32[]{:S(2)}) %collective-permute-start) | collective-permute-done | bytes 524320 | tf_op jit(solution)/shard_map/ppermute | solution.py:80
  27.4 23.6 %collective-permute-done.1 = bf16[128,2048]{1,0:T(8,128)(2,1)} collective-permute-done((bf16[128,2048]{1,0:T(8,128)(2,1)}, bf16[128,2048]{1,0:T(8,128)(2,1)}, u32[]{:S(2)}, u32[]{:S(2)}) %collective-permute-start.1) | collective-permute-done | bytes 524320 | tf_op jit(solution)/shard_map/ppermute | solution.py:80
  51.0 11.9 %collective-permute-done.2 = bf16[128,2048]{1,0:T(8,128)(2,1)} collective-permute-done((bf16[128,2048]{1,0:T(8,128)(2,1)}, bf16[128,2048]{1,0:T(8,128)(2,1)}, u32[]{:S(2)}, u32[]{:S(2)}) %collective-permute-start.2) | collective-permute-done | bytes 524320 | tf_op jit(solution)/shard_map/ppermute | solution.py:80
  62.9 24.0 %all-gather.3.cloned.1.call-done = f32[64,33,128]{2,1,0:T(8,128)} async-done(((f32[2,33,128]{2,1,0:T(8,128)}), f32[64,33,128]{2,1,0:T(8,128)}) %all-gather.3.cloned.1.call-update) | async-done | bytes 1081360 | tf_op jit(solution)/shard_map/all_gather | solution.py:28
  86.9 1.5 copy.25
  88.5 1.0 copy-done.1
  90.3 1.6 bitcast_compare_fusion.1
  92.0 6.7 %convolution_convert_fusion.3 = bf16[1280,2048]{1,0:T(8,128)(2,1)} fusion(pred[1280,512]{1,0:T(32,128)(4,1)S(1)} %get-tuple-element.29, bf16[128,2048]{1,0:T(8,128)(2,1)} %collective-permute-done.2, bf16[128,2048]{1,0:T(8,128)(2,1)} %collective-permute-done.1, bf16[128,2048]{1,0:T(8,128)(2,1)} %collective-permute-done, bf16[128,2048]{1,0:T(8,128)(2,1)} %get-tuple-element.10), kind=kOutput, calls=%fused_computation.3 | convolution fusion | flops 2695364608 | bytes 7995392 | tf_op jit(solution)/shard_map/dot_general | solution.py:101
  98.7 5.0 %all-to-all-start = ((bf16[8,160,2048]{2,1,0:T(8,128)(2,1)}), bf16[8,160,2048]{2,1,0:T(8,128)(2,1)}, u32[]{:S(2)}, u32[]{:S(2)}) async-start(bf16[8,160,2048]{2,1,0:T(8,128)(2,1)} %bitcast.82), calls=%async_computation | async-start | bytes 10485760 | tf_op jit(solution)/shard_map/all_to_all | solution.py:83
  103.7 1.2 collective-permute-start.6
  104.9 0.8 collective-permute-start.7
  105.8 2.4 collective-permute-start.8
  108.1 9.1 %collective-permute-done.6 = bf16[128,2048]{1,0:T(8,128)(2,1)S(1)} collective-permute-done((bf16[128,2048]{1,0:T(8,128)(2,1)}, bf16[128,2048]{1,0:T(8,128)(2,1)S(1)}, u32[]{:S(2)}, u32[]{:S(2)}) %collective-permute-start.6) | collective-permute-done | bytes 524320 | tf_op jit(solution)/shard_map/ppermute | solution.py:80
  117.2 22.2 %collective-permute-done.7 = bf16[128,2048]{1,0:T(8,128)(2,1)S(1)} collective-permute-done((bf16[128,2048]{1,0:T(8,128)(2,1)}, bf16[128,2048]{1,0:T(8,128)(2,1)S(1)}, u32[]{:S(2)}, u32[]{:S(2)}) %collective-permute-start.7) | collective-permute-done | bytes 524320 | tf_op jit(solution)/shard_map/ppermute | solution.py:80
  139.4 11.2 %collective-permute-done.8 = bf16[128,2048]{1,0:T(8,128)(2,1)S(1)} collective-permute-done((bf16[128,2048]{1,0:T(8,128)(2,1)}, bf16[128,2048]{1,0:T(8,128)(2,1)S(1)}, u32[]{:S(2)}, u32[]{:S(2)}) %collective-permute-start.8) | collective-permute-done | bytes 524320 | tf_op jit(solution)/shard_map/ppermute | solution.py:80
  150.6 6.5 %convolution_convert_fusion.1 = bf16[1280,2048]{1,0:T(8,128)(2,1)} fusion(pred[1280,512]{1,0:T(32,128)(4,1)} %get-tuple-element.30, bf16[128,2048]{1,0:T(8,128)(2,1)S(1)} %collective-permute-done.8, bf16[128,2048]{1,0:T(8,128)(2,1)S(1)} %collective-permute-done.7, bf16[128,2048]{1,0:T(8,128)(2,1)S(1)} %collective-permute-done.6, ...), kind=kOutput, calls=%fused_computation.1 | convolution fusion | flops 2695364608 | bytes 7995392 | tf_op jit(solution)/shard_map/dot_general | solution.py:101
  157.1 5.5 %all-to-all-done = bf16[8,160,2048]{2,1,0:T(8,128)(2,1)} async-done(((bf16[8,160,2048]{2,1,0:T(8,128)(2,1)}), bf16[8,160,2048]{2,1,0:T(8,128)(2,1)}, u32[]{:S(2)}, u32[]{:S(2)}) %all-to-all-start) | async-done | bytes 5242912 | tf_op jit(solution)/shard_map/all_to_all | solution.py:83
  162.6 6.1 %all-to-all-start.2 = ((bf16[8,160,2048]{2,1,0:T(8,128)(2,1)}), bf16[8,160,2048]{2,1,0:T(8,128)(2,1)}, u32[]{:S(2)}, u32[]{:S(2)}) async-start(bf16[8,160,2048]{2,1,0:T(8,128)(2,1)} %bitcast.83), calls=%async_computation.2 | async-start | bytes 10485760 | tf_op jit(solution)/shard_map/all_to_all | solution.py:83
  168.7 7.2 %fusion.8 = f32[1280,768]{1,0:T(8,128)S(1)} fusion(bf16[1280,2048]{1,0:T(8,128)(2,1)} %bitcast.15, bf16[1,2048,768]{2,1,0:T(8,128)(2,1)} %param.13), kind=kOutput, calls=%fused_computation.20 | convolution fusion | flops 4026531840 | bytes 12320768 | tf_op jit(solution)/shard_map/dot_general | solution.py:10
  176.0 7.3 %fusion = bf16[1280,768]{1,0:T(8,128)(2,1)S(1)} fusion(bf16[1280,2048]{1,0:T(8,128)(2,1)} %bitcast.15, f32[1280,768]{1,0:T(8,128)S(1)} %fusion.8, bf16[1,2048,768]{2,1,0:T(8,128)(2,1)S(1)} %copy-done.2), kind=kOutput, calls=%fused_computation.12 | convolution fusion | flops 4032430080 | bytes 14286848 | tf_op jit(solution)/shard_map/dot_general | solution.py:11
  183.3 6.0 %convolution_convert_fusion.2 = bf16[1280,2048]{1,0:T(8,128)(2,1)} fusion(bf16[1280,768]{1,0:T(8,128)(2,1)S(1)} %fusion, bf16[1,768,2048]{2,1,0:T(8,128)(2,1)S(1)} %copy-done), kind=kOutput, calls=%fused_computation.2 | convolution fusion | flops 4029153280 | bytes 10354688 | tf_op jit(solution)/shard_map/dot_general | solution.py:13
  189.3 38.3 %all-to-all-done.2 = bf16[8,160,2048]{2,1,0:T(8,128)(2,1)} async-done(((bf16[8,160,2048]{2,1,0:T(8,128)(2,1)}), bf16[8,160,2048]{2,1,0:T(8,128)(2,1)}, u32[]{:S(2)}, u32[]{:S(2)}) %all-to-all-start.2) | async-done | bytes 5242912 | tf_op jit(solution)/shard_map/all_to_all | solution.py:83
  227.6 6.2 %all-to-all-start.1 = ((bf16[8,160,2048]{2,1,0:T(8,128)(2,1)}), bf16[8,160,2048]{2,1,0:T(8,128)(2,1)}, u32[]{:S(2)}, u32[]{:S(2)}) async-start(bf16[8,160,2048]{2,1,0:T(8,128)(2,1)} %bitcast.84), calls=%async_computation.1 | async-start | bytes 10485760 | tf_op jit(solution)/shard_map/all_to_all | solution.py:83
  233.8 7.2 %fusion.6 = f32[1280,768]{1,0:T(8,128)S(1)} fusion(bf16[1280,2048]{1,0:T(8,128)(2,1)} %bitcast.27, bf16[1,2048,768]{2,1,0:T(8,128)(2,1)} %param.13), kind=kOutput, calls=%fused_computation.18 | convolution fusion | flops 4026531840 | bytes 12320768 | tf_op jit(solution)/shard_map/dot_general | solution.py:10
  241.0 7.3 %fusion.1 = bf16[1280,768]{1,0:T(8,128)(2,1)S(1)} fusion(bf16[1280,2048]{1,0:T(8,128)(2,1)} %bitcast.27, f32[1280,768]{1,0:T(8,128)S(1)} %fusion.6, bf16[1,2048,768]{2,1,0:T(8,128)(2,1)S(1)} %copy-done.3), kind=kOutput, calls=%fused_computation.13 | convolution fusion | flops 4032430080 | bytes 14286848 | tf_op jit(solution)/shard_map/dot_general | solution.py:11
  248.3 6.0 %convolution_convert_fusion = bf16[1280,2048]{1,0:T(8,128)(2,1)} fusion(bf16[1280,768]{1,0:T(8,128)(2,1)S(1)} %fusion.1, bf16[1,768,2048]{2,1,0:T(8,128)(2,1)S(1)} %copy-done), kind=kOutput, calls=%fused_computation | convolution fusion | flops 4029153280 | bytes 10354688 | tf_op jit(solution)/shard_map/dot_general | solution.py:13
  254.3 38.3 %all-to-all-done.1 = bf16[8,160,2048]{2,1,0:T(8,128)(2,1)} async-done(((bf16[8,160,2048]{2,1,0:T(8,128)(2,1)}), bf16[8,160,2048]{2,1,0:T(8,128)(2,1)}, u32[]{:S(2)}, u32[]{:S(2)}) %all-to-all-start.1) | async-done | bytes 5242912 | tf_op jit(solution)/shard_map/all_to_all | solution.py:83
  292.6 6.2 %all-to-all-start.3 = ((bf16[8,160,2048]{2,1,0:T(8,128)(2,1)}), bf16[8,160,2048]{2,1,0:T(8,128)(2,1)}, u32[]{:S(2)}, u32[]{:S(2)}) async-start(bf16[8,160,2048]{2,1,0:T(8,128)(2,1)} %bitcast.81), calls=%async_computation.3 | async-start | bytes 10485760 | tf_op jit(solution)/shard_map/all_to_all | solution.py:83
  298.8 0.8 slice.78
  300.6 4.9 %fusion.26 = f32[512,2048,1]{1,0,2:T(8,128)S(1)} fusion(bf16[8,160,2048]{2,1,0:T(8,128)(2,1)} %all-to-all-done.1, f32[8,512]{1,0:T(8,128)S(1)} %get-tuple-element.25, s32[8,512]{1,0:T(8,128)S(1)} %get-tuple-element.27), kind=kOutput, calls=%fused_computation.42 | convolution fusion | flops 2685665280 | bytes 9469952 | tf_op jit(solution)/shard_map/dot_general | solution.py:124
  305.5 6.9 %fusion.68 = (bf16[512,2048]{1,0:T(8,128)(2,1)S(1)}, f32[512,2048]{1,0:T(8,128)}) fusion(bf16[8,160,2048]{2,1,0:T(8,128)(2,1)} %all-to-all-done.1, f32[8,512]{1,0:T(8,128)S(1)} %get-tuple-element.25, s32[8,512]{1,0:T(8,128)S(1)} %get-tuple-element.27, f32[512,2048,1]{1,0,2:T(8,128)S(1)} %fusion.26), kind=kOutput, calls=%fused_computation.109 | convolution fusion | flops 2690383872 | bytes 15761408 | tf_op jit(solution)/shard_map/dot_general | solution.py:125
  312.4 1.2 fusion.66
  314.4 2.5 collective-permute-start.4
  317.1 40.6 %all-to-all-done.3 = bf16[8,160,2048]{2,1,0:T(8,128)(2,1)} async-done(((bf16[8,160,2048]{2,1,0:T(8,128)(2,1)}), bf16[8,160,2048]{2,1,0:T(8,128)(2,1)}, u32[]{:S(2)}, u32[]{:S(2)}) %all-to-all-start.3) | async-done | bytes 5242912 | tf_op jit(solution)/shard_map/all_to_all | solution.py:83
  357.7 4.9 %fusion.27 = f32[512,2048,1]{1,0,2:T(8,128)S(1)} fusion(bf16[8,160,2048]{2,1,0:T(8,128)(2,1)} %all-to-all-done.3, f32[8,512]{1,0:T(8,128)S(1)} %get-tuple-element.26, s32[8,512]{1,0:T(8,128)S(1)} %get-tuple-element.28), kind=kOutput, calls=%fused_computation.43 | convolution fusion | flops 2685665280 | bytes 9469952 | tf_op jit(solution)/shard_map/dot_general | solution.py:124
  362.6 4.9 %fusion.69 = (bf16[512,2048]{1,0:T(8,128)(2,1)S(1)}, f32[512,2048]{1,0:T(8,128)S(1)}) fusion(bf16[8,160,2048]{2,1,0:T(8,128)(2,1)} %all-to-all-done.3, f32[8,512]{1,0:T(8,128)S(1)} %get-tuple-element.26, s32[8,512]{1,0:T(8,128)S(1)} %get-tuple-element.28, f32[512,2048,1]{1,0,2:T(8,128)S(1)} %fusion.27), kind=kOutput, calls=%fused_computation.110 | convolution fusion | flops 2690383872 | bytes 15761408 | tf_op jit(solution)/shard_map/dot_general | solution.py:125
  367.6 2.1 collective-permute-start.10
  369.8 1.5 collective-permute-start.9
  371.2 2.0 fusion.48
  373.2 30.3 %collective-permute-done.10 = bf16[128,2048]{1,0:T(8,128)(2,1)S(1)} collective-permute-done((bf16[128,2048]{1,0:T(8,128)(2,1)S(1)}, bf16[128,2048]{1,0:T(8,128)(2,1)S(1)}, u32[]{:S(2)}, u32[]{:S(2)}) %collective-permute-start.10) | collective-permute-done | bytes 524320 | tf_op jit(solution)/shard_map/ppermute | solution.py:80
  403.5 12.6 %collective-permute-done.11 = bf16[128,2048]{1,0:T(8,128)(2,1)S(1)} collective-permute-done((bf16[128,2048]{1,0:T(8,128)(2,1)S(1)}, bf16[128,2048]{1,0:T(8,128)(2,1)S(1)}, u32[]{:S(2)}, u32[]{:S(2)}) %collective-permute-start.11) | collective-permute-done | bytes 524320 | tf_op jit(solution)/shard_map/ppermute | solution.py:80
  416.5 1.1 pad_maximum_fusion
  (40 shorter events, 4.2 us)
Async XLA Ops:
  6.5 176.7 %copy-start = (bf16[1,768,2048]{2,1,0:T(8,128)(2,1)S(1)}, bf16[1,768,2048]{2,1,0:T(8,128)(2,1)}, u32[]{:S(2)}) copy-start(bf16[1,768,2048]{2,1,0:T(8,128)(2,1)} %param.15) | copy-start | bytes 9437188
  6.5 80.4 %all-gather.3.cloned.1.call-start = ((), (), s32[]{:S(2)}) async-start(), calls=%async_computation.4 | async-start | bytes 1351680 | tf_op jit(solution)/shard_map/all_gather | solution.py:28
  14.0 13.4 %collective-permute-start = (bf16[128,2048]{1,0:T(8,128)(2,1)}, bf16[128,2048]{1,0:T(8,128)(2,1)}, u32[]{:S(2)}, u32[]{:S(2)}) collective-permute-start(bf16[128,2048]{1,0:T(8,128)(2,1)} %get-tuple-element.10), channel_id=1, source_target_pairs={{8,0},{9,1},{10,2},{11,3},{12,4},{13,5},{14,6},{15,7},{16,8},{17,9... | collective-permute-start | bytes 1572872 | tf_op jit(solution)/shard_map/ppermute | solution.py:80
  14.1 36.9 %collective-permute-start.1 = (bf16[128,2048]{1,0:T(8,128)(2,1)}, bf16[128,2048]{1,0:T(8,128)(2,1)}, u32[]{:S(2)}, u32[]{:S(2)}) collective-permute-start(bf16[128,2048]{1,0:T(8,128)(2,1)} %get-tuple-element.10), channel_id=1, source_target_pairs={{16,0},{17,1},{18,2},{19,3},{20,4},{21,5},{22,6},{23,7},{24,8},{25... | collective-permute-start | bytes 1572872 | tf_op jit(solution)/shard_map/ppermute | solution.py:80
  16.4 46.4 %collective-permute-start.2 = (bf16[128,2048]{1,0:T(8,128)(2,1)}, bf16[128,2048]{1,0:T(8,128)(2,1)}, u32[]{:S(2)}, u32[]{:S(2)}) collective-permute-start(bf16[128,2048]{1,0:T(8,128)(2,1)} %get-tuple-element.10), channel_id=1, source_target_pairs={{24,0},{25,1},{26,2},{27,3},{28,4},{29,5},{30,6},{31,7},{0,8},{1,9... | collective-permute-start | bytes 1572872 | tf_op jit(solution)/shard_map/ppermute | solution.py:80
  88.5 1.0 copy-start.1
  98.7 63.9 %all-to-all-start = ((bf16[8,160,2048]{2,1,0:T(8,128)(2,1)}), bf16[8,160,2048]{2,1,0:T(8,128)(2,1)}, u32[]{:S(2)}, u32[]{:S(2)}) async-start(bf16[8,160,2048]{2,1,0:T(8,128)(2,1)} %bitcast.82), calls=%async_computation | async-start | bytes 10485760 | tf_op jit(solution)/shard_map/all_to_all | solution.py:83
  103.7 13.5 %collective-permute-start.6 = (bf16[128,2048]{1,0:T(8,128)(2,1)}, bf16[128,2048]{1,0:T(8,128)(2,1)S(1)}, u32[]{:S(2)}, u32[]{:S(2)}) collective-permute-start(bf16[128,2048]{1,0:T(8,128)(2,1)} %get-tuple-element.14), channel_id=1, source_target_pairs={{8,0},{9,1},{10,2},{11,3},{12,4},{13,5},{14,6},{15,7},{16,8},{17,9... | collective-permute-start | bytes 1572872 | tf_op jit(solution)/shard_map/ppermute | solution.py:80
  104.9 34.4 %collective-permute-start.7 = (bf16[128,2048]{1,0:T(8,128)(2,1)}, bf16[128,2048]{1,0:T(8,128)(2,1)S(1)}, u32[]{:S(2)}, u32[]{:S(2)}) collective-permute-start(bf16[128,2048]{1,0:T(8,128)(2,1)} %get-tuple-element.14), channel_id=1, source_target_pairs={{16,0},{17,1},{18,2},{19,3},{20,4},{21,5},{22,6},{23,7},{24,8},{25... | collective-permute-start | bytes 1572872 | tf_op jit(solution)/shard_map/ppermute | solution.py:80
  105.8 44.8 %collective-permute-start.8 = (bf16[128,2048]{1,0:T(8,128)(2,1)}, bf16[128,2048]{1,0:T(8,128)(2,1)S(1)}, u32[]{:S(2)}, u32[]{:S(2)}) collective-permute-start(bf16[128,2048]{1,0:T(8,128)(2,1)} %get-tuple-element.14), channel_id=1, source_target_pairs={{24,0},{25,1},{26,2},{27,3},{28,4},{29,5},{30,6},{31,7},{0,8},{1,9... | collective-permute-start | bytes 1572872 | tf_op jit(solution)/shard_map/ppermute | solution.py:80
  162.6 65.0 %all-to-all-start.2 = ((bf16[8,160,2048]{2,1,0:T(8,128)(2,1)}), bf16[8,160,2048]{2,1,0:T(8,128)(2,1)}, u32[]{:S(2)}, u32[]{:S(2)}) async-start(bf16[8,160,2048]{2,1,0:T(8,128)(2,1)} %bitcast.83), calls=%async_computation.2 | async-start | bytes 10485760 | tf_op jit(solution)/shard_map/all_to_all | solution.py:83
  168.7 7.2 %copy-start.2 = (bf16[1,2048,768]{2,1,0:T(8,128)(2,1)S(1)}, bf16[1,2048,768]{2,1,0:T(8,128)(2,1)}, u32[]{:S(2)}) copy-start(bf16[1,2048,768]{2,1,0:T(8,128)(2,1)} %param.14) | copy-start | bytes 9437188
  227.6 65.0 %all-to-all-start.1 = ((bf16[8,160,2048]{2,1,0:T(8,128)(2,1)}), bf16[8,160,2048]{2,1,0:T(8,128)(2,1)}, u32[]{:S(2)}, u32[]{:S(2)}) async-start(bf16[8,160,2048]{2,1,0:T(8,128)(2,1)} %bitcast.84), calls=%async_computation.1 | async-start | bytes 10485760 | tf_op jit(solution)/shard_map/all_to_all | solution.py:83
  233.8 7.2 %copy-start.3 = (bf16[1,2048,768]{2,1,0:T(8,128)(2,1)S(1)}, bf16[1,2048,768]{2,1,0:T(8,128)(2,1)}, u32[]{:S(2)}) copy-start(bf16[1,2048,768]{2,1,0:T(8,128)(2,1)} %param.14) | copy-start | bytes 9437188
  292.6 65.0 %all-to-all-start.3 = ((bf16[8,160,2048]{2,1,0:T(8,128)(2,1)}), bf16[8,160,2048]{2,1,0:T(8,128)(2,1)}, u32[]{:S(2)}, u32[]{:S(2)}) async-start(bf16[8,160,2048]{2,1,0:T(8,128)(2,1)} %bitcast.81), calls=%async_computation.3 | async-start | bytes 10485760 | tf_op jit(solution)/shard_map/all_to_all | solution.py:83
  313.6 56.2 %collective-permute-start.3 = (bf16[128,2048]{1,0:T(8,128)(2,1)}, bf16[128,2048]{1,0:T(8,128)(2,1)}, u32[]{:S(2)}, u32[]{:S(2)}) collective-permute-start(bf16[128,2048]{1,0:T(8,128)(2,1)} %get-tuple-element.17), channel_id=1, source_target_pairs={{24,0},{25,1},{26,2},{27,3},{28,4},{29,5},{30,6},{31,7},{0,8},{1,9... | collective-permute-start | bytes 1572872 | tf_op jit(solution)/shard_map/ppermute | solution.py:80
  314.4 56.9 %collective-permute-start.4 = (bf16[128,2048]{1,0:T(8,128)(2,1)}, bf16[128,2048]{1,0:T(8,128)(2,1)}, u32[]{:S(2)}, u32[]{:S(2)}) collective-permute-start(bf16[128,2048]{1,0:T(8,128)(2,1)} %get-tuple-element.19), channel_id=1, source_target_pairs={{16,0},{17,1},{18,2},{19,3},{20,4},{21,5},{22,6},{23,7},{24,8},{25... | collective-permute-start | bytes 1572872 | tf_op jit(solution)/shard_map/ppermute | solution.py:80
  316.9 54.3 %collective-permute-start.5 = (bf16[128,2048]{1,0:T(8,128)(2,1)}, bf16[128,2048]{1,0:T(8,128)(2,1)}, u32[]{:S(2)}, u32[]{:S(2)}) collective-permute-start(bf16[128,2048]{1,0:T(8,128)(2,1)} %get-tuple-element.18), channel_id=1, source_target_pairs={{8,0},{9,1},{10,2},{11,3},{12,4},{13,5},{14,6},{15,7},{16,8},{17,9... | collective-permute-start | bytes 1572872 | tf_op jit(solution)/shard_map/ppermute | solution.py:80
  367.6 35.9 %collective-permute-start.10 = (bf16[128,2048]{1,0:T(8,128)(2,1)S(1)}, bf16[128,2048]{1,0:T(8,128)(2,1)S(1)}, u32[]{:S(2)}, u32[]{:S(2)}) collective-permute-start(bf16[128,2048]{1,0:T(8,128)(2,1)S(1)} %get-tuple-element.22), channel_id=1, source_target_pairs={{16,0},{17,1},{18,2},{19,3},{20,4},{21,5},{22,6},{23,7},{24,8},{25... | collective-permute-start | bytes 1572872 | tf_op jit(solution)/shard_map/ppermute | solution.py:80
  369.8 46.4 %collective-permute-start.11 = (bf16[128,2048]{1,0:T(8,128)(2,1)S(1)}, bf16[128,2048]{1,0:T(8,128)(2,1)S(1)}, u32[]{:S(2)}, u32[]{:S(2)}) collective-permute-start(bf16[128,2048]{1,0:T(8,128)(2,1)S(1)} %get-tuple-element.21), channel_id=1, source_target_pairs={{8,0},{9,1},{10,2},{11,3},{12,4},{13,5},{14,6},{15,7},{16,8},{17,9... | collective-permute-start | bytes 1572872 | tf_op jit(solution)/shard_map/ppermute | solution.py:80
  369.8 46.4 %collective-permute-start.9 = (bf16[128,2048]{1,0:T(8,128)(2,1)S(1)}, bf16[128,2048]{1,0:T(8,128)(2,1)S(1)}, u32[]{:S(2)}, u32[]{:S(2)}) collective-permute-start(bf16[128,2048]{1,0:T(8,128)(2,1)S(1)} %get-tuple-element.20), channel_id=1, source_target_pairs={{24,0},{25,1},{26,2},{27,3},{28,4},{29,5},{30,6},{31,7},{0,8},{1,9... | collective-permute-start | bytes 1572872 | tf_op jit(solution)/shard_map/ppermute | solution.py:80
Sparse Core Ops, SparseCore 0:
  11.8 75.0 all-gather.2

commit v3 on v2

v3 whole, which is shorter than its diff:
```python
import jax
import jax.numpy as jnp
from jax import lax
from jax.sharding import PartitionSpec as P

AXES = ("expert", "group")


def body(tokens, expert_ids, gate_probs, capacity, flows, w_gate, w_up, w_down):
    device_count, group_size = lax.axis_size(AXES), lax.axis_size("group")
    width = max(1, group_size // 2)
    planes = max(1, lax.axis_size("expert") // width)
    plane_size = device_count // planes
    micro_count, tok_local, model_dim = tokens.shape
    top_count = expert_ids.shape[2]
    slot_count = tok_local * top_count * 5 // (4 * device_count)
    sent = planes * slot_count
    column = planes * tok_local
    me = lax.axis_index(AXES)
    my_z, my_spot = me // plane_size, me % plane_size
    pairwise = plane_size <= 16 and plane_size & (plane_size - 1) == 0
    plane_iota = jnp.arange(planes, dtype=jnp.int32)
    spot_iota = jnp.arange(plane_size, dtype=jnp.int32)
    mate = my_spot ^ spot_iota if pairwise else spot_iota
    device_iota = jnp.arange(device_count, dtype=jnp.int32)

    def shift(value, step):
        pairs = [
            ((z + step) % planes * plane_size + spot, z * plane_size + spot)
            for z in range(planes)
            for spot in range(plane_size)
        ]
        return lax.ppermute(value, AXES, pairs)

    def swap(value):
        value = value.reshape(plane_size, sent, value.shape[-1])
        if not pairwise:
            groups = [
                [z * plane_size + spot for spot in range(plane_size)] for z in range(planes)
            ]
            value = lax.all_to_all(
                value, AXES, split_axis=0, concat_axis=0, tiled=True, axis_index_groups=groups
            )
            return [value.reshape(plane_size * sent, value.shape[-1])]
        pieces = [value[0]]
        for k in range(1, plane_size):
            pairs = [
                (z * plane_size + spot, z * plane_size + (spot ^ k))
                for z in range(planes)
                for spot in range(plane_size)
            ]
            pieces.append(lax.ppermute(value[k], AXES, pairs))
        return pieces

    def split(value, parts):
        return jnp.split(value, parts, axis=-1)

    cuts_out = [2 if m == 0 else 1 for m in range(micro_count)]
    cuts_back = [2 if m == micro_count - 1 else 1 for m in range(micro_count)]
    columns, last = [], None
    for micro_index in range(micro_count):
        parts = []
        for own in split(tokens[micro_index], cuts_out[micro_index]):
            if last is not None:
                own, last = lax.optimization_barrier((own, last))
                holder[-1] = last
            holder = [own] + [shift(own, step) for step in range(1, planes)]
            last = holder[-1]
            parts.append(holder)
        columns.append(parts)

    gate_norm = gate_probs / jnp.sum(gate_probs, 2, keepdims=True)
    toward = ((my_z - plane_iota) % planes)[:, None] * plane_size + mate[None, :]
    named = expert_ids[None, :, None] == toward[:, None, :, None, None]
    spread = jnp.sum(jnp.where(named, gate_norm[None, :, None], 0.0), 4)
    weight = jnp.stack([spread[0]] + [shift(spread[step], step) for step in range(1, planes)])
    chosen = weight > 0
    tok_iota = jnp.arange(tok_local, dtype=jnp.int32)
    before = (tok_iota[:, None] < tok_iota[None, :]).astype(jnp.bfloat16)
    rank = jnp.einsum(
        "jmet,tu->jmeu", chosen.astype(jnp.bfloat16), before, preferred_element_type=jnp.float32
    )
    block = (plane_iota * slot_count)[:, None, None, None]
    code = jnp.where(chosen, block + rank.astype(jnp.int32), -1)
    code = jnp.transpose(code, (1, 2, 0, 3)).reshape(micro_count, plane_size, column)
    weight = jnp.transpose(weight, (1, 2, 0, 3)).reshape(micro_count, plane_size, column)

    counts = jnp.sum(
        (expert_ids.reshape(1, micro_count, -1) == device_iota[:, None, None]).astype(jnp.int32), 2
    )
    counts = lax.all_to_all(counts, AXES, split_axis=0, concat_axis=0, tiled=True)
    from_device = ((my_z + plane_iota) % planes)[None, :] * plane_size + mate[:, None]
    ahead = device_iota[None, None, :] < from_device[:, :, None]
    offset = jnp.sum(jnp.where(ahead[..., None], counts, 0), 2)
    keep_limit = capacity[0] + jnp.sum(flows[0])
    slot_iota = jnp.arange(slot_count, dtype=jnp.int32)
    live = offset[:, :, None, :] + slot_iota[None, None, :, None] < keep_limit
    live = live.reshape(plane_size * sent, micro_count)

    sent_iota = jnp.arange(sent, dtype=jnp.int32)
    arrived, matches = [], []
    for micro_index in range(micro_count):
        match = code[micro_index][:, None, :] == sent_iota[None, :, None]
        matches.append(match)
        select = match.astype(jnp.bfloat16).reshape(plane_size * sent, column)
        parts = []
        for holder in columns[micro_index]:
            rows = jnp.dot(
                select, jnp.concatenate(holder, 0), preferred_element_type=jnp.float32
            ).astype(jnp.bfloat16)
            parts.append(swap(rows))
        arrived.append(parts)

    answers = []
    for micro_index in range(micro_count):
        rows = jnp.concatenate([jnp.concatenate(p, 0) for p in arrived[micro_index]], 1)
        gate_val = jnp.dot(rows, w_gate[0], preferred_element_type=jnp.float32)
        up_val = jnp.dot(rows, w_up[0], preferred_element_type=jnp.float32)
        hidden = (jax.nn.silu(gate_val) * up_val).astype(jnp.bfloat16)
        parts = []
        for down in split(w_down[0], cuts_back[micro_index]):
            out = jnp.dot(hidden, down, preferred_element_type=jnp.float32)
            out = jnp.where(live[:, micro_index][:, None], out, 0.0).astype(jnp.bfloat16)
            parts.append(swap(out))
        answers.append(parts)

    results = []
    for micro_index in range(micro_count):
        spread = jnp.where(matches[micro_index], weight[micro_index][:, None, :], 0.0)
        spread = spread.astype(jnp.bfloat16).reshape(plane_size * sent, column)
        parts = []
        for pieces in answers[micro_index]:
            back = jnp.concatenate(pieces, 0)
            contract = (((0,), (0,)), ((), ()))
            others = lax.dot_general(
                spread[:, tok_local:], back, contract, preferred_element_type=jnp.float32
            ).astype(jnp.bfloat16)
            others = others.reshape(planes - 1, tok_local, back.shape[1])
            total = lax.dot_general(
                spread[:, :tok_local], back, contract, preferred_element_type=jnp.float32
            )
            for step in range(1, planes):
                total = total + shift(others[step - 1], -step).astype(jnp.float32)
            parts.append(total.astype(jnp.bfloat16))
        results.append(jnp.concatenate(parts, 1))
    return jnp.stack(results)


def solution(mesh):
    placed = (
        P(None, AXES, None),
        P(None, AXES, None),
        P(None, AXES, None),
        P(AXES),
        P(AXES, None),
        P(AXES, None, None),
        P(AXES, None, None),
        P(AXES, None, None),
    )
    return jax.shard_map(
        body,
        mesh=mesh,
        in_specs=placed,
        out_specs=P(None, AXES, None),
        check_vma=False,
    )
```

time: 425 us -> 414 us (0.974)
  the two profiles are of different devices: /device:TPU:11 before, /device:TPU:0 now
where the time goes in v3:
time: 414 us; the launch traced here: 408 us
  waiting for transfers between devices  245 us (59%)
  starting transfers between devices  89 us (21%)
  matrix products  50.7 us (12%)
  local copies, waits for them, and re-layouts  11.6 us (3%)
  other arithmetic  8.74 us (2%)
    ppermute x42, waiting for transfers between devices, swap(): pieces.append(lax.ppermute(value[k], AXES, pairs))  192 us
    ppermute x42, starting transfers between devices, swap(): pieces.append(lax.ppermute(value[k], AXES, pairs))  49.7 us
    ppermute x21, waiting for transfers between devices, shift(): return lax.ppermute(value, AXES, pairs)  47.5 us
    ppermute x21, starting transfers between devices, shift(): return lax.ppermute(value, AXES, pairs)  35.1 us
    dot_general x3, matrix products, body(): out = jnp.dot(hidden, down, preferred_element_type=jnp.float32)  19 us
    dot_general x2, matrix products, body(): gate_val = jnp.dot(rows, w_gate[0], preferred_element_type=jnp.float32)  10.5 us
    dot_general x3, matrix products, body(): jnp.dot(select, jnp.concatenate(holder, 0), preferred_element_type=jnp.fl...  8.55 us
  transfers between devices with their start and end apart: 64, of which 25 were waited for; matrix products, arithmetic and copies ran while one was open for 16% of the time, Pallas kernels for 0%

profile of v3, /device:TPU:0, one launch (start us, length us, event | category | flops | bytes accessed | tf_op | source)
XLA Modules:
  0.0 407.9 jit_solution(1103259306576050239)
XLA Ops:
  0.0 2.3 slice_bitcast_fusion.1
  3.0 3.0 collective-permute-start.5
  6.0 2.6 collective-permute-start.4
  15.0 4.3 %all-to-all-start = ((s32[32,1,2]{2,1,0:T(1,128)}), s32[32,1,2]{2,1,0:T(1,128)S(1)}, u32[]{:S(2)}, u32[]{:S(2)}) async-start(s32[32,1,2]{2,1,0:T(1,128)} %copy.23), calls=%async_computation | async-start | bytes 32768 | tf_op jit(solution)/shard_map/all_to_all | solution.py:91
  22.9 5.9 %all-to-all-done = s32[32,1,2]{2,1,0:T(1,128)S(1)} async-done(((s32[32,1,2]{2,1,0:T(1,128)}), s32[32,1,2]{2,1,0:T(1,128)S(1)}, u32[]{:S(2)}, u32[]{:S(2)}) %all-to-all-start) | async-done | bytes 288 | tf_op jit(solution)/shard_map/all_to_all | solution.py:91
  37.5 2.7 collective-permute-start.13
  40.2 2.6 convolution_convert_fusion.2
  43.8 3.7 collective-permute-done.15
  47.5 9.8 %collective-permute-done.14 = bf16[128,1024]{1,0:T(8,128)(2,1)S(1)} collective-permute-done((bf16[128,1024]{1,0:T(8,128)(2,1)S(1)}, bf16[128,1024]{1,0:T(8,128)(2,1)S(1)}, u32[]{:S(2)}, u32[]{:S(2)}) %collective-permute-start.14) | collective-permute-done | bytes 262176 | tf_op jit(solution)/shard_map/ppermute | solution.py:33
  61.4 2.4 collective-permute-start.12
  63.8 3.9 collective-permute-start.35
  67.7 14.3 %collective-permute-done.9 = bf16[160,1024]{1,0:T(8,128)(2,1)S(1)} collective-permute-done((bf16[160,1024]{1,0:T(8,128)(2,1)S(1)}, bf16[160,1024]{1,0:T(8,128)(2,1)S(1)}, u32[]{:S(2)}, u32[]{:S(2)}) %collective-permute-start.9) | collective-permute-done | bytes 327712 | tf_op jit(solution)/shard_map/ppermute | solution.py:52
  82.0 2.4 collective-permute-done.10
  88.4 8.4 %collective-permute-done.17 = bf16[160,1024]{1,0:T(8,128)(2,1)S(1)} collective-permute-done((bf16[160,1024]{1,0:T(8,128)(2,1)S(1)}, bf16[160,1024]{1,0:T(8,128)(2,1)S(1)}, u32[]{:S(2)}, u32[]{:S(2)}) %collective-permute-start.17) | collective-permute-done | bytes 327712 | tf_op jit(solution)/shard_map/ppermute | solution.py:52
  96.8 5.1 %collective-permute-done.18 = bf16[160,1024]{1,0:T(8,128)(2,1)S(1)} collective-permute-done((bf16[160,1024]{1,0:T(8,128)(2,1)S(1)}, bf16[160,1024]{1,0:T(8,128)(2,1)S(1)}, u32[]{:S(2)}, u32[]{:S(2)}) %collective-permute-start.18) | collective-permute-done | bytes 327712 | tf_op jit(solution)/shard_map/ppermute | solution.py:52
  102.6 2.8 collective-permute-start.22
  106.0 8.0 %collective-permute-start.33 = (bf16[128,2048]{1,0:T(8,128)(2,1)}, bf16[128,2048]{1,0:T(8,128)(2,1)}, u32[]{:S(2)}, u32[]{:S(2)}) collective-permute-start(bf16[128,2048]{1,0:T(8,128)(2,1)} %get-tuple-element.12), channel_id=1, source_target_pairs={{8,0},{9,1},{10,2},{11,3},{12,4},{13,5},{14,6},{15,7},{16,8},{17,9... | collective-permute-start | bytes 1572872 | tf_op jit(solution)/shard_map/ppermute | solution.py:33
  114.0 6.4 %collective-permute-done.22 = bf16[160,1024]{1,0:T(8,128)(2,1)S(1)} collective-permute-done((bf16[160,1024]{1,0:T(8,128)(2,1)S(1)}, bf16[160,1024]{1,0:T(8,128)(2,1)S(1)}, u32[]{:S(2)}, u32[]{:S(2)}) %collective-permute-start.22) | collective-permute-done | bytes 327712 | tf_op jit(solution)/shard_map/ppermute | solution.py:52
  120.4 6.2 %fusion.1 = f32[1280,768]{1,0:T(8,128)} fusion(bf16[1280,1024]{1,0:T(8,128)(2,1)S(1)} %constant_dynamic-update-slice_fusion.7, bf16[1280,1024]{1,0:T(8,128)(2,1)S(1)} %constant_dynamic-update-slice_fusion, bf16[1,2048,768]{2,1,0:T(8,128)(2,1)S(1)} %copy-done.9), kind=kOutput, calls=%fused_computation.10 | convolution fusion | flops 4037017600 | bytes 12320768 | tf_op jit(solution)/shard_map/dot_general | solution.py:117
  126.7 14.6 %select_convert_fusion = bf16[1280,2048]{1,0:T(8,128)(2,1)} fusion(pred[1280]{0:T(1024)(128)(4,1)S(1)} %get-tuple-element.13, f32[1280,768]{1,0:T(8,128)} %fusion.1, bf16[1280,1024]{1,0:T(8,128)(2,1)} %copy-done.4, bf16[1280,1024]{1,0:T(8,128)(2,1)} %copy-done.5, bf16[1,2048,768]{2,1,0:T(8,128)(2,1)S(1)} %copy-done, bf16[1,768,2048]{2,1,0:T(8,128)(2,1)} %param.15), kind=kOutput, calls=%fused_computation | convolution fusion | flops 8074690560 | bytes 20710656 | tf_op jit(solution)/shard_map/dot_general | solution.py:122
  141.2 3.2 fusion.75
  144.4 6.5 %collective-permute-start.23 = (bf16[160,2048]{1,0:T(8,128)(2,1)S(1)}, bf16[160,2048]{1,0:T(8,128)(2,1)S(1)}, u32[]{:S(2)}, u32[]{:S(2)}) collective-permute-start(bf16[160,2048]{1,0:T(8,128)(2,1)S(1)} %get-tuple-element.21), channel_id=1, source_target_pairs={{0,1},{1,0},{2,3},{3,2},{4,5},{5,4},{6,7},{7,6},{8,9},{9,8},{10,11... | collective-permute-start | bytes 1966088 | tf_op jit(solution)/shard_map/ppermute | solution.py:52
  152.4 3.1 collective-permute-start.26
  155.5 4.4 %convolution_convert_fusion = bf16[1280,2048]{1,0:T(8,128)(2,1)S(1)} fusion(pred[1280,512]{1,0:T(32,128)(4,1)S(1)} %copy-done.3, bf16[128,2048]{1,0:T(8,128)(2,1)} %collective-permute-done.35, bf16[128,2048]{1,0:T(8,128)(2,1)} %collective-permute-done.34, bf16[128,2048]{1,0:T(8,128)(2,1)} %collective-permute-done.33, bf16[128,2048]{1,0:T(8,128)(2,1)} %get-tuple-element.12), kind=kOutput, calls=%fused_computation.1 | convolution fusion | flops 2695364608 | bytes 7995392 | tf_op jit(solution)/shard_map/dot_general | solution.py:108
  161.9 6.6 %collective-permute-done.24 = bf16[160,2048]{1,0:T(8,128)(2,1)S(1)} collective-permute-done((bf16[160,2048]{1,0:T(8,128)(2,1)S(1)}, bf16[160,2048]{1,0:T(8,128)(2,1)S(1)}, u32[]{:S(2)}, u32[]{:S(2)}) %collective-permute-start.24) | collective-permute-done | bytes 655392 | tf_op jit(solution)/shard_map/ppermute | solution.py:52
  169.9 10.9 %collective-permute-done.25 = bf16[160,2048]{1,0:T(8,128)(2,1)S(1)} collective-permute-done((bf16[160,2048]{1,0:T(8,128)(2,1)S(1)}, bf16[160,2048]{1,0:T(8,128)(2,1)S(1)}, u32[]{:S(2)}, u32[]{:S(2)}) %collective-permute-start.25) | collective-permute-done | bytes 655392 | tf_op jit(solution)/shard_map/ppermute | solution.py:52
  182.9 29.2 %collective-permute-done.27 = bf16[160,2048]{1,0:T(8,128)(2,1)S(1)} collective-permute-done((bf16[160,2048]{1,0:T(8,128)(2,1)S(1)}, bf16[160,2048]{1,0:T(8,128)(2,1)S(1)}, u32[]{:S(2)}, u32[]{:S(2)}) %collective-permute-start.27) | collective-permute-done | bytes 655392 | tf_op jit(solution)/shard_map/ppermute | solution.py:52
  214.7 2.3 convolution_convert_fusion.3
  217.2 2.6 collective-permute-start.41
  219.8 5.0 %collective-permute-done.37 = bf16[160,2048]{1,0:T(8,128)(2,1)S(1)} collective-permute-done((bf16[160,2048]{1,0:T(8,128)(2,1)S(1)}, bf16[160,2048]{1,0:T(8,128)(2,1)S(1)}, u32[]{:S(2)}, u32[]{:S(2)}) %collective-permute-start.37) | collective-permute-done | bytes 655392 | tf_op jit(solution)/shard_map/ppermute | solution.py:52
  226.1 10.9 %collective-permute-done.38 = bf16[160,2048]{1,0:T(8,128)(2,1)S(1)} collective-permute-done((bf16[160,2048]{1,0:T(8,128)(2,1)S(1)}, bf16[160,2048]{1,0:T(8,128)(2,1)S(1)}, u32[]{:S(2)}, u32[]{:S(2)}) %collective-permute-start.38) | collective-permute-done | bytes 655392 | tf_op jit(solution)/shard_map/ppermute | solution.py:52
  237.0 2.4 collective-permute-start.32
  239.7 31.5 %collective-permute-done.40 = bf16[160,2048]{1,0:T(8,128)(2,1)S(1)} collective-permute-done((bf16[160,2048]{1,0:T(8,128)(2,1)S(1)}, bf16[160,2048]{1,0:T(8,128)(2,1)S(1)}, u32[]{:S(2)}, u32[]{:S(2)}) %collective-permute-start.40) | collective-permute-done | bytes 655392 | tf_op jit(solution)/shard_map/ppermute | solution.py:52
  271.4 4.3 %fusion.7 = f32[1280,768]{1,0:T(8,128)S(1)} fusion(bf16[1280,2048]{1,0:T(8,128)(2,1)S(1)} %constant_dynamic-update-slice_fusion.21, bf16[1,2048,768]{2,1,0:T(8,128)(2,1)S(1)} %copy-done.10), kind=kOutput, calls=%fused_computation.14 | convolution fusion | flops 4026531840 | bytes 12320768 | tf_op jit(solution)/shard_map/dot_general | solution.py:117
  275.7 4.8 %multiply_convert_fusion = bf16[1280,768]{1,0:T(8,128)(2,1)S(1)} fusion(f32[1280,768]{1,0:T(8,128)S(1)} %fusion.7, bf16[1280,2048]{1,0:T(8,128)(2,1)S(1)} %constant_dynamic-update-slice_fusion.21, bf16[1,2048,768]{2,1,0:T(8,128)(2,1)S(1)} %copy-done), kind=kOutput, calls=%fused_computation.5 | convolution fusion | flops 4032430080 | bytes 14286848 | tf_op jit(solution)/shard_map/dot_general | solution.py:118
  280.5 2.2 select_convert_fusion.1
  289.7 7.0 %collective-permute-done.54 = bf16[160,1024]{1,0:T(8,128)(2,1)S(1)} collective-permute-done((bf16[160,1024]{1,0:T(8,128)(2,1)S(1)}, bf16[160,1024]{1,0:T(8,128)(2,1)S(1)}, u32[]{:S(2)}, u32[]{:S(2)}) %collective-permute-start.54) | collective-permute-done | bytes 327712 | tf_op jit(solution)/shard_map/ppermute | solution.py:52
  296.7 5.1 %collective-permute-done.55 = bf16[160,1024]{1,0:T(8,128)(2,1)S(1)} collective-permute-done((bf16[160,1024]{1,0:T(8,128)(2,1)S(1)}, bf16[160,1024]{1,0:T(8,128)(2,1)S(1)}, u32[]{:S(2)}, u32[]{:S(2)}) %collective-permute-start.55) | collective-permute-done | bytes 327712 | tf_op jit(solution)/shard_map/ppermute | solution.py:52
  301.8 2.6 collective-permute-start.58
  305.3 15.2 %collective-permute-done.57 = bf16[160,1024]{1,0:T(8,128)(2,1)S(1)} collective-permute-done((bf16[160,1024]{1,0:T(8,128)(2,1)S(1)}, bf16[160,1024]{1,0:T(8,128)(2,1)S(1)}, u32[]{:S(2)}, u32[]{:S(2)}) %collective-permute-start.57) | collective-permute-done | bytes 327712 | tf_op jit(solution)/shard_map/ppermute | solution.py:52
  323.3 8.3 %collective-permute-done.44 = bf16[160,1024]{1,0:T(8,128)(2,1)S(1)} collective-permute-done((bf16[160,1024]{1,0:T(8,128)(2,1)S(1)}, bf16[160,1024]{1,0:T(8,128)(2,1)S(1)}, u32[]{:S(2)}, u32[]{:S(2)}) %collective-permute-start.44) | collective-permute-done | bytes 327712 | tf_op jit(solution)/shard_map/ppermute | solution.py:52
  331.6 5.9 %collective-permute-done.45 = bf16[160,1024]{1,0:T(8,128)(2,1)S(1)} collective-permute-done((bf16[160,1024]{1,0:T(8,128)(2,1)S(1)}, bf16[160,1024]{1,0:T(8,128)(2,1)S(1)}, u32[]{:S(2)}, u32[]{:S(2)}) %collective-permute-start.45) | collective-permute-done | bytes 327712 | tf_op jit(solution)/shard_map/ppermute | solution.py:52
  337.6 3.1 collective-permute-start.48
  342.0 11.7 %collective-permute-done.47 = bf16[160,1024]{1,0:T(8,128)(2,1)S(1)} collective-permute-done((bf16[160,1024]{1,0:T(8,128)(2,1)S(1)}, bf16[160,1024]{1,0:T(8,128)(2,1)S(1)}, u32[]{:S(2)}, u32[]{:S(2)}) %collective-permute-start.47) | collective-permute-done | bytes 327712 | tf_op jit(solution)/shard_map/ppermute | solution.py:52
  356.3 7.5 %collective-permute-done.49 = bf16[160,1024]{1,0:T(8,128)(2,1)S(1)} collective-permute-done((bf16[160,1024]{1,0:T(8,128)(2,1)S(1)}, bf16[160,1024]{1,0:T(8,128)(2,1)S(1)}, u32[]{:S(2)}, u32[]{:S(2)}) %collective-permute-start.49) | collective-permute-done | bytes 327712 | tf_op jit(solution)/shard_map/ppermute | solution.py:52
  371.3 12.1 %collective-permute-done.61 = bf16[128,1024]{1,0:T(8,128)(2,1)S(1)} collective-permute-done((bf16[128,1024]{1,0:T(8,128)(2,1)S(1)}, bf16[128,1024]{1,0:T(8,128)(2,1)S(1)}, u32[]{:S(2)}, u32[]{:S(2)}) %collective-permute-start.61) | collective-permute-done | bytes 262176 | tf_op jit(solution)/shard_map/ppermute | solution.py:33
  384.0 2.3 collective-permute-done.52
  386.3 19.5 %collective-permute-done.51 = bf16[128,1024]{1,0:T(8,128)(2,1)S(1)} collective-permute-done((bf16[128,1024]{1,0:T(8,128)(2,1)S(1)}, bf16[128,1024]{1,0:T(8,128)(2,1)S(1)}, u32[]{:S(2)}, u32[]{:S(2)}) %collective-permute-start.51) | collective-permute-done | bytes 262176 | tf_op jit(solution)/shard_map/ppermute | solution.py:33
  (206 shorter events, 64.0 us)
Async XLA Ops:
  3.0 33.4 %collective-permute-start.5 = (bf16[128,1024]{1,0:T(8,128)(2,1)}, bf16[128,1024]{1,0:T(8,128)(2,1)}, u32[]{:S(2)}, u32[]{:S(2)}) collective-permute-start(bf16[128,1024]{1,0:T(8,128)(2,1)} %get-tuple-element.74), channel_id=1, source_target_pairs={{24,0},{25,1},{26,2},{27,3},{28,4},{29,5},{30,6},{31,7},{0,8},{1,9... | collective-permute-start | bytes 786440 | tf_op jit(solution)/shard_map/ppermute | solution.py:33
  6.0 34.2 %collective-permute-start.4 = (bf16[128,1024]{1,0:T(8,128)(2,1)}, bf16[128,1024]{1,0:T(8,128)(2,1)}, u32[]{:S(2)}, u32[]{:S(2)}) collective-permute-start(bf16[128,1024]{1,0:T(8,128)(2,1)} %get-tuple-element.74), channel_id=1, source_target_pairs={{16,0},{17,1},{18,2},{19,3},{20,4},{21,5},{22,6},{23,7},{24,8},{25... | collective-permute-start | bytes 786440 | tf_op jit(solution)/shard_map/ppermute | solution.py:33
  10.1 19.3 %collective-permute-start.2 = (f32[2,8,128]{2,1,0:T(8,128)}, f32[2,8,128]{2,1,0:T(8,128)}, u32[]{:S(2)}, u32[]{:S(2)}) collective-permute-start(f32[2,8,128]{2,1,0:T(8,128)} %get-tuple-element.79), channel_id=1, source_target_pairs={{24,0},{25,1},{26,2},{27,3},{28,4},{29,5},{30,6},{31,7},{0,8},{1,9... | collective-permute-start | bytes 24584 | tf_op jit(solution)/shard_map/ppermute | solution.py:33
  10.1 21.0 %collective-permute-start.1 = (f32[2,8,128]{2,1,0:T(8,128)}, f32[2,8,128]{2,1,0:T(8,128)}, u32[]{:S(2)}, u32[]{:S(2)}) collective-permute-start(f32[2,8,128]{2,1,0:T(8,128)} %get-tuple-element.80), channel_id=1, source_target_pairs={{16,0},{17,1},{18,2},{19,3},{20,4},{21,5},{22,6},{23,7},{24,8},{25... | collective-permute-start | bytes 24584 | tf_op jit(solution)/shard_map/ppermute | solution.py:33
  12.0 19.0 %collective-permute-start = (f32[2,8,128]{2,1,0:T(8,128)}, f32[2,8,128]{2,1,0:T(8,128)}, u32[]{:S(2)}, u32[]{:S(2)}) collective-permute-start(f32[2,8,128]{2,1,0:T(8,128)} %get-tuple-element.81), channel_id=1, source_target_pairs={{8,0},{9,1},{10,2},{11,3},{12,4},{13,5},{14,6},{15,7},{16,8},{17,9... | collective-permute-start | bytes 24584 | tf_op jit(solution)/shard_map/ppermute | solution.py:33
  36.8 20.5 %collective-permute-start.14 = (bf16[128,1024]{1,0:T(8,128)(2,1)S(1)}, bf16[128,1024]{1,0:T(8,128)(2,1)S(1)}, u32[]{:S(2)}, u32[]{:S(2)}) collective-permute-start(bf16[128,1024]{1,0:T(8,128)(2,1)S(1)} %get-tuple-element.10), channel_id=1, source_target_pairs={{16,0},{17,1},{18,2},{19,3},{20,4},{21,5},{22,6},{23,7},{24,8},{25... | collective-permute-start | bytes 786440 | tf_op jit(solution)/shard_map/ppermute | solution.py:33
  37.5 20.4 %collective-permute-start.13 = (bf16[128,1024]{1,0:T(8,128)(2,1)S(1)}, bf16[128,1024]{1,0:T(8,128)(2,1)S(1)}, u32[]{:S(2)}, u32[]{:S(2)}) collective-permute-start(bf16[128,1024]{1,0:T(8,128)(2,1)S(1)} %get-tuple-element.10), channel_id=1, source_target_pairs={{8,0},{9,1},{10,2},{11,3},{12,4},{13,5},{14,6},{15,7},{16,8},{17,9... | collective-permute-start | bytes 786440 | tf_op jit(solution)/shard_map/ppermute | solution.py:33
  43.1 16.7 %collective-permute-start.6 = (bf16[160,1024]{1,0:T(8,128)(2,1)S(1)}, bf16[160,1024]{1,0:T(8,128)(2,1)S(1)}, u32[]{:S(2)}, u32[]{:S(2)}) collective-permute-start(bf16[160,1024]{1,0:T(8,128)(2,1)S(1)} %get-tuple-element.37), channel_id=1, source_target_pairs={{0,1},{1,0},{2,3},{3,2},{4,5},{5,4},{6,7},{7,6},{8,9},{9,8},{10,11... | collective-permute-start | bytes 983048 | tf_op jit(solution)/shard_map/ppermute | solution.py:52
  43.2 18.2 %collective-permute-start.7 = (bf16[160,1024]{1,0:T(8,128)(2,1)S(1)}, bf16[160,1024]{1,0:T(8,128)(2,1)S(1)}, u32[]{:S(2)}, u32[]{:S(2)}) collective-permute-start(bf16[160,1024]{1,0:T(8,128)(2,1)S(1)} %get-tuple-element.36), channel_id=1, source_target_pairs={{0,2},{1,3},{2,0},{3,1},{4,6},{5,7},{6,4},{7,5},{8,10},{9,11},{10,... | collective-permute-start | bytes 983048 | tf_op jit(solution)/shard_map/ppermute | solution.py:52
  47.5 16.2 %collective-permute-start.8 = (bf16[160,1024]{1,0:T(8,128)(2,1)S(1)}, bf16[160,1024]{1,0:T(8,128)(2,1)S(1)}, u32[]{:S(2)}, u32[]{:S(2)}) collective-permute-start(bf16[160,1024]{1,0:T(8,128)(2,1)S(1)} %get-tuple-element.35), channel_id=1, source_target_pairs={{0,3},{1,2},{2,1},{3,0},{4,7},{5,6},{6,5},{7,4},{8,11},{9,10},{10,... | collective-permute-start | bytes 983048 | tf_op jit(solution)/shard_map/ppermute | solution.py:52
  57.3 24.7 %collective-permute-start.9 = (bf16[160,1024]{1,0:T(8,128)(2,1)S(1)}, bf16[160,1024]{1,0:T(8,128)(2,1)S(1)}, u32[]{:S(2)}, u32[]{:S(2)}) collective-permute-start(bf16[160,1024]{1,0:T(8,128)(2,1)S(1)} %get-tuple-element.34), channel_id=1, source_target_pairs={{0,4},{1,5},{2,6},{3,7},{4,0},{5,1},{6,2},{7,3},{8,12},{9,13},{10,... | collective-permute-start | bytes 983048 | tf_op jit(solution)/shard_map/ppermute | solution.py:52
  57.9 26.5 %collective-permute-start.10 = (bf16[160,1024]{1,0:T(8,128)(2,1)S(1)}, bf16[160,1024]{1,0:T(8,128)(2,1)S(1)}, u32[]{:S(2)}, u32[]{:S(2)}) collective-permute-start(bf16[160,1024]{1,0:T(8,128)(2,1)S(1)} %get-tuple-element.33), channel_id=1, source_target_pairs={{0,5},{1,4},{2,7},{3,6},{4,1},{5,0},{6,3},{7,2},{8,13},{9,12},{10,... | collective-permute-start | bytes 983048 | tf_op jit(solution)/shard_map/ppermute | solution.py:52
  59.8 26.4 %collective-permute-start.11 = (bf16[160,1024]{1,0:T(8,128)(2,1)S(1)}, bf16[160,1024]{1,0:T(8,128)(2,1)S(1)}, u32[]{:S(2)}, u32[]{:S(2)}) collective-permute-start(bf16[160,1024]{1,0:T(8,128)(2,1)S(1)} %get-tuple-element.32), channel_id=1, source_target_pairs={{0,6},{1,7},{2,4},{3,5},{4,2},{5,3},{6,0},{7,1},{8,14},{9,15},{10,... | collective-permute-start | bytes 983048 | tf_op jit(solution)/shard_map/ppermute | solution.py:52
  61.4 25.5 %collective-permute-start.12 = (bf16[160,1024]{1,0:T(8,128)(2,1)S(1)}, bf16[160,1024]{1,0:T(8,128)(2,1)S(1)}, u32[]{:S(2)}, u32[]{:S(2)}) collective-permute-start(bf16[160,1024]{1,0:T(8,128)(2,1)S(1)} %get-tuple-element.31), channel_id=1, source_target_pairs={{0,7},{1,6},{2,5},{3,4},{4,3},{5,2},{6,1},{7,0},{8,15},{9,14},{10,... | collective-permute-start | bytes 983048 | tf_op jit(solution)/shard_map/ppermute | solution.py:52
  63.8 87.2 %collective-permute-start.35 = (bf16[128,2048]{1,0:T(8,128)(2,1)}, bf16[128,2048]{1,0:T(8,128)(2,1)}, u32[]{:S(2)}, u32[]{:S(2)}) collective-permute-start(bf16[128,2048]{1,0:T(8,128)(2,1)} %get-tuple-element.12), channel_id=1, source_target_pairs={{24,0},{25,1},{26,2},{27,3},{28,4},{29,5},{30,6},{31,7},{0,8},{1,9... | collective-permute-start | bytes 1572872 | tf_op jit(solution)/shard_map/ppermute | solution.py:33
  82.0 70.4 %collective-permute-start.34 = (bf16[128,2048]{1,0:T(8,128)(2,1)}, bf16[128,2048]{1,0:T(8,128)(2,1)}, u32[]{:S(2)}, u32[]{:S(2)}) collective-permute-start(bf16[128,2048]{1,0:T(8,128)(2,1)} %get-tuple-element.12), channel_id=1, source_target_pairs={{16,0},{17,1},{18,2},{19,3},{20,4},{21,5},{22,6},{23,7},{24,8},{25... | collective-permute-start | bytes 1572872 | tf_op jit(solution)/shard_map/ppermute | solution.py:33
  86.9 15.0 %collective-permute-start.18 = (bf16[160,1024]{1,0:T(8,128)(2,1)S(1)}, bf16[160,1024]{1,0:T(8,128)(2,1)S(1)}, u32[]{:S(2)}, u32[]{:S(2)}) collective-permute-start(bf16[160,1024]{1,0:T(8,128)(2,1)S(1)} %get-tuple-element.43), channel_id=1, source_target_pairs={{0,3},{1,2},{2,1},{3,0},{4,7},{5,6},{6,5},{7,4},{8,11},{9,10},{10,... | collective-permute-start | bytes 983048 | tf_op jit(solution)/shard_map/ppermute | solution.py:52
  102.6 17.8 %collective-permute-start.22 = (bf16[160,1024]{1,0:T(8,128)(2,1)S(1)}, bf16[160,1024]{1,0:T(8,128)(2,1)S(1)}, u32[]{:S(2)}, u32[]{:S(2)}) collective-permute-start(bf16[160,1024]{1,0:T(8,128)(2,1)S(1)} %get-tuple-element.39), channel_id=1, source_target_pairs={{0,7},{1,6},{2,5},{3,4},{4,3},{5,2},{6,1},{7,0},{8,15},{9,14},{10,... | collective-permute-start | bytes 983048 | tf_op jit(solution)/shard_map/ppermute | solution.py:52
  106.0 49.5 %collective-permute-start.33 = (bf16[128,2048]{1,0:T(8,128)(2,1)}, bf16[128,2048]{1,0:T(8,128)(2,1)}, u32[]{:S(2)}, u32[]{:S(2)}) collective-permute-start(bf16[128,2048]{1,0:T(8,128)(2,1)} %get-tuple-element.12), channel_id=1, source_target_pairs={{8,0},{9,1},{10,2},{11,3},{12,4},{13,5},{14,6},{15,7},{16,8},{17,9... | collective-permute-start | bytes 1572872 | tf_op jit(solution)/shard_map/ppermute | solution.py:33
  144.4 16.1 %collective-permute-start.23 = (bf16[160,2048]{1,0:T(8,128)(2,1)S(1)}, bf16[160,2048]{1,0:T(8,128)(2,1)S(1)}, u32[]{:S(2)}, u32[]{:S(2)}) collective-permute-start(bf16[160,2048]{1,0:T(8,128)(2,1)S(1)} %get-tuple-element.21), channel_id=1, source_target_pairs={{0,1},{1,0},{2,3},{3,2},{4,5},{5,4},{6,7},{7,6},{8,9},{9,8},{10,11... | collective-permute-start | bytes 1966088 | tf_op jit(solution)/shard_map/ppermute | solution.py:52
  150.9 17.6 %collective-permute-start.24 = (bf16[160,2048]{1,0:T(8,128)(2,1)S(1)}, bf16[160,2048]{1,0:T(8,128)(2,1)S(1)}, u32[]{:S(2)}, u32[]{:S(2)}) collective-permute-start(bf16[160,2048]{1,0:T(8,128)(2,1)S(1)} %get-tuple-element.20), channel_id=1, source_target_pairs={{0,2},{1,3},{2,0},{3,1},{4,6},{5,7},{6,4},{7,5},{8,10},{9,11},{10,... | collective-permute-start | bytes 1966088 | tf_op jit(solution)/shard_map/ppermute | solution.py:52
  150.9 29.9 %collective-permute-start.25 = (bf16[160,2048]{1,0:T(8,128)(2,1)S(1)}, bf16[160,2048]{1,0:T(8,128)(2,1)S(1)}, u32[]{:S(2)}, u32[]{:S(2)}) collective-permute-start(bf16[160,2048]{1,0:T(8,128)(2,1)S(1)} %get-tuple-element.19), channel_id=1, source_target_pairs={{0,3},{1,2},{2,1},{3,0},{4,7},{5,6},{6,5},{7,4},{8,11},{9,10},{10,... | collective-permute-start | bytes 1966088 | tf_op jit(solution)/shard_map/ppermute | solution.py:52
  152.4 30.4 %collective-permute-start.26 = (bf16[160,2048]{1,0:T(8,128)(2,1)S(1)}, bf16[160,2048]{1,0:T(8,128)(2,1)S(1)}, u32[]{:S(2)}, u32[]{:S(2)}) collective-permute-start(bf16[160,2048]{1,0:T(8,128)(2,1)S(1)} %get-tuple-element.18), channel_id=1, source_target_pairs={{0,4},{1,5},{2,6},{3,7},{4,0},{5,1},{6,2},{7,3},{8,12},{9,13},{10,... | collective-permute-start | bytes 1966088 | tf_op jit(solution)/shard_map/ppermute | solution.py:52
  155.4 56.7 %collective-permute-start.27 = (bf16[160,2048]{1,0:T(8,128)(2,1)S(1)}, bf16[160,2048]{1,0:T(8,128)(2,1)S(1)}, u32[]{:S(2)}, u32[]{:S(2)}) collective-permute-start(bf16[160,2048]{1,0:T(8,128)(2,1)S(1)} %get-tuple-element.17), channel_id=1, source_target_pairs={{0,5},{1,4},{2,7},{3,6},{4,1},{5,0},{6,3},{7,2},{8,13},{9,12},{10,... | collective-permute-start | bytes 1966088 | tf_op jit(solution)/shard_map/ppermute | solution.py:52
  160.5 52.2 %collective-permute-start.28 = (bf16[160,2048]{1,0:T(8,128)(2,1)S(1)}, bf16[160,2048]{1,0:T(8,128)(2,1)S(1)}, u32[]{:S(2)}, u32[]{:S(2)}) collective-permute-start(bf16[160,2048]{1,0:T(8,128)(2,1)S(1)} %get-tuple-element.16), channel_id=1, source_target_pairs={{0,6},{1,7},{2,4},{3,5},{4,2},{5,3},{6,0},{7,1},{8,14},{9,15},{10,... | collective-permute-start | bytes 1966088 | tf_op jit(solution)/shard_map/ppermute | solution.py:52
  168.5 46.0 %collective-permute-start.29 = (bf16[160,2048]{1,0:T(8,128)(2,1)S(1)}, bf16[160,2048]{1,0:T(8,128)(2,1)S(1)}, u32[]{:S(2)}, u32[]{:S(2)}) collective-permute-start(bf16[160,2048]{1,0:T(8,128)(2,1)S(1)} %get-tuple-element.15), channel_id=1, source_target_pairs={{0,7},{1,6},{2,5},{3,4},{4,3},{5,2},{6,1},{7,0},{8,15},{9,14},{10,... | collective-permute-start | bytes 1966088 | tf_op jit(solution)/shard_map/ppermute | solution.py:52
  180.8 36.3 %collective-permute-start.36 = (bf16[160,2048]{1,0:T(8,128)(2,1)S(1)}, bf16[160,2048]{1,0:T(8,128)(2,1)S(1)}, u32[]{:S(2)}, u32[]{:S(2)}) collective-permute-start(bf16[160,2048]{1,0:T(8,128)(2,1)S(1)} %get-tuple-element.29), channel_id=1, source_target_pairs={{0,1},{1,0},{2,3},{3,2},{4,5},{5,4},{6,7},{7,6},{8,9},{9,8},{10,11... | collective-permute-start | bytes 1966088 | tf_op jit(solution)/shard_map/ppermute | solution.py:52
  182.8 42.0 %collective-permute-start.37 = (bf16[160,2048]{1,0:T(8,128)(2,1)S(1)}, bf16[160,2048]{1,0:T(8,128)(2,1)S(1)}, u32[]{:S(2)}, u32[]{:S(2)}) collective-permute-start(bf16[160,2048]{1,0:T(8,128)(2,1)S(1)} %get-tuple-element.28), channel_id=1, source_target_pairs={{0,2},{1,3},{2,0},{3,1},{4,6},{5,7},{6,4},{7,5},{8,10},{9,11},{10,... | collective-permute-start | bytes 1966088 | tf_op jit(solution)/shard_map/ppermute | solution.py:52
  212.1 24.9 %collective-permute-start.38 = (bf16[160,2048]{1,0:T(8,128)(2,1)S(1)}, bf16[160,2048]{1,0:T(8,128)(2,1)S(1)}, u32[]{:S(2)}, u32[]{:S(2)}) collective-permute-start(bf16[160,2048]{1,0:T(8,128)(2,1)S(1)} %get-tuple-element.27), channel_id=1, source_target_pairs={{0,3},{1,2},{2,1},{3,0},{4,7},{5,6},{6,5},{7,4},{8,11},{9,10},{10,... | collective-permute-start | bytes 1966088 | tf_op jit(solution)/shard_map/ppermute | solution.py:52
  212.7 26.8 %collective-permute-start.39 = (bf16[160,2048]{1,0:T(8,128)(2,1)S(1)}, bf16[160,2048]{1,0:T(8,128)(2,1)S(1)}, u32[]{:S(2)}, u32[]{:S(2)}) collective-permute-start(bf16[160,2048]{1,0:T(8,128)(2,1)S(1)} %get-tuple-element.26), channel_id=1, source_target_pairs={{0,4},{1,5},{2,6},{3,7},{4,0},{5,1},{6,2},{7,3},{8,12},{9,13},{10,... | collective-permute-start | bytes 1966088 | tf_op jit(solution)/shard_map/ppermute | solution.py:52
  214.6 56.6 %collective-permute-start.40 = (bf16[160,2048]{1,0:T(8,128)(2,1)S(1)}, bf16[160,2048]{1,0:T(8,128)(2,1)S(1)}, u32[]{:S(2)}, u32[]{:S(2)}) collective-permute-start(bf16[160,2048]{1,0:T(8,128)(2,1)S(1)} %get-tuple-element.25), channel_id=1, source_target_pairs={{0,5},{1,4},{2,7},{3,6},{4,1},{5,0},{6,3},{7,2},{8,13},{9,12},{10,... | collective-permute-start | bytes 1966088 | tf_op jit(solution)/shard_map/ppermute | solution.py:52
  217.2 54.1 %collective-permute-start.41 = (bf16[160,2048]{1,0:T(8,128)(2,1)S(1)}, bf16[160,2048]{1,0:T(8,128)(2,1)S(1)}, u32[]{:S(2)}, u32[]{:S(2)}) collective-permute-start(bf16[160,2048]{1,0:T(8,128)(2,1)S(1)} %get-tuple-element.24), channel_id=1, source_target_pairs={{0,6},{1,7},{2,4},{3,5},{4,2},{5,3},{6,0},{7,1},{8,14},{9,15},{10,... | collective-permute-start | bytes 1966088 | tf_op jit(solution)/shard_map/ppermute | solution.py:52
  224.7 46.6 %collective-permute-start.42 = (bf16[160,2048]{1,0:T(8,128)(2,1)S(1)}, bf16[160,2048]{1,0:T(8,128)(2,1)S(1)}, u32[]{:S(2)}, u32[]{:S(2)}) collective-permute-start(bf16[160,2048]{1,0:T(8,128)(2,1)S(1)} %get-tuple-element.23), channel_id=1, source_target_pairs={{0,7},{1,6},{2,5},{3,4},{4,3},{5,2},{6,1},{7,0},{8,15},{9,14},{10,... | collective-permute-start | bytes 1966088 | tf_op jit(solution)/shard_map/ppermute | solution.py:52
  237.0 128.0 %collective-permute-start.32 = (bf16[128,2048]{1,0:T(8,128)(2,1)S(1)}, bf16[128,2048]{1,0:T(8,128)(2,1)S(1)}, u32[]{:S(2)}, u32[]{:S(2)}) collective-permute-start(bf16[128,2048]{1,0:T(8,128)(2,1)S(1)} %get-tuple-element.64), channel_id=1, source_target_pairs={{8,0},{9,1},{10,2},{11,3},{12,4},{13,5},{14,6},{15,7},{16,8},{17,9... | collective-permute-start | bytes 1572872 | tf_op jit(solution)/shard_map/ppermute | solution.py:33
  239.5 127.3 %collective-permute-start.31 = (bf16[128,2048]{1,0:T(8,128)(2,1)S(1)}, bf16[128,2048]{1,0:T(8,128)(2,1)S(1)}, u32[]{:S(2)}, u32[]{:S(2)}) collective-permute-start(bf16[128,2048]{1,0:T(8,128)(2,1)S(1)} %get-tuple-element.65), channel_id=1, source_target_pairs={{16,0},{17,1},{18,2},{19,3},{20,4},{21,5},{22,6},{23,7},{24,8},{25... | collective-permute-start | bytes 1572872 | tf_op jit(solution)/shard_map/ppermute | solution.py:33
  287.8 16.6 %collective-permute-start.56 = (bf16[160,1024]{1,0:T(8,128)(2,1)S(1)}, bf16[160,1024]{1,0:T(8,128)(2,1)S(1)}, u32[]{:S(2)}, u32[]{:S(2)}) collective-permute-start(bf16[160,1024]{1,0:T(8,128)(2,1)S(1)} %get-tuple-element.58), channel_id=1, source_target_pairs={{0,4},{1,5},{2,6},{3,7},{4,0},{5,1},{6,2},{7,3},{8,12},{9,13},{10,... | collective-permute-start | bytes 983048 | tf_op jit(solution)/shard_map/ppermute | solution.py:52
  296.7 23.8 %collective-permute-start.57 = (bf16[160,1024]{1,0:T(8,128)(2,1)S(1)}, bf16[160,1024]{1,0:T(8,128)(2,1)S(1)}, u32[]{:S(2)}, u32[]{:S(2)}) collective-permute-start(bf16[160,1024]{1,0:T(8,128)(2,1)S(1)} %get-tuple-element.57), channel_id=1, source_target_pairs={{0,5},{1,4},{2,7},{3,6},{4,1},{5,0},{6,3},{7,2},{8,13},{9,12},{10,... | collective-permute-start | bytes 983048 | tf_op jit(solution)/shard_map/ppermute | solution.py:52
  301.8 19.1 %collective-permute-start.58 = (bf16[160,1024]{1,0:T(8,128)(2,1)S(1)}, bf16[160,1024]{1,0:T(8,128)(2,1)S(1)}, u32[]{:S(2)}, u32[]{:S(2)}) collective-permute-start(bf16[160,1024]{1,0:T(8,128)(2,1)S(1)} %get-tuple-element.56), channel_id=1, source_target_pairs={{0,6},{1,7},{2,4},{3,5},{4,2},{5,3},{6,0},{7,1},{8,14},{9,15},{10,... | collective-permute-start | bytes 983048 | tf_op jit(solution)/shard_map/ppermute | solution.py:52
  304.5 18.0 %collective-permute-start.59 = (bf16[160,1024]{1,0:T(8,128)(2,1)S(1)}, bf16[160,1024]{1,0:T(8,128)(2,1)S(1)}, u32[]{:S(2)}, u32[]{:S(2)}) collective-permute-start(bf16[160,1024]{1,0:T(8,128)(2,1)S(1)} %get-tuple-element.55), channel_id=1, source_target_pairs={{0,7},{1,6},{2,5},{3,4},{4,3},{5,2},{6,1},{7,0},{8,15},{9,14},{10,... | collective-permute-start | bytes 983048 | tf_op jit(solution)/shard_map/ppermute | solution.py:52
  331.5 37.4 %collective-permute-start.30 = (bf16[128,2048]{1,0:T(8,128)(2,1)S(1)}, bf16[128,2048]{1,0:T(8,128)(2,1)S(1)}, u32[]{:S(2)}, u32[]{:S(2)}) collective-permute-start(bf16[128,2048]{1,0:T(8,128)(2,1)S(1)} %get-tuple-element.63), channel_id=1, source_target_pairs={{24,0},{25,1},{26,2},{27,3},{28,4},{29,5},{30,6},{31,7},{0,8},{1,9... | collective-permute-start | bytes 1572872 | tf_op jit(solution)/shard_map/ppermute | solution.py:33
  337.4 16.2 %collective-permute-start.47 = (bf16[160,1024]{1,0:T(8,128)(2,1)S(1)}, bf16[160,1024]{1,0:T(8,128)(2,1)S(1)}, u32[]{:S(2)}, u32[]{:S(2)}) collective-permute-start(bf16[160,1024]{1,0:T(8,128)(2,1)S(1)} %get-tuple-element.49), channel_id=1, source_target_pairs={{0,5},{1,4},{2,7},{3,6},{4,1},{5,0},{6,3},{7,2},{8,13},{9,12},{10,... | collective-permute-start | bytes 983048 | tf_op jit(solution)/shard_map/ppermute | solution.py:52
  337.6 17.9 %collective-permute-start.48 = (bf16[160,1024]{1,0:T(8,128)(2,1)S(1)}, bf16[160,1024]{1,0:T(8,128)(2,1)S(1)}, u32[]{:S(2)}, u32[]{:S(2)}) collective-permute-start(bf16[160,1024]{1,0:T(8,128)(2,1)S(1)} %get-tuple-element.48), channel_id=1, source_target_pairs={{0,6},{1,7},{2,4},{3,5},{4,2},{5,3},{6,0},{7,1},{8,14},{9,15},{10,... | collective-permute-start | bytes 983048 | tf_op jit(solution)/shard_map/ppermute | solution.py:52
  355.6 15.6 %collective-permute-start.62 = (bf16[128,1024]{1,0:T(8,128)(2,1)S(1)}, bf16[128,1024]{1,0:T(8,128)(2,1)S(1)}, u32[]{:S(2)}, u32[]{:S(2)}) collective-permute-start(bf16[128,1024]{1,0:T(8,128)(2,1)S(1)} %get-tuple-element.72), channel_id=1, source_target_pairs={{8,0},{9,1},{10,2},{11,3},{12,4},{13,5},{14,6},{15,7},{16,8},{17,9... | collective-permute-start | bytes 786440 | tf_op jit(solution)/shard_map/ppermute | solution.py:33
  363.8 19.6 %collective-permute-start.61 = (bf16[128,1024]{1,0:T(8,128)(2,1)S(1)}, bf16[128,1024]{1,0:T(8,128)(2,1)S(1)}, u32[]{:S(2)}, u32[]{:S(2)}) collective-permute-start(bf16[128,1024]{1,0:T(8,128)(2,1)S(1)} %get-tuple-element.73), channel_id=1, source_target_pairs={{16,0},{17,1},{18,2},{19,3},{20,4},{21,5},{22,6},{23,7},{24,8},{25... | collective-permute-start | bytes 786440 | tf_op jit(solution)/shard_map/ppermute | solution.py:33
  365.1 18.3 %collective-permute-start.60 = (bf16[128,1024]{1,0:T(8,128)(2,1)S(1)}, bf16[128,1024]{1,0:T(8,128)(2,1)S(1)}, u32[]{:S(2)}, u32[]{:S(2)}) collective-permute-start(bf16[128,1024]{1,0:T(8,128)(2,1)S(1)} %get-tuple-element.71), channel_id=1, source_target_pairs={{24,0},{25,1},{26,2},{27,3},{28,4},{29,5},{30,6},{31,7},{0,8},{1,9... | collective-permute-start | bytes 786440 | tf_op jit(solution)/shard_map/ppermute | solution.py:33
  366.8 19.5 %collective-permute-start.52 = (bf16[128,1024]{1,0:T(8,128)(2,1)S(1)}, bf16[128,1024]{1,0:T(8,128)(2,1)S(1)}, u32[]{:S(2)}, u32[]{:S(2)}) collective-permute-start(bf16[128,1024]{1,0:T(8,128)(2,1)S(1)} %get-tuple-element.69), channel_id=1, source_target_pairs={{8,0},{9,1},{10,2},{11,3},{12,4},{13,5},{14,6},{15,7},{16,8},{17,9... | collective-permute-start | bytes 786440 | tf_op jit(solution)/shard_map/ppermute | solution.py:33
  368.9 36.8 %collective-permute-start.51 = (bf16[128,1024]{1,0:T(8,128)(2,1)S(1)}, bf16[128,1024]{1,0:T(8,128)(2,1)S(1)}, u32[]{:S(2)}, u32[]{:S(2)}) collective-permute-start(bf16[128,1024]{1,0:T(8,128)(2,1)S(1)} %get-tuple-element.70), channel_id=1, source_target_pairs={{16,0},{17,1},{18,2},{19,3},{20,4},{21,5},{22,6},{23,7},{24,8},{25... | collective-permute-start | bytes 786440 | tf_op jit(solution)/shard_map/ppermute | solution.py:33
  371.1 34.6 %collective-permute-start.50 = (bf16[128,1024]{1,0:T(8,128)(2,1)S(1)}, bf16[128,1024]{1,0:T(8,128)(2,1)S(1)}, u32[]{:S(2)}, u32[]{:S(2)}) collective-permute-start(bf16[128,1024]{1,0:T(8,128)(2,1)S(1)} %get-tuple-element.68), channel_id=1, source_target_pairs={{24,0},{25,1},{26,2},{27,3},{28,4},{29,5},{30,6},{31,7},{0,8},{1,9... | collective-permute-start | bytes 786440 | tf_op jit(solution)/shard_map/ppermute | solution.py:33
  (28 other events, 514.1 us)

commit v4 on v3

--- a/solution.py
+++ b/solution.py
@@ -18,10 +18,9 @@
     column = planes * tok_local
     me = lax.axis_index(AXES)
     my_z, my_spot = me // plane_size, me % plane_size
-    pairwise = plane_size <= 16 and plane_size & (plane_size - 1) == 0
+    groups = [[z * plane_size + spot for spot in range(plane_size)] for z in range(planes)]
     plane_iota = jnp.arange(planes, dtype=jnp.int32)
     spot_iota = jnp.arange(plane_size, dtype=jnp.int32)
-    mate = my_spot ^ spot_iota if pairwise else spot_iota
     device_iota = jnp.arange(device_count, dtype=jnp.int32)
 
     def shift(value, step):
@@ -34,23 +33,10 @@
 
     def swap(value):
         value = value.reshape(plane_size, sent, value.shape[-1])
-        if not pairwise:
-            groups = [
-                [z * plane_size + spot for spot in range(plane_size)] for z in range(planes)
-            ]
-            value = lax.all_to_all(
-                value, AXES, split_axis=0, concat_axis=0, tiled=True, axis_index_groups=groups
-            )
-            return [value.reshape(plane_size * sent, value.shape[-1])]
-        pieces = [value[0]]
-        for k in range(1, plane_size):
-            pairs = [
-                (z * plane_size + spot, z * plane_size + (spot ^ k))
-                for z in range(planes)
-                for spot in range(plane_size)
-            ]
-            pieces.append(lax.ppermute(value[k], AXES, pairs))
-        return pieces
+        value = lax.all_to_all(
+            value, AXES, split_axis=0, concat_axis=0, tiled=True, axis_index_groups=groups
+        )
+        return value.reshape(plane_size * sent, value.shape[-1])
 
     def split(value, parts):
         return jnp.split(value, parts, axis=-1)
@@ -70,10 +56,22 @@
         columns.append(parts)
 
     gate_norm = gate_probs / jnp.sum(gate_probs, 2, keepdims=True)
-    toward = ((my_z - plane_iota) % planes)[:, None] * plane_size + mate[None, :]
-    named = expert_ids[None, :, None] == toward[:, None, :, None, None]
-    spread = jnp.sum(jnp.where(named, gate_norm[None, :, None], 0.0), 4)
-    weight = jnp.stack([spread[0]] + [shift(spread[step], step) for step in range(1, planes)])
+    named = expert_ids[None] == device_iota[:, None, None, None]
+    spread = jnp.sum(jnp.where(named, gate_norm[None], 0.0), 3)
+    counts = jnp.sum(named.astype(jnp.float32), (2, 3))
+    toward = jnp.swapaxes(spread.reshape(planes, plane_size, micro_count, tok_local), 1, 2)
+    toward = jnp.broadcast_to(
+        toward[:, None], (planes, plane_size, micro_count, plane_size, tok_local)
+    ).reshape(device_count, micro_count, plane_size, tok_local)
+    tally = jnp.broadcast_to(
+        counts[:, :, None, None], (device_count, micro_count, 1, tok_local)
+    )
+    arrived = lax.all_to_all(
+        jnp.concatenate([toward, tally], 2), AXES, split_axis=0, concat_axis=0, tiled=True
+    )
+    weight = arrived[:, :, :plane_size].reshape((planes, plane_size) + toward.shape[1:])
+    weight = lax.dynamic_index_in_dim(weight, my_spot, 1, keepdims=False)
+    weight = jnp.roll(weight, -my_z, 0)
     chosen = weight > 0
     tok_iota = jnp.arange(tok_local, dtype=jnp.int32)
     before = (tok_iota[:, None] < tok_iota[None, :]).astype(jnp.bfloat16)
@@ -85,20 +83,17 @@
     code = jnp.transpose(code, (1, 2, 0, 3)).reshape(micro_count, plane_size, column)
     weight = jnp.transpose(weight, (1, 2, 0, 3)).reshape(micro_count, plane_size, column)
 
-    counts = jnp.sum(
-        (expert_ids.reshape(1, micro_count, -1) == device_iota[:, None, None]).astype(jnp.int32), 2
-    )
-    counts = lax.all_to_all(counts, AXES, split_axis=0, concat_axis=0, tiled=True)
-    from_device = ((my_z + plane_iota) % planes)[None, :] * plane_size + mate[:, None]
+    counts = arrived[:, :, plane_size, 0]
+    from_device = ((my_z + plane_iota) % planes)[None, :] * plane_size + spot_iota[:, None]
     ahead = device_iota[None, None, :] < from_device[:, :, None]
-    offset = jnp.sum(jnp.where(ahead[..., None], counts, 0), 2)
+    offset = jnp.sum(jnp.where(ahead[..., None], counts, 0.0), 2).astype(jnp.int32)
     keep_limit = capacity[0] + jnp.sum(flows[0])
     slot_iota = jnp.arange(slot_count, dtype=jnp.int32)
     live = offset[:, :, None, :] + slot_iota[None, None, :, None] < keep_limit
     live = live.reshape(plane_size * sent, micro_count)
 
     sent_iota = jnp.arange(sent, dtype=jnp.int32)
-    arrived, matches = [], []
+    slots, matches, leaving = [], [], []
     for micro_index in range(micro_count):
         match = code[micro_index][:, None, :] == sent_iota[None, :, None]
         matches.append(match)
@@ -109,11 +104,17 @@
                 select, jnp.concatenate(holder, 0), preferred_element_type=jnp.float32
             ).astype(jnp.bfloat16)
             parts.append(swap(rows))
-        arrived.append(parts)
+        leaving.append(rows)
+        slots.append(parts)
 
     answers = []
     for micro_index in range(micro_count):
-        rows = jnp.concatenate([jnp.concatenate(p, 0) for p in arrived[micro_index]], 1)
+        rows = slots[micro_index]
+        if micro_index + 1 < micro_count:
+            rows, leaving[micro_index + 1] = lax.optimization_barrier(
+                (rows, leaving[micro_index + 1])
+            )
+        rows = jnp.concatenate(rows, 1)
         gate_val = jnp.dot(rows, w_gate[0], preferred_element_type=jnp.float32)
         up_val = jnp.dot(rows, w_up[0], preferred_element_type=jnp.float32)
         hidden = (jax.nn.silu(gate_val) * up_val).astype(jnp.bfloat16)
@@ -129,8 +130,7 @@
         spread = jnp.where(matches[micro_index], weight[micro_index][:, None, :], 0.0)
         spread = spread.astype(jnp.bfloat16).reshape(plane_size * sent, column)
         parts = []
-        for pieces in answers[micro_index]:
-            back = jnp.concatenate(pieces, 0)
+        for back in answers[micro_index]:
             contract = (((0,), (0,)), ((), ()))
             others = lax.dot_general(
                 spread[:, tok_local:], back, contract, preferred_element_type=jnp.float32

time: 414 us -> 422 us (1.019); the launches traced: 408 us -> 421 us
  matrix products: 50.7 us -> 81 us
  waiting for transfers between devices: 245 us -> 220 us
  starting transfers between devices: 89 us -> 98.8 us
    ppermute x42 -> x0, waiting for transfers between devices: 192 us -> none  [swap(): pieces.append(lax.ppermute(value[k], AXES, pairs))]
    all_to_all x1 -> x7, waiting for transfers between devices: 5.87 us -> 115 us  [the longest x6 108 us: swap(): lax.all_to_all(value, AXES, split_axis=0, concat_axis=0, tiled=True, axis...]
    ppermute x21 -> x18, waiting for transfers between devices: 47.5 us -> 105 us  [shift(): return lax.ppermute(value, AXES, pairs)]
    ppermute x42 -> x0, starting transfers between devices: 49.7 us -> none  [swap(): pieces.append(lax.ppermute(value[k], AXES, pairs))]
    all_to_all x1 -> x7, starting transfers between devices: 4.26 us -> 34.6 us  [the longest x6 27.3 us: swap(): lax.all_to_all(value, AXES, split_axis=0, concat_axis=0, tiled=True, axis...]
    ppermute x21 -> x18, starting transfers between devices: 35.1 us -> 64.2 us  [shift(): return lax.ppermute(value, AXES, pairs)]
    dot_general x3, matrix products: 4.72 us -> 11.9 us  [body(): lax.dot_general(spread[:, tok_local:], back, contract, preferred_element_...]
    dot_general x3, matrix products: 8.55 us -> 15.4 us  [body(): jnp.dot(select, jnp.concatenate(holder, 0), preferred_element_type=jnp.fl...]
  transfers between devices with their start and end apart: 64 -> 25, of which waited for: 25 -> 15; matrix products, arithmetic and copies ran while one was open for 16% -> 21% of each run, Pallas kernels for 0% -> 0%
where the time goes in v4:
time: 422 us; the launch traced here: 421 us
  waiting for transfers between devices  220 us (52%)
  starting transfers between devices  98.8 us (23%)
  matrix products  81 us (19%)
  local copies, waits for them, and re-layouts  12.7 us (3%)
  other arithmetic  7.38 us (2%)
    all_to_all x6, waiting for transfers between devices, swap(): lax.all_to_all(value, AXES, split_axis=0, concat_axis=0, tiled=True, axis...  108 us
    ppermute x18, waiting for transfers between devices, shift(): return lax.ppermute(value, AXES, pairs)  105 us
    ppermute x18, starting transfers between devices, shift(): return lax.ppermute(value, AXES, pairs)  64.2 us
    all_to_all x6, starting transfers between devices, swap(): lax.all_to_all(value, AXES, split_axis=0, concat_axis=0, tiled=True, axis...  27.3 us
    dot_general x3, matrix products, body(): out = jnp.dot(hidden, down, preferred_element_type=jnp.float32)  24.1 us
    dot_general x3, matrix products, body(): jnp.dot(select, jnp.concatenate(holder, 0), preferred_element_type=jnp.fl...  15.4 us
    dot_general x2, matrix products, body(): gate_val = jnp.dot(rows, w_gate[0], preferred_element_type=jnp.float32)  13.3 us
    dot_general x3, matrix products, body(): lax.dot_general(spread[:, tok_local:], back, contract, preferred_element_...  11.9 us
  transfers between devices with their start and end apart: 25, of which 15 were waited for; matrix products, arithmetic and copies ran while one was open for 21% of the time, Pallas kernels for 0%

profile of v4, /device:TPU:0, one launch (start us, length us, event | category | flops | bytes accessed | tf_op | source)
XLA Modules:
  0.0 421.1 jit_solution(14704122591127454763)
XLA Ops:
  3.0 7.3 %all-to-all-start = ((f32[32,2,9,128]{3,1,2,0:T(2,128)}), f32[32,2,9,128]{3,1,2,0:T(2,128)S(1)}, u32[]{:S(2)}, u32[]{:S(2)}) async-start(f32[32,2,9,128]{3,1,2,0:T(2,128)} %copy.33), calls=%async_computation | async-start | bytes 589824 | tf_op jit(solution)/shard_map/all_to_all | solution.py:69
  10.3 2.1 slice_bitcast_fusion.1
  13.2 1.8 collective-permute-start.2
  15.0 2.4 collective-permute-start.1
  18.9 7.1 %collective-permute-done.2 = bf16[128,1024]{1,0:T(8,128)(2,1)} collective-permute-done((bf16[128,1024]{1,0:T(8,128)(2,1)}, bf16[128,1024]{1,0:T(8,128)(2,1)}, u32[]{:S(2)}, u32[]{:S(2)}) %collective-permute-start.2) | collective-permute-done | bytes 262176 | tf_op jit(solution)/shard_map/ppermute | solution.py:32
  26.0 6.6 %all-to-all-done = f32[32,2,9,128]{3,1,2,0:T(2,128)S(1)} async-done(((f32[32,2,9,128]{3,1,2,0:T(2,128)}), f32[32,2,9,128]{3,1,2,0:T(2,128)S(1)}, u32[]{:S(2)}, u32[]{:S(2)}) %all-to-all-start) | async-done | bytes 294944 | tf_op jit(solution)/shard_map/all_to_all | solution.py:69
  34.4 3.4 collective-permute-done.1
  37.8 4.3 %convolution_convert_fusion.2 = bf16[1280,1024]{1,0:T(8,128)(2,1)} fusion(pred[1280,512]{1,0:T(32,128)(4,1)S(1)} %get-tuple-element.40, bf16[128,1024]{1,0:T(8,128)(2,1)} %collective-permute-done.2, bf16[128,1024]{1,0:T(8,128)(2,1)} %collective-permute-done.1, bf16[128,1024]{1,0:T(8,128)(2,1)} %collective-permute-done, bf16[128,1024]{1,0:T(8,128)(2,1)} %get-tuple-element.32), kind=kOutput, calls=%fused_computation.7 | convolution fusion | flops 1347682304 | bytes 4325376 | tf_op jit(solution)/shard_map/dot_general | solution.py:103
  42.1 4.4 %all-to-all-start.1 = ((bf16[8,160,1024]{2,1,0:T(8,128)(2,1)}), bf16[8,160,1024]{2,1,0:T(8,128)(2,1)}, u32[]{:S(2)}, u32[]{:S(2)}) async-start(bf16[8,160,1024]{2,1,0:T(8,128)(2,1)} %bitcast.102), calls=%async_computation.1 | async-start | bytes 5242880 | tf_op jit(solution)/shard_map/all_to_all | solution.py:36
  46.5 5.8 %collective-permute-start.5 = (bf16[128,1024]{1,0:T(8,128)(2,1)}, bf16[128,1024]{1,0:T(8,128)(2,1)S(1)}, u32[]{:S(2)}, u32[]{:S(2)}) collective-permute-start(bf16[128,1024]{1,0:T(8,128)(2,1)} %get-tuple-element.12), channel_id=1, source_target_pairs={{24,0},{25,1},{26,2},{27,3},{28,4},{29,5},{30,6},{31,7},{0,8},{1,9... | collective-permute-start | bytes 786440 | tf_op jit(solution)/shard_map/ppermute | solution.py:32
  54.7 5.8 %collective-permute-done.5 = bf16[128,1024]{1,0:T(8,128)(2,1)S(1)} collective-permute-done((bf16[128,1024]{1,0:T(8,128)(2,1)}, bf16[128,1024]{1,0:T(8,128)(2,1)S(1)}, u32[]{:S(2)}, u32[]{:S(2)}) %collective-permute-start.5) | collective-permute-done | bytes 262176 | tf_op jit(solution)/shard_map/ppermute | solution.py:32
  60.5 10.9 %collective-permute-done.4 = bf16[128,1024]{1,0:T(8,128)(2,1)S(1)} collective-permute-done((bf16[128,1024]{1,0:T(8,128)(2,1)}, bf16[128,1024]{1,0:T(8,128)(2,1)S(1)}, u32[]{:S(2)}, u32[]{:S(2)}) %collective-permute-start.4) | collective-permute-done | bytes 262176 | tf_op jit(solution)/shard_map/ppermute | solution.py:32
  71.4 4.2 convolution_convert_fusion.1
  75.6 3.2 all-to-all-done.1
  78.8 4.4 %all-to-all-start.2 = ((bf16[8,160,1024]{2,1,0:T(8,128)(2,1)}), bf16[8,160,1024]{2,1,0:T(8,128)(2,1)}, u32[]{:S(2)}, u32[]{:S(2)}) async-start(bf16[8,160,1024]{2,1,0:T(8,128)(2,1)} %bitcast.100), calls=%async_computation.2 | async-start | bytes 5242880 | tf_op jit(solution)/shard_map/all_to_all | solution.py:36
  85.9 5.7 %collective-permute-start.8 = (bf16[128,2048]{1,0:T(8,128)(2,1)}, bf16[128,2048]{1,0:T(8,128)(2,1)}, u32[]{:S(2)}, u32[]{:S(2)}) collective-permute-start(bf16[128,2048]{1,0:T(8,128)(2,1)} %get-tuple-element.14), channel_id=1, source_target_pairs={{24,0},{25,1},{26,2},{27,3},{28,4},{29,5},{30,6},{31,7},{0,8},{1,9... | collective-permute-start | bytes 1572872 | tf_op jit(solution)/shard_map/ppermute | solution.py:32
  95.2 10.4 %collective-permute-done.8 = bf16[128,2048]{1,0:T(8,128)(2,1)} collective-permute-done((bf16[128,2048]{1,0:T(8,128)(2,1)}, bf16[128,2048]{1,0:T(8,128)(2,1)}, u32[]{:S(2)}, u32[]{:S(2)}) %collective-permute-start.8) | collective-permute-done | bytes 524320 | tf_op jit(solution)/shard_map/ppermute | solution.py:32
  105.7 22.2 %collective-permute-done.7 = bf16[128,2048]{1,0:T(8,128)(2,1)} collective-permute-done((bf16[128,2048]{1,0:T(8,128)(2,1)}, bf16[128,2048]{1,0:T(8,128)(2,1)}, u32[]{:S(2)}, u32[]{:S(2)}) %collective-permute-start.7) | collective-permute-done | bytes 524320 | tf_op jit(solution)/shard_map/ppermute | solution.py:32
  127.8 6.9 %convolution_convert_fusion = bf16[1280,2048]{1,0:T(8,128)(2,1)} fusion(pred[1280,512]{1,0:T(32,128)(4,1)} %get-tuple-element.41, bf16[128,2048]{1,0:T(8,128)(2,1)} %collective-permute-done.8, bf16[128,2048]{1,0:T(8,128)(2,1)} %collective-permute-done.7, bf16[128,2048]{1,0:T(8,128)(2,1)} %collective-permute-done.6, bf16[128,2048]{1,0:T(8,128)(2,1)} %get-tuple-element.14), kind=kOutput, calls=%fused_computation.1 | convolution fusion | flops 2695364608 | bytes 7995392 | tf_op jit(solution)/shard_map/dot_general | solution.py:103
  134.8 4.8 %all-to-all-start.4 = ((bf16[8,160,2048]{2,1,0:T(8,128)(2,1)}), bf16[8,160,2048]{2,1,0:T(8,128)(2,1)}, u32[]{:S(2)}, u32[]{:S(2)}) async-start(bf16[8,160,2048]{2,1,0:T(8,128)(2,1)} %bitcast.98), calls=%async_computation.4 | async-start | bytes 10485760 | tf_op jit(solution)/shard_map/all_to_all | solution.py:36
  139.7 2.0 constant_dynamic-update-slice_fusion.1
  141.7 2.2 constant_dynamic-update-slice_fusion
  144.4 6.2 %fusion.6 = f32[1280,768]{1,0:T(8,128)} fusion(bf16[1280,2048]{1,0:T(8,128)(2,1)S(1)} %constant_dynamic-update-slice_fusion, bf16[1,2048,768]{2,1,0:T(8,128)(2,1)S(1)} %copy-done.6), kind=kOutput, calls=%fused_computation.14 | convolution fusion | flops 4026531840 | bytes 12320768 | tf_op jit(solution)/shard_map/dot_general | solution.py:118
  150.6 14.5 %select_convert_fusion = bf16[1280,2048]{1,0:T(8,128)(2,1)} fusion(pred[1280]{0:T(1024)(128)(4,1)S(1)} %get-tuple-element.19, bf16[1280,2048]{1,0:T(8,128)(2,1)} %copy-done.4, f32[1280,768]{1,0:T(8,128)} %fusion.6, bf16[1,2048,768]{2,1,0:T(8,128)(2,1)S(1)} %copy-done, bf16[1,768,2048]{2,1,0:T(8,128)(2,1)} %param.15), kind=kOutput, calls=%fused_computation | convolution fusion | flops 8064204800 | bytes 20710656 | tf_op jit(solution)/shard_map/dot_general | solution.py:123
  165.1 34.7 %all-to-all-done.4 = bf16[8,160,2048]{2,1,0:T(8,128)(2,1)} async-done(((bf16[8,160,2048]{2,1,0:T(8,128)(2,1)}), bf16[8,160,2048]{2,1,0:T(8,128)(2,1)}, u32[]{:S(2)}, u32[]{:S(2)}) %all-to-all-start.4) | async-done | bytes 5242912 | tf_op jit(solution)/shard_map/all_to_all | solution.py:36
  199.8 4.9 %all-to-all-start.3 = ((bf16[8,160,2048]{2,1,0:T(8,128)(2,1)}), bf16[8,160,2048]{2,1,0:T(8,128)(2,1)}, u32[]{:S(2)}, u32[]{:S(2)}) async-start(bf16[8,160,2048]{2,1,0:T(8,128)(2,1)} %bitcast.99), calls=%async_computation.3 | async-start | bytes 10485760 | tf_op jit(solution)/shard_map/all_to_all | solution.py:36
  204.7 7.1 %fusion.4 = f32[1280,768]{1,0:T(8,128)S(1)} fusion(bf16[1280,2048]{1,0:T(8,128)(2,1)} %bitcast.32, bf16[1,2048,768]{2,1,0:T(8,128)(2,1)} %param.13), kind=kOutput, calls=%fused_computation.12 | convolution fusion | flops 4026531840 | bytes 12320768 | tf_op jit(solution)/shard_map/dot_general | solution.py:118
  211.8 7.4 %fusion.1 = bf16[1280,768]{1,0:T(8,128)(2,1)S(1)} fusion(bf16[1280,2048]{1,0:T(8,128)(2,1)} %bitcast.32, f32[1280,768]{1,0:T(8,128)S(1)} %fusion.4, bf16[1,2048,768]{2,1,0:T(8,128)(2,1)S(1)} %copy-done), kind=kOutput, calls=%fused_computation.9 | convolution fusion | flops 4032430080 | bytes 14286848 | tf_op jit(solution)/shard_map/dot_general | solution.py:119
  220.5 3.8 select_convert_fusion.1
  224.3 40.5 %all-to-all-done.3 = bf16[8,160,2048]{2,1,0:T(8,128)(2,1)} async-done(((bf16[8,160,2048]{2,1,0:T(8,128)(2,1)}), bf16[8,160,2048]{2,1,0:T(8,128)(2,1)}, u32[]{:S(2)}, u32[]{:S(2)}) %all-to-all-start.3) | async-done | bytes 5242912 | tf_op jit(solution)/shard_map/all_to_all | solution.py:36
  264.8 4.4 %all-to-all-start.6 = ((bf16[8,160,1024]{2,1,0:T(8,128)(2,1)}), bf16[8,160,1024]{2,1,0:T(8,128)(2,1)}, u32[]{:S(2)}, u32[]{:S(2)}) async-start(bf16[8,160,1024]{2,1,0:T(8,128)(2,1)} %bitcast.103), calls=%async_computation.6 | async-start | bytes 5242880 | tf_op jit(solution)/shard_map/all_to_all | solution.py:36
  269.2 5.8 %select_convert_fusion.2 = bf16[1280,1024]{1,0:T(8,128)(2,1)} fusion(bf16[1280,768]{1,0:T(8,128)(2,1)} %copy-done.9, pred[1280]{0:T(1024)(128)(4,1)S(1)} %get-tuple-element.20, bf16[768,2048]{1,0:T(8,128)(2,1)} %bitcast.108), kind=kOutput, calls=%fused_computation.3 | convolution fusion | flops 2015887360 | bytes 6161664 | tf_op jit(solution)/shard_map/dot_general | solution.py:123
  275.0 26.5 %all-to-all-done.6 = bf16[8,160,1024]{2,1,0:T(8,128)(2,1)} async-done(((bf16[8,160,1024]{2,1,0:T(8,128)(2,1)}), bf16[8,160,1024]{2,1,0:T(8,128)(2,1)}, u32[]{:S(2)}, u32[]{:S(2)}) %all-to-all-start.6) | async-done | bytes 2621472 | tf_op jit(solution)/shard_map/all_to_all | solution.py:36
  301.5 4.4 %all-to-all-start.5 = ((bf16[8,160,1024]{2,1,0:T(8,128)(2,1)}), bf16[8,160,1024]{2,1,0:T(8,128)(2,1)}, u32[]{:S(2)}, u32[]{:S(2)}) async-start(bf16[8,160,1024]{2,1,0:T(8,128)(2,1)} %bitcast.101), calls=%async_computation.5 | async-start | bytes 5242880 | tf_op jit(solution)/shard_map/all_to_all | solution.py:36
  306.5 5.7 %convolution_convert_fusion.3 = bf16[384,2048]{1,0:T(8,128)(2,1)S(1)} fusion(bf16[1280,2048]{1,0:T(8,128)(2,1)} %bitcast.27, bf16[1280,512]{1,0:T(8,128)(2,1)S(1)} %get-tuple-element.38), kind=kOutput, calls=%fused_computation.16 | convolution fusion | flops 2014052352 | bytes 7798784 | tf_op jit(solution)/shard_map/dot_general | solution.py:135
  313.4 12.7 %collective-permute-start.11 = (bf16[128,2048]{1,0:T(8,128)(2,1)}, bf16[128,2048]{1,0:T(8,128)(2,1)}, u32[]{:S(2)}, u32[]{:S(2)}) collective-permute-start(bf16[128,2048]{1,0:T(8,128)(2,1)} %get-tuple-element.22), channel_id=1, source_target_pairs={{8,0},{9,1},{10,2},{11,3},{12,4},{13,5},{14,6},{15,7},{16,8},{17,9... | collective-permute-start | bytes 1572872 | tf_op jit(solution)/shard_map/ppermute | solution.py:32
  326.7 3.0 convolution_convert_fusion.4
  330.5 3.7 collective-permute-start.17
  334.9 3.3 all-to-all-done.5
  338.2 3.2 convolution_convert_fusion.5
  341.5 21.2 %collective-permute-start.15 = (bf16[128,1024]{1,0:T(8,128)(2,1)S(1)}, bf16[128,1024]{1,0:T(8,128)(2,1)S(1)}, u32[]{:S(2)}, u32[]{:S(2)}) collective-permute-start(bf16[128,1024]{1,0:T(8,128)(2,1)S(1)} %get-tuple-element.29), channel_id=1, source_target_pairs={{24,0},{25,1},{26,2},{27,3},{28,4},{29,5},{30,6},{31,7},{0,8},{1,9... | collective-permute-start | bytes 786440 | tf_op jit(solution)/shard_map/ppermute | solution.py:32
  362.7 21.9 %collective-permute-done.10 = bf16[128,2048]{1,0:T(8,128)(2,1)} collective-permute-done((bf16[128,2048]{1,0:T(8,128)(2,1)}, bf16[128,2048]{1,0:T(8,128)(2,1)}, u32[]{:S(2)}, u32[]{:S(2)}) %collective-permute-start.10) | collective-permute-done | bytes 524320 | tf_op jit(solution)/shard_map/ppermute | solution.py:32
  386.2 4.0 fusion.41
  390.2 1.9 collective-permute-start.12
  392.1 14.9 %collective-permute-done.16 = bf16[128,1024]{1,0:T(8,128)(2,1)} collective-permute-done((bf16[128,1024]{1,0:T(8,128)(2,1)}, bf16[128,1024]{1,0:T(8,128)(2,1)}, u32[]{:S(2)}, u32[]{:S(2)}) %collective-permute-start.16) | collective-permute-done | bytes 262176 | tf_op jit(solution)/shard_map/ppermute | solution.py:32
  407.1 2.4 add_convert_fusion.1
  409.5 8.1 %collective-permute-done.13 = bf16[128,1024]{1,0:T(8,128)(2,1)S(1)} collective-permute-done((bf16[128,1024]{1,0:T(8,128)(2,1)S(1)}, bf16[128,1024]{1,0:T(8,128)(2,1)S(1)}, u32[]{:S(2)}, u32[]{:S(2)}) %collective-permute-start.13) | collective-permute-done | bytes 262176 | tf_op jit(solution)/shard_map/ppermute | solution.py:32
  417.6 2.3 add_convert_fusion.2
  (81 shorter events, 23.0 us)
Async XLA Ops:
  0.0 150.6 %copy-start = (bf16[1,2048,768]{2,1,0:T(8,128)(2,1)S(1)}, bf16[1,2048,768]{2,1,0:T(8,128)(2,1)}, u32[]{:S(2)}) copy-start(bf16[1,2048,768]{2,1,0:T(8,128)(2,1)} %param.14) | copy-start | bytes 9437188
  3.0 29.6 %all-to-all-start = ((f32[32,2,9,128]{3,1,2,0:T(2,128)}), f32[32,2,9,128]{3,1,2,0:T(2,128)S(1)}, u32[]{:S(2)}, u32[]{:S(2)}) async-start(f32[32,2,9,128]{3,1,2,0:T(2,128)} %copy.33), calls=%async_computation | async-start | bytes 589824 | tf_op jit(solution)/shard_map/all_to_all | solution.py:69
  13.2 12.7 %collective-permute-start.2 = (bf16[128,1024]{1,0:T(8,128)(2,1)}, bf16[128,1024]{1,0:T(8,128)(2,1)}, u32[]{:S(2)}, u32[]{:S(2)}) collective-permute-start(bf16[128,1024]{1,0:T(8,128)(2,1)} %get-tuple-element.32), channel_id=1, source_target_pairs={{24,0},{25,1},{26,2},{27,3},{28,4},{29,5},{30,6},{31,7},{0,8},{1,9... | collective-permute-start | bytes 786440 | tf_op jit(solution)/shard_map/ppermute | solution.py:32
  15.0 22.8 %collective-permute-start.1 = (bf16[128,1024]{1,0:T(8,128)(2,1)}, bf16[128,1024]{1,0:T(8,128)(2,1)}, u32[]{:S(2)}, u32[]{:S(2)}) collective-permute-start(bf16[128,1024]{1,0:T(8,128)(2,1)} %get-tuple-element.32), channel_id=1, source_target_pairs={{16,0},{17,1},{18,2},{19,3},{20,4},{21,5},{22,6},{23,7},{24,8},{25... | collective-permute-start | bytes 786440 | tf_op jit(solution)/shard_map/ppermute | solution.py:32
  17.4 20.4 %collective-permute-start = (bf16[128,1024]{1,0:T(8,128)(2,1)}, bf16[128,1024]{1,0:T(8,128)(2,1)}, u32[]{:S(2)}, u32[]{:S(2)}) collective-permute-start(bf16[128,1024]{1,0:T(8,128)(2,1)} %get-tuple-element.32), channel_id=1, source_target_pairs={{8,0},{9,1},{10,2},{11,3},{12,4},{13,5},{14,6},{15,7},{16,8},{17,9... | collective-permute-start | bytes 786440 | tf_op jit(solution)/shard_map/ppermute | solution.py:32
  34.4 7.7 %copy-start.5 = (pred[1280,512]{1,0:T(32,128)(4,1)}, pred[1280,512]{1,0:T(32,128)(4,1)S(1)}, u32[]{:S(2)}) copy-start(pred[1280,512]{1,0:T(32,128)(4,1)S(1)} %get-tuple-element.40) | copy-start | bytes 1966084
  42.1 36.7 %all-to-all-start.1 = ((bf16[8,160,1024]{2,1,0:T(8,128)(2,1)}), bf16[8,160,1024]{2,1,0:T(8,128)(2,1)}, u32[]{:S(2)}, u32[]{:S(2)}) async-start(bf16[8,160,1024]{2,1,0:T(8,128)(2,1)} %bitcast.102), calls=%async_computation.1 | async-start | bytes 5242880 | tf_op jit(solution)/shard_map/all_to_all | solution.py:36
  46.5 14.0 %collective-permute-start.5 = (bf16[128,1024]{1,0:T(8,128)(2,1)}, bf16[128,1024]{1,0:T(8,128)(2,1)S(1)}, u32[]{:S(2)}, u32[]{:S(2)}) collective-permute-start(bf16[128,1024]{1,0:T(8,128)(2,1)} %get-tuple-element.12), channel_id=1, source_target_pairs={{24,0},{25,1},{26,2},{27,3},{28,4},{29,5},{30,6},{31,7},{0,8},{1,9... | collective-permute-start | bytes 786440 | tf_op jit(solution)/shard_map/ppermute | solution.py:32
  52.3 19.2 %collective-permute-start.4 = (bf16[128,1024]{1,0:T(8,128)(2,1)}, bf16[128,1024]{1,0:T(8,128)(2,1)S(1)}, u32[]{:S(2)}, u32[]{:S(2)}) collective-permute-start(bf16[128,1024]{1,0:T(8,128)(2,1)} %get-tuple-element.12), channel_id=1, source_target_pairs={{16,0},{17,1},{18,2},{19,3},{20,4},{21,5},{22,6},{23,7},{24,8},{25... | collective-permute-start | bytes 786440 | tf_op jit(solution)/shard_map/ppermute | solution.py:32
  53.6 17.8 %collective-permute-start.3 = (bf16[128,1024]{1,0:T(8,128)(2,1)}, bf16[128,1024]{1,0:T(8,128)(2,1)S(1)}, u32[]{:S(2)}, u32[]{:S(2)}) collective-permute-start(bf16[128,1024]{1,0:T(8,128)(2,1)} %get-tuple-element.12), channel_id=1, source_target_pairs={{8,0},{9,1},{10,2},{11,3},{12,4},{13,5},{14,6},{15,7},{16,8},{17,9... | collective-permute-start | bytes 786440 | tf_op jit(solution)/shard_map/ppermute | solution.py:32
  75.6 8.2 %copy-start.8 = (s32[1,3]{1,0:T(1,128)S(1)}, s32[1,3]{1,0:T(1,128)}, u32[]{:S(2)}) copy-start(s32[1,3]{1,0:T(1,128)} %param.12) | copy-start | bytes 40
  78.8 56.0 %all-to-all-start.2 = ((bf16[8,160,1024]{2,1,0:T(8,128)(2,1)}), bf16[8,160,1024]{2,1,0:T(8,128)(2,1)}, u32[]{:S(2)}, u32[]{:S(2)}) async-start(bf16[8,160,1024]{2,1,0:T(8,128)(2,1)} %bitcast.100), calls=%async_computation.2 | async-start | bytes 5242880 | tf_op jit(solution)/shard_map/all_to_all | solution.py:36
  85.9 19.7 %collective-permute-start.8 = (bf16[128,2048]{1,0:T(8,128)(2,1)}, bf16[128,2048]{1,0:T(8,128)(2,1)}, u32[]{:S(2)}, u32[]{:S(2)}) collective-permute-start(bf16[128,2048]{1,0:T(8,128)(2,1)} %get-tuple-element.14), channel_id=1, source_target_pairs={{24,0},{25,1},{26,2},{27,3},{28,4},{29,5},{30,6},{31,7},{0,8},{1,9... | collective-permute-start | bytes 1572872 | tf_op jit(solution)/shard_map/ppermute | solution.py:32
  91.7 36.1 %collective-permute-start.7 = (bf16[128,2048]{1,0:T(8,128)(2,1)}, bf16[128,2048]{1,0:T(8,128)(2,1)}, u32[]{:S(2)}, u32[]{:S(2)}) collective-permute-start(bf16[128,2048]{1,0:T(8,128)(2,1)} %get-tuple-element.14), channel_id=1, source_target_pairs={{16,0},{17,1},{18,2},{19,3},{20,4},{21,5},{22,6},{23,7},{24,8},{25... | collective-permute-start | bytes 1572872 | tf_op jit(solution)/shard_map/ppermute | solution.py:32
  93.0 34.8 %collective-permute-start.6 = (bf16[128,2048]{1,0:T(8,128)(2,1)}, bf16[128,2048]{1,0:T(8,128)(2,1)}, u32[]{:S(2)}, u32[]{:S(2)}) collective-permute-start(bf16[128,2048]{1,0:T(8,128)(2,1)} %get-tuple-element.14), channel_id=1, source_target_pairs={{8,0},{9,1},{10,2},{11,3},{12,4},{13,5},{14,6},{15,7},{16,8},{17,9... | collective-permute-start | bytes 1572872 | tf_op jit(solution)/shard_map/ppermute | solution.py:32
  134.8 65.0 %all-to-all-start.4 = ((bf16[8,160,2048]{2,1,0:T(8,128)(2,1)}), bf16[8,160,2048]{2,1,0:T(8,128)(2,1)}, u32[]{:S(2)}, u32[]{:S(2)}) async-start(bf16[8,160,2048]{2,1,0:T(8,128)(2,1)} %bitcast.98), calls=%async_computation.4 | async-start | bytes 10485760 | tf_op jit(solution)/shard_map/all_to_all | solution.py:36
  141.7 2.7 copy-start.6
  144.4 6.2 %copy-start.4 = (bf16[1280,2048]{1,0:T(8,128)(2,1)}, bf16[1280,2048]{1,0:T(8,128)(2,1)S(1)}, u32[]{:S(2)}) copy-start(bf16[1280,2048]{1,0:T(8,128)(2,1)S(1)} %constant_dynamic-update-slice_fusion) | copy-start | bytes 15728644
  199.8 65.0 %all-to-all-start.3 = ((bf16[8,160,2048]{2,1,0:T(8,128)(2,1)}), bf16[8,160,2048]{2,1,0:T(8,128)(2,1)}, u32[]{:S(2)}, u32[]{:S(2)}) async-start(bf16[8,160,2048]{2,1,0:T(8,128)(2,1)} %bitcast.99), calls=%async_computation.3 | async-start | bytes 10485760 | tf_op jit(solution)/shard_map/all_to_all | solution.py:36
  211.8 8.7 %copy-start.7 = (bf16[1,768,2048]{2,1,0:T(8,128)(2,1)S(1)}, bf16[1,768,2048]{2,1,0:T(8,128)(2,1)}, u32[]{:S(2)}) copy-start(bf16[1,768,2048]{2,1,0:T(8,128)(2,1)} %param.15) | copy-start | bytes 9437188
  219.2 1.3 copy-start.9
  264.8 36.7 %all-to-all-start.6 = ((bf16[8,160,1024]{2,1,0:T(8,128)(2,1)}), bf16[8,160,1024]{2,1,0:T(8,128)(2,1)}, u32[]{:S(2)}, u32[]{:S(2)}) async-start(bf16[8,160,1024]{2,1,0:T(8,128)(2,1)} %bitcast.103), calls=%async_computation.6 | async-start | bytes 5242880 | tf_op jit(solution)/shard_map/all_to_all | solution.py:36
  301.5 36.7 %all-to-all-start.5 = ((bf16[8,160,1024]{2,1,0:T(8,128)(2,1)}), bf16[8,160,1024]{2,1,0:T(8,128)(2,1)}, u32[]{:S(2)}, u32[]{:S(2)}) async-start(bf16[8,160,1024]{2,1,0:T(8,128)(2,1)} %bitcast.101), calls=%async_computation.5 | async-start | bytes 5242880 | tf_op jit(solution)/shard_map/all_to_all | solution.py:36
  306.5 5.7 %copy-start.3 = (bf16[1280,512]{1,0:T(8,128)(2,1)}, bf16[1280,512]{1,0:T(8,128)(2,1)S(1)}, u32[]{:S(2)}) copy-start(bf16[1280,512]{1,0:T(8,128)(2,1)S(1)} %get-tuple-element.38) | copy-start | bytes 3932164
  306.5 20.2 %copy-start.1 = (bf16[1280,512]{1,0:T(8,128)(2,1)}, bf16[1280,512]{1,0:T(8,128)(2,1)S(1)}, u32[]{:S(2)}) copy-start(bf16[1280,512]{1,0:T(8,128)(2,1)S(1)} %get-tuple-element.39) | copy-start | bytes 3932164
  313.4 28.1 %collective-permute-start.11 = (bf16[128,2048]{1,0:T(8,128)(2,1)}, bf16[128,2048]{1,0:T(8,128)(2,1)}, u32[]{:S(2)}, u32[]{:S(2)}) collective-permute-start(bf16[128,2048]{1,0:T(8,128)(2,1)} %get-tuple-element.22), channel_id=1, source_target_pairs={{8,0},{9,1},{10,2},{11,3},{12,4},{13,5},{14,6},{15,7},{16,8},{17,9... | collective-permute-start | bytes 1572872 | tf_op jit(solution)/shard_map/ppermute | solution.py:32
  326.1 58.5 %collective-permute-start.10 = (bf16[128,2048]{1,0:T(8,128)(2,1)}, bf16[128,2048]{1,0:T(8,128)(2,1)}, u32[]{:S(2)}, u32[]{:S(2)}) collective-permute-start(bf16[128,2048]{1,0:T(8,128)(2,1)} %get-tuple-element.23), channel_id=1, source_target_pairs={{16,0},{17,1},{18,2},{19,3},{20,4},{21,5},{22,6},{23,7},{24,8},{25... | collective-permute-start | bytes 1572872 | tf_op jit(solution)/shard_map/ppermute | solution.py:32
  326.6 58.0 %collective-permute-start.9 = (bf16[128,2048]{1,0:T(8,128)(2,1)}, bf16[128,2048]{1,0:T(8,128)(2,1)}, u32[]{:S(2)}, u32[]{:S(2)}) collective-permute-start(bf16[128,2048]{1,0:T(8,128)(2,1)} %get-tuple-element.21), channel_id=1, source_target_pairs={{24,0},{25,1},{26,2},{27,3},{28,4},{29,5},{30,6},{31,7},{0,8},{1,9... | collective-permute-start | bytes 1572872 | tf_op jit(solution)/shard_map/ppermute | solution.py:32
  330.5 59.7 %collective-permute-start.17 = (bf16[128,1024]{1,0:T(8,128)(2,1)}, bf16[128,1024]{1,0:T(8,128)(2,1)}, u32[]{:S(2)}, u32[]{:S(2)}) collective-permute-start(bf16[128,1024]{1,0:T(8,128)(2,1)} %get-tuple-element.30), channel_id=1, source_target_pairs={{8,0},{9,1},{10,2},{11,3},{12,4},{13,5},{14,6},{15,7},{16,8},{17,9... | collective-permute-start | bytes 786440 | tf_op jit(solution)/shard_map/ppermute | solution.py:32
  334.3 72.8 %collective-permute-start.16 = (bf16[128,1024]{1,0:T(8,128)(2,1)}, bf16[128,1024]{1,0:T(8,128)(2,1)}, u32[]{:S(2)}, u32[]{:S(2)}) collective-permute-start(bf16[128,1024]{1,0:T(8,128)(2,1)} %get-tuple-element.31), channel_id=1, source_target_pairs={{16,0},{17,1},{18,2},{19,3},{20,4},{21,5},{22,6},{23,7},{24,8},{25... | collective-permute-start | bytes 786440 | tf_op jit(solution)/shard_map/ppermute | solution.py:32
  341.5 65.5 %collective-permute-start.15 = (bf16[128,1024]{1,0:T(8,128)(2,1)S(1)}, bf16[128,1024]{1,0:T(8,128)(2,1)S(1)}, u32[]{:S(2)}, u32[]{:S(2)}) collective-permute-start(bf16[128,1024]{1,0:T(8,128)(2,1)S(1)} %get-tuple-element.29), channel_id=1, source_target_pairs={{24,0},{25,1},{26,2},{27,3},{28,4},{29,5},{30,6},{31,7},{0,8},{1,9... | collective-permute-start | bytes 786440 | tf_op jit(solution)/shard_map/ppermute | solution.py:32
  384.6 24.9 %collective-permute-start.14 = (bf16[128,1024]{1,0:T(8,128)(2,1)S(1)}, bf16[128,1024]{1,0:T(8,128)(2,1)S(1)}, u32[]{:S(2)}, u32[]{:S(2)}) collective-permute-start(bf16[128,1024]{1,0:T(8,128)(2,1)S(1)} %get-tuple-element.27), channel_id=1, source_target_pairs={{8,0},{9,1},{10,2},{11,3},{12,4},{13,5},{14,6},{15,7},{16,8},{17,9... | collective-permute-start | bytes 786440 | tf_op jit(solution)/shard_map/ppermute | solution.py:32
  384.6 22.5 %copy-start.2 = (bf16[1280,512]{1,0:T(8,128)(2,1)S(1)}, bf16[1280,512]{1,0:T(8,128)(2,1)}, u32[]{:S(2)}) copy-start(bf16[1280,512]{1,0:T(8,128)(2,1)} %copy-done.1) | copy-start | bytes 3932164
  384.6 33.0 %collective-permute-start.13 = (bf16[128,1024]{1,0:T(8,128)(2,1)S(1)}, bf16[128,1024]{1,0:T(8,128)(2,1)S(1)}, u32[]{:S(2)}, u32[]{:S(2)}) collective-permute-start(bf16[128,1024]{1,0:T(8,128)(2,1)S(1)} %get-tuple-element.28), channel_id=1, source_target_pairs={{16,0},{17,1},{18,2},{19,3},{20,4},{21,5},{22,6},{23,7},{24,8},{25... | collective-permute-start | bytes 786440 | tf_op jit(solution)/shard_map/ppermute | solution.py:32
  390.2 27.4 %collective-permute-start.12 = (bf16[128,1024]{1,0:T(8,128)(2,1)S(1)}, bf16[128,1024]{1,0:T(8,128)(2,1)S(1)}, u32[]{:S(2)}, u32[]{:S(2)}) collective-permute-start(bf16[128,1024]{1,0:T(8,128)(2,1)S(1)} %get-tuple-element.26), channel_id=1, source_target_pairs={{24,0},{25,1},{26,2},{27,3},{28,4},{29,5},{30,6},{31,7},{0,8},{1,9... | collective-permute-start | bytes 786440 | tf_op jit(solution)/shard_map/ppermute | solution.py:32

commit v5 on v4

--- a/solution.py
+++ b/solution.py
@@ -37,6 +37,10 @@
             value, AXES, split_axis=0, concat_axis=0, tiled=True, axis_index_groups=groups
         )
         return value.reshape(plane_size * sent, value.shape[-1])
+
+    def known(value):
+        first = value[(0,) * value.ndim]
+        return first == first
 
     def split(value, parts):
         return jnp.split(value, parts, axis=-1)
@@ -107,38 +111,42 @@
         leaving.append(rows)
         slots.append(parts)
 
-    answers = []
+    def plane_sum(micro_index, back):
+        spread = jnp.where(matches[micro_index], weight[micro_index][:, None, :], 0.0)
+        spread = spread.astype(jnp.bfloat16).reshape(plane_size * sent, column)
+        contract = (((0,), (0,)), ((), ()))
+        others = lax.dot_general(
+            spread[:, tok_local:], back, contract, preferred_element_type=jnp.float32
+        ).astype(jnp.bfloat16)
+        own = lax.dot_general(
+            spread[:, :tok_local], back, contract, preferred_element_type=jnp.float32
+        )
+        return others.reshape(planes - 1, tok_local, back.shape[1]), own
+
+    sums = []
     for micro_index in range(micro_count):
-        rows = slots[micro_index]
-        if micro_index + 1 < micro_count:
-            rows, leaving[micro_index + 1] = lax.optimization_barrier(
-                (rows, leaving[micro_index + 1])
-            )
-        rows = jnp.concatenate(rows, 1)
+        rows = jnp.concatenate(slots[micro_index], 1)
         gate_val = jnp.dot(rows, w_gate[0], preferred_element_type=jnp.float32)
         up_val = jnp.dot(rows, w_up[0], preferred_element_type=jnp.float32)
         hidden = (jax.nn.silu(gate_val) * up_val).astype(jnp.bfloat16)
         parts = []
         for down in split(w_down[0], cuts_back[micro_index]):
+            shown = live[:, micro_index]
+            if micro_index + 1 < micro_count:
+                shown = shown & known(leaving[micro_index + 1])
+            if parts and sums:
+                shown = shown & known(sums[-1][-1][0]) & known(out)
             out = jnp.dot(hidden, down, preferred_element_type=jnp.float32)
-            out = jnp.where(live[:, micro_index][:, None], out, 0.0).astype(jnp.bfloat16)
-            parts.append(swap(out))
-        answers.append(parts)
+            out = jnp.where(shown[:, None], out, 0.0).astype(jnp.bfloat16)
+            parts.append(plane_sum(micro_index, swap(out)))
+        sums.append(parts)
 
     results = []
     for micro_index in range(micro_count):
-        spread = jnp.where(matches[micro_index], weight[micro_index][:, None, :], 0.0)
-        spread = spread.astype(jnp.bfloat16).reshape(plane_size * sent, column)
         parts = []
-        for back in answers[micro_index]:
-            contract = (((0,), (0,)), ((), ()))
-            others = lax.dot_general(
-                spread[:, tok_local:], back, contract, preferred_element_type=jnp.float32
-            ).astype(jnp.bfloat16)
-            others = others.reshape(planes - 1, tok_local, back.shape[1])
-            total = lax.dot_general(
-                spread[:, :tok_local], back, contract, preferred_element_type=jnp.float32
-            )
+        for others, total in sums[micro_index]:
+            if results:
+                others = jnp.where(known(results[-1]), others, 0)
             for step in range(1, planes):
                 total = total + shift(others[step - 1], -step).astype(jnp.float32)
             parts.append(total.astype(jnp.bfloat16))

time: 422 us -> 436 us (1.033)
  waiting for transfers between devices: 220 us -> 247 us
  starting transfers between devices: 98.8 us -> 77.5 us
  between operations: 1.63 us -> 6.76 us
    ppermute x18, waiting for transfers between devices: 105 us -> 147 us  [shift(): return lax.ppermute(value, AXES, pairs)]
    ppermute x18, starting transfers between devices: 64.2 us -> 42.7 us  [shift(): return lax.ppermute(value, AXES, pairs)]
    all_to_all x6, waiting for transfers between devices: 108 us -> 101 us  [swap(): lax.all_to_all(value, AXES, split_axis=0, concat_axis=0, tiled=True, axis...]
    all_to_all x1, waiting for transfers between devices: 6.6 us -> 0.01 us  [body(): lax.all_to_all(jnp.concatenate([toward, tally], 2), AXES, split_axis=0, c...]
  transfers between devices with their start and end apart: 25 -> 25, of which waited for: 15 -> 14; matrix products, arithmetic and copies ran while one was open for 21% -> 20% of each run, Pallas kernels for 0% -> 0%
where the time goes in v5:
time: 436 us; the launch traced here: 435 us
  waiting for transfers between devices  247 us (57%)
  matrix products  81.4 us (19%)
  starting transfers between devices  77.5 us (18%)
  local copies, waits for them, and re-layouts  14.2 us (3%)
  other arithmetic  7.89 us (2%)
  between operations  6.76 us (2%)
    ppermute x18, waiting for transfers between devices, shift(): return lax.ppermute(value, AXES, pairs)  147 us
    all_to_all x6, waiting for transfers between devices, swap(): lax.all_to_all(value, AXES, split_axis=0, concat_axis=0, tiled=True, axis...  101 us
    ppermute x18, starting transfers between devices, shift(): return lax.ppermute(value, AXES, pairs)  42.7 us
    all_to_all x6, starting transfers between devices, swap(): lax.all_to_all(value, AXES, split_axis=0, concat_axis=0, tiled=True, axis...  27.6 us
    dot_general x3, matrix products, body(): out = jnp.dot(hidden, down, preferred_element_type=jnp.float32)  22.1 us
    dot_general x2, matrix products, body(): gate_val = jnp.dot(rows, w_gate[0], preferred_element_type=jnp.float32)  16.7 us
    dot_general x3, matrix products, body(): jnp.dot(select, jnp.concatenate(holder, 0), preferred_element_type=jnp.fl...  15.4 us
    dot_general x3, matrix products, plane_sum(): lax.dot_general(spread[:, tok_local:], back, contract, preferred_element_...  11.2 us
  transfers between devices with their start and end apart: 25, of which 14 were waited for; matrix products, arithmetic and copies ran while one was open for 20% of the time, Pallas kernels for 0%

profile of v5, /device:TPU:0, one launch (start us, length us, event | category | flops | bytes accessed | tf_op | source)
XLA Modules:
  0.0 435.2 jit_solution(14425823571439496985)
XLA Ops:
  3.0 7.3 %all-to-all-start = ((f32[32,2,9,128]{3,1,2,0:T(2,128)}), f32[32,2,9,128]{3,1,2,0:T(2,128)S(1)}, u32[]{:S(2)}, u32[]{:S(2)}) async-start(f32[32,2,9,128]{3,1,2,0:T(2,128)} %copy.33), calls=%async_computation | async-start | bytes 589824 | tf_op jit(solution)/shard_map/all_to_all | solution.py:73
  10.3 2.1 slice_bitcast_fusion
  13.9 1.8 collective-permute-start
  15.6 9.7 %collective-permute-done = bf16[128,1024]{1,0:T(8,128)(2,1)S(1)} collective-permute-done((bf16[128,1024]{1,0:T(8,128)(2,1)S(1)}, bf16[128,1024]{1,0:T(8,128)(2,1)S(1)}, u32[]{:S(2)}, u32[]{:S(2)}) %collective-permute-start) | collective-permute-done | bytes 262176 | tf_op jit(solution)/shard_map/ppermute | solution.py:32
  26.2 1.9 collective-permute-start.8
  28.1 2.2 collective-permute-start.7
  30.2 7.3 %collective-permute-done.1 = bf16[128,1024]{1,0:T(8,128)(2,1)} collective-permute-done((bf16[128,1024]{1,0:T(8,128)(2,1)}, bf16[128,1024]{1,0:T(8,128)(2,1)}, u32[]{:S(2)}, u32[]{:S(2)}) %collective-permute-start.1) | collective-permute-done | bytes 262176 | tf_op jit(solution)/shard_map/ppermute | solution.py:32
  39.4 8.1 %collective-permute-done.8 = bf16[128,1024]{1,0:T(8,128)(2,1)} collective-permute-done((bf16[128,1024]{1,0:T(8,128)(2,1)}, bf16[128,1024]{1,0:T(8,128)(2,1)}, u32[]{:S(2)}, u32[]{:S(2)}) %collective-permute-start.8) | collective-permute-done | bytes 262176 | tf_op jit(solution)/shard_map/ppermute | solution.py:32
  47.5 4.2 convolution_convert_fusion.1
  51.7 4.4 %all-to-all-start.2 = ((bf16[8,160,1024]{2,1,0:T(8,128)(2,1)}), bf16[8,160,1024]{2,1,0:T(8,128)(2,1)}, u32[]{:S(2)}, u32[]{:S(2)}) async-start(bf16[8,160,1024]{2,1,0:T(8,128)(2,1)} %bitcast.105), calls=%async_computation.2 | async-start | bytes 5242880 | tf_op jit(solution)/shard_map/all_to_all | solution.py:36
  56.1 4.3 collective-permute-start.6
  60.4 3.4 collective-permute-start.5
  63.8 9.5 %collective-permute-done.6 = bf16[128,1024]{1,0:T(8,128)(2,1)S(1)} collective-permute-done((bf16[128,1024]{1,0:T(8,128)(2,1)}, bf16[128,1024]{1,0:T(8,128)(2,1)S(1)}, u32[]{:S(2)}, u32[]{:S(2)}) %collective-permute-start.6) | collective-permute-done | bytes 262176 | tf_op jit(solution)/shard_map/ppermute | solution.py:32
  73.3 4.3 convolution_convert_fusion.2
  77.6 10.8 %all-to-all-done.2 = bf16[8,160,1024]{2,1,0:T(8,128)(2,1)} async-done(((bf16[8,160,1024]{2,1,0:T(8,128)(2,1)}), bf16[8,160,1024]{2,1,0:T(8,128)(2,1)}, u32[]{:S(2)}, u32[]{:S(2)}) %all-to-all-start.2) | async-done | bytes 2621472 | tf_op jit(solution)/shard_map/all_to_all | solution.py:36
  88.4 4.5 %all-to-all-start.1 = ((bf16[8,160,1024]{2,1,0:T(8,128)(2,1)}), bf16[8,160,1024]{2,1,0:T(8,128)(2,1)}, u32[]{:S(2)}, u32[]{:S(2)}) async-start(bf16[8,160,1024]{2,1,0:T(8,128)(2,1)} %bitcast.103), calls=%async_computation.1 | async-start | bytes 5242880 | tf_op jit(solution)/shard_map/all_to_all | solution.py:36
  95.0 5.3 %collective-permute-start.4 = (bf16[128,2048]{1,0:T(8,128)(2,1)}, bf16[128,2048]{1,0:T(8,128)(2,1)}, u32[]{:S(2)}, u32[]{:S(2)}) collective-permute-start(bf16[128,2048]{1,0:T(8,128)(2,1)} %get-tuple-element.10), channel_id=1, source_target_pairs={{24,0},{25,1},{26,2},{27,3},{28,4},{29,5},{30,6},{31,7},{0,8},{1,9... | collective-permute-start | bytes 1572872 | tf_op jit(solution)/shard_map/ppermute | solution.py:32
  103.7 10.6 %collective-permute-done.4 = bf16[128,2048]{1,0:T(8,128)(2,1)} collective-permute-done((bf16[128,2048]{1,0:T(8,128)(2,1)}, bf16[128,2048]{1,0:T(8,128)(2,1)}, u32[]{:S(2)}, u32[]{:S(2)}) %collective-permute-start.4) | collective-permute-done | bytes 524320 | tf_op jit(solution)/shard_map/ppermute | solution.py:32
  114.2 22.2 %collective-permute-done.3 = bf16[128,2048]{1,0:T(8,128)(2,1)} collective-permute-done((bf16[128,2048]{1,0:T(8,128)(2,1)}, bf16[128,2048]{1,0:T(8,128)(2,1)}, u32[]{:S(2)}, u32[]{:S(2)}) %collective-permute-start.3) | collective-permute-done | bytes 524320 | tf_op jit(solution)/shard_map/ppermute | solution.py:32
  136.4 6.9 %convolution_convert_fusion = bf16[1280,2048]{1,0:T(8,128)(2,1)} fusion(pred[1280,512]{1,0:T(32,128)(4,1)} %get-tuple-element.37, bf16[128,2048]{1,0:T(8,128)(2,1)} %collective-permute-done.4, bf16[128,2048]{1,0:T(8,128)(2,1)} %collective-permute-done.3, bf16[128,2048]{1,0:T(8,128)(2,1)} %collective-permute-done.2, bf16[128,2048]{1,0:T(8,128)(2,1)} %get-tuple-element.10), kind=kOutput, calls=%fused_computation.1 | convolution fusion | flops 2695364608 | bytes 7995392 | tf_op jit(solution)/shard_map/dot_general | solution.py:107
  143.3 5.0 %all-to-all-start.4 = ((bf16[8,160,2048]{2,1,0:T(8,128)(2,1)}), bf16[8,160,2048]{2,1,0:T(8,128)(2,1)}, u32[]{:S(2)}, u32[]{:S(2)}) async-start(bf16[8,160,2048]{2,1,0:T(8,128)(2,1)} %bitcast.100), calls=%async_computation.4 | async-start | bytes 10485760 | tf_op jit(solution)/shard_map/all_to_all | solution.py:36
  151.2 9.6 %fusion.2 = f32[1280,768]{1,0:T(8,128)} fusion(bf16[1280,1024]{1,0:T(8,128)(2,1)} %bitcast.23, bf16[1280,1024]{1,0:T(8,128)(2,1)} %bitcast.21, bf16[1,2048,768]{2,1,0:T(8,128)(2,1)} %param.13), kind=kOutput, calls=%fused_computation.11 | convolution fusion | flops 4037017600 | bytes 12320768 | tf_op jit(solution)/shard_map/dot_general | solution.py:129
  160.8 14.5 %select_convert_fusion = bf16[1280,2048]{1,0:T(8,128)(2,1)} fusion(pred[1280]{0:T(1024)(128)(4,1)S(1)} %get-tuple-element.15, f32[1280,768]{1,0:T(8,128)} %fusion.2, bf16[1280,1024]{1,0:T(8,128)(2,1)} %bitcast.23, bf16[1280,1024]{1,0:T(8,128)(2,1)} %bitcast.21, bf16[1,2048,768]{2,1,0:T(8,128)(2,1)S(1)} %copy-done, bf16[1,768,2048]{2,1,0:T(8,128)(2,1)} %param.15), kind=kOutput, calls=%fused_computation | convolution fusion | flops 8074690560 | bytes 20710656 | tf_op jit(solution)/shard_map/dot_general | solution.py:139
  175.4 33.1 %all-to-all-done.4 = bf16[8,160,2048]{2,1,0:T(8,128)(2,1)} async-done(((bf16[8,160,2048]{2,1,0:T(8,128)(2,1)}), bf16[8,160,2048]{2,1,0:T(8,128)(2,1)}, u32[]{:S(2)}, u32[]{:S(2)}) %all-to-all-start.4) | async-done | bytes 5242912 | tf_op jit(solution)/shard_map/all_to_all | solution.py:36
  208.5 4.9 %all-to-all-start.3 = ((bf16[8,160,2048]{2,1,0:T(8,128)(2,1)}), bf16[8,160,2048]{2,1,0:T(8,128)(2,1)}, u32[]{:S(2)}, u32[]{:S(2)}) async-start(bf16[8,160,2048]{2,1,0:T(8,128)(2,1)} %bitcast.101), calls=%async_computation.3 | async-start | bytes 10485760 | tf_op jit(solution)/shard_map/all_to_all | solution.py:36
  213.3 7.1 %fusion.5 = f32[1280,768]{1,0:T(8,128)S(1)} fusion(bf16[1280,2048]{1,0:T(8,128)(2,1)} %bitcast.33, bf16[1,2048,768]{2,1,0:T(8,128)(2,1)} %param.13), kind=kOutput, calls=%fused_computation.14 | convolution fusion | flops 4026531840 | bytes 12320768 | tf_op jit(solution)/shard_map/dot_general | solution.py:129
  220.5 7.4 %fusion.1 = bf16[1280,768]{1,0:T(8,128)(2,1)S(1)} fusion(bf16[1280,2048]{1,0:T(8,128)(2,1)} %bitcast.33, f32[1280,768]{1,0:T(8,128)S(1)} %fusion.5, bf16[1,2048,768]{2,1,0:T(8,128)(2,1)S(1)} %copy-done), kind=kOutput, calls=%fused_computation.10 | convolution fusion | flops 4032430080 | bytes 14286848 | tf_op jit(solution)/shard_map/dot_general | solution.py:130
  229.1 3.8 select_convert_fusion.2
  232.9 40.5 %all-to-all-done.3 = bf16[8,160,2048]{2,1,0:T(8,128)(2,1)} async-done(((bf16[8,160,2048]{2,1,0:T(8,128)(2,1)}), bf16[8,160,2048]{2,1,0:T(8,128)(2,1)}, u32[]{:S(2)}, u32[]{:S(2)}) %all-to-all-start.3) | async-done | bytes 5242912 | tf_op jit(solution)/shard_map/all_to_all | solution.py:36
  273.5 4.4 %all-to-all-start.5 = ((bf16[8,160,1024]{2,1,0:T(8,128)(2,1)}), bf16[8,160,1024]{2,1,0:T(8,128)(2,1)}, u32[]{:S(2)}, u32[]{:S(2)}) async-start(bf16[8,160,1024]{2,1,0:T(8,128)(2,1)} %bitcast.104), calls=%async_computation.5 | async-start | bytes 5242880 | tf_op jit(solution)/shard_map/all_to_all | solution.py:36
  282.0 4.9 %convolution_convert_fusion.3 = bf16[384,2048]{1,0:T(8,128)(2,1)S(1)} fusion(bf16[1280,2048]{1,0:T(8,128)(2,1)} %bitcast.28, bf16[1280,512]{1,0:T(8,128)(2,1)S(1)} %get-tuple-element.35), kind=kOutput, calls=%fused_computation.17 | convolution fusion | flops 2014052352 | bytes 7798784 | tf_op jit(solution)/shard_map/dot_general | solution.py:118
  289.9 3.8 select_convert_fusion.1
  293.8 16.4 %all-to-all-done.5 = bf16[8,160,1024]{2,1,0:T(8,128)(2,1)} async-done(((bf16[8,160,1024]{2,1,0:T(8,128)(2,1)}), bf16[8,160,1024]{2,1,0:T(8,128)(2,1)}, u32[]{:S(2)}, u32[]{:S(2)}) %all-to-all-start.5) | async-done | bytes 2621472 | tf_op jit(solution)/shard_map/all_to_all | solution.py:36
  310.1 4.4 %all-to-all-start.6 = ((bf16[8,160,1024]{2,1,0:T(8,128)(2,1)}), bf16[8,160,1024]{2,1,0:T(8,128)(2,1)}, u32[]{:S(2)}, u32[]{:S(2)}) async-start(bf16[8,160,1024]{2,1,0:T(8,128)(2,1)} %bitcast.102), calls=%async_computation.6 | async-start | bytes 5242880 | tf_op jit(solution)/shard_map/all_to_all | solution.py:36
  316.1 12.9 %collective-permute-start.11 = (bf16[128,2048]{1,0:T(8,128)(2,1)S(1)}, bf16[128,2048]{1,0:T(8,128)(2,1)S(1)}, u32[]{:S(2)}, u32[]{:S(2)}) collective-permute-start(bf16[128,2048]{1,0:T(8,128)(2,1)S(1)} %get-tuple-element.18), channel_id=1, source_target_pairs={{8,0},{9,1},{10,2},{11,3},{12,4},{13,5},{14,6},{15,7},{16,8},{17,9... | collective-permute-start | bytes 1572872 | tf_op jit(solution)/shard_map/ppermute | solution.py:32
  329.6 11.7 %collective-permute-done.11 = bf16[128,2048]{1,0:T(8,128)(2,1)S(1)} collective-permute-done((bf16[128,2048]{1,0:T(8,128)(2,1)S(1)}, bf16[128,2048]{1,0:T(8,128)(2,1)S(1)}, u32[]{:S(2)}, u32[]{:S(2)}) %collective-permute-start.11) | collective-permute-done | bytes 524320 | tf_op jit(solution)/shard_map/ppermute | solution.py:32
  341.3 33.9 %collective-permute-done.10 = bf16[128,2048]{1,0:T(8,128)(2,1)S(1)} collective-permute-done((bf16[128,2048]{1,0:T(8,128)(2,1)S(1)}, bf16[128,2048]{1,0:T(8,128)(2,1)S(1)}, u32[]{:S(2)}, u32[]{:S(2)}) %collective-permute-start.10) | collective-permute-done | bytes 524320 | tf_op jit(solution)/shard_map/ppermute | solution.py:32
  375.2 3.7 add_convert_fusion
  380.5 2.9 fusion.21
  384.3 1.8 collective-permute-start.13
  386.1 2.0 collective-permute-start.12
  388.2 3.3 fusion.22
  391.6 1.9 collective-permute-start.17
  393.4 2.1 collective-permute-start.15
  395.6 16.2 %collective-permute-done.13 = bf16[128,1024]{1,0:T(8,128)(2,1)} collective-permute-done((bf16[128,1024]{1,0:T(8,128)(2,1)}, bf16[128,1024]{1,0:T(8,128)(2,1)}, u32[]{:S(2)}, u32[]{:S(2)}) %collective-permute-start.13) | collective-permute-done | bytes 262176 | tf_op jit(solution)/shard_map/ppermute | solution.py:32
  411.8 2.5 add_convert_fusion.2
  414.4 17.3 %collective-permute-done.16 = bf16[128,1024]{1,0:T(8,128)(2,1)S(1)} collective-permute-done((bf16[128,1024]{1,0:T(8,128)(2,1)S(1)}, bf16[128,1024]{1,0:T(8,128)(2,1)S(1)}, u32[]{:S(2)}, u32[]{:S(2)}) %collective-permute-start.16) | collective-permute-done | bytes 262176 | tf_op jit(solution)/shard_map/ppermute | solution.py:32
  431.7 2.3 add_convert_fusion.1
  (96 shorter events, 23.2 us)
Async XLA Ops:
  0.0 160.8 %copy-start = (bf16[1,2048,768]{2,1,0:T(8,128)(2,1)S(1)}, bf16[1,2048,768]{2,1,0:T(8,128)(2,1)}, u32[]{:S(2)}) copy-start(bf16[1,2048,768]{2,1,0:T(8,128)(2,1)} %param.14) | copy-start | bytes 9437188
  3.0 34.5 %all-to-all-start = ((f32[32,2,9,128]{3,1,2,0:T(2,128)}), f32[32,2,9,128]{3,1,2,0:T(2,128)S(1)}, u32[]{:S(2)}, u32[]{:S(2)}) async-start(f32[32,2,9,128]{3,1,2,0:T(2,128)} %copy.33), calls=%async_computation | async-start | bytes 589824 | tf_op jit(solution)/shard_map/all_to_all | solution.py:73
  13.2 0.7 copy-start.8
  13.9 11.5 %collective-permute-start = (bf16[128,1024]{1,0:T(8,128)(2,1)S(1)}, bf16[128,1024]{1,0:T(8,128)(2,1)S(1)}, u32[]{:S(2)}, u32[]{:S(2)}) collective-permute-start(bf16[128,1024]{1,0:T(8,128)(2,1)S(1)} %get-tuple-element.28), channel_id=1, source_target_pairs={{24,0},{25,1},{26,2},{27,3},{28,4},{29,5},{30,6},{31,7},{0,8},{1,9... | collective-permute-start | bytes 786440 | tf_op jit(solution)/shard_map/ppermute | solution.py:32
  25.4 0.7 copy-start.12
  26.1 11.4 %collective-permute-start.1 = (bf16[128,1024]{1,0:T(8,128)(2,1)}, bf16[128,1024]{1,0:T(8,128)(2,1)}, u32[]{:S(2)}, u32[]{:S(2)}) collective-permute-start(bf16[128,1024]{1,0:T(8,128)(2,1)} %get-tuple-element.9), channel_id=1, source_target_pairs={{24,0},{25,1},{26,2},{27,3},{28,4},{29,5},{30,6},{31,7},{0,8},{1,9... | collective-permute-start | bytes 786440 | tf_op jit(solution)/shard_map/ppermute | solution.py:32
  26.2 21.3 %collective-permute-start.8 = (bf16[128,1024]{1,0:T(8,128)(2,1)}, bf16[128,1024]{1,0:T(8,128)(2,1)}, u32[]{:S(2)}, u32[]{:S(2)}) collective-permute-start(bf16[128,1024]{1,0:T(8,128)(2,1)} %get-tuple-element.9), channel_id=1, source_target_pairs={{16,0},{17,1},{18,2},{19,3},{20,4},{21,5},{22,6},{23,7},{24,8},{25... | collective-permute-start | bytes 786440 | tf_op jit(solution)/shard_map/ppermute | solution.py:32
  28.1 19.4 %collective-permute-start.7 = (bf16[128,1024]{1,0:T(8,128)(2,1)}, bf16[128,1024]{1,0:T(8,128)(2,1)}, u32[]{:S(2)}, u32[]{:S(2)}) collective-permute-start(bf16[128,1024]{1,0:T(8,128)(2,1)} %get-tuple-element.9), channel_id=1, source_target_pairs={{8,0},{9,1},{10,2},{11,3},{12,4},{13,5},{14,6},{15,7},{16,8},{17,9... | collective-permute-start | bytes 786440 | tf_op jit(solution)/shard_map/ppermute | solution.py:32
  39.4 12.3 %copy-start.7 = (pred[1280,512]{1,0:T(32,128)(4,1)}, pred[1280,512]{1,0:T(32,128)(4,1)S(1)}, u32[]{:S(2)}) copy-start(pred[1280,512]{1,0:T(32,128)(4,1)S(1)} %get-tuple-element.36) | copy-start | bytes 1966084
  51.7 36.7 %all-to-all-start.2 = ((bf16[8,160,1024]{2,1,0:T(8,128)(2,1)}), bf16[8,160,1024]{2,1,0:T(8,128)(2,1)}, u32[]{:S(2)}, u32[]{:S(2)}) async-start(bf16[8,160,1024]{2,1,0:T(8,128)(2,1)} %bitcast.105), calls=%async_computation.2 | async-start | bytes 5242880 | tf_op jit(solution)/shard_map/all_to_all | solution.py:36
  56.1 17.2 %collective-permute-start.6 = (bf16[128,1024]{1,0:T(8,128)(2,1)}, bf16[128,1024]{1,0:T(8,128)(2,1)S(1)}, u32[]{:S(2)}, u32[]{:S(2)}) collective-permute-start(bf16[128,1024]{1,0:T(8,128)(2,1)} %copy-done.8), channel_id=1, source_target_pairs={{16,0},{17,1},{18,2},{19,3},{20,4},{21,5},{22,6},{23,7},{24,8},{25... | collective-permute-start | bytes 786440 | tf_op jit(solution)/shard_map/ppermute | solution.py:32
  60.4 12.9 %collective-permute-start.5 = (bf16[128,1024]{1,0:T(8,128)(2,1)}, bf16[128,1024]{1,0:T(8,128)(2,1)S(1)}, u32[]{:S(2)}, u32[]{:S(2)}) collective-permute-start(bf16[128,1024]{1,0:T(8,128)(2,1)} %copy-done.8), channel_id=1, source_target_pairs={{8,0},{9,1},{10,2},{11,3},{12,4},{13,5},{14,6},{15,7},{16,8},{17,9... | collective-permute-start | bytes 786440 | tf_op jit(solution)/shard_map/ppermute | solution.py:32
  88.4 5.2 %copy-start.13 = (s32[1,3]{1,0:T(1,128)S(1)}, s32[1,3]{1,0:T(1,128)}, u32[]{:S(2)}) copy-start(s32[1,3]{1,0:T(1,128)} %param.12) | copy-start | bytes 40
  88.4 54.9 %all-to-all-start.1 = ((bf16[8,160,1024]{2,1,0:T(8,128)(2,1)}), bf16[8,160,1024]{2,1,0:T(8,128)(2,1)}, u32[]{:S(2)}, u32[]{:S(2)}) async-start(bf16[8,160,1024]{2,1,0:T(8,128)(2,1)} %bitcast.103), calls=%async_computation.1 | async-start | bytes 5242880 | tf_op jit(solution)/shard_map/all_to_all | solution.py:36
  95.0 19.2 %collective-permute-start.4 = (bf16[128,2048]{1,0:T(8,128)(2,1)}, bf16[128,2048]{1,0:T(8,128)(2,1)}, u32[]{:S(2)}, u32[]{:S(2)}) collective-permute-start(bf16[128,2048]{1,0:T(8,128)(2,1)} %get-tuple-element.10), channel_id=1, source_target_pairs={{24,0},{25,1},{26,2},{27,3},{28,4},{29,5},{30,6},{31,7},{0,8},{1,9... | collective-permute-start | bytes 1572872 | tf_op jit(solution)/shard_map/ppermute | solution.py:32
  100.4 36.0 %collective-permute-start.3 = (bf16[128,2048]{1,0:T(8,128)(2,1)}, bf16[128,2048]{1,0:T(8,128)(2,1)}, u32[]{:S(2)}, u32[]{:S(2)}) collective-permute-start(bf16[128,2048]{1,0:T(8,128)(2,1)} %get-tuple-element.10), channel_id=1, source_target_pairs={{16,0},{17,1},{18,2},{19,3},{20,4},{21,5},{22,6},{23,7},{24,8},{25... | collective-permute-start | bytes 1572872 | tf_op jit(solution)/shard_map/ppermute | solution.py:32
  101.6 34.8 %collective-permute-start.2 = (bf16[128,2048]{1,0:T(8,128)(2,1)}, bf16[128,2048]{1,0:T(8,128)(2,1)}, u32[]{:S(2)}, u32[]{:S(2)}) collective-permute-start(bf16[128,2048]{1,0:T(8,128)(2,1)} %get-tuple-element.10), channel_id=1, source_target_pairs={{8,0},{9,1},{10,2},{11,3},{12,4},{13,5},{14,6},{15,7},{16,8},{17,9... | collective-permute-start | bytes 1572872 | tf_op jit(solution)/shard_map/ppermute | solution.py:32
  143.3 5.0 %copy-start.9 = (pred[8,4,32]{2,0,1:T(8,128)(4,1)S(1)}, pred[8,4,32]{2,0,1:T(8,128)(4,1)}, u32[]{:S(2)}) copy-start(pred[8,4,32]{2,0,1:T(8,128)(4,1)} %iota_compare_fusion.2) | copy-start | bytes 3076
  143.3 65.2 %all-to-all-start.4 = ((bf16[8,160,2048]{2,1,0:T(8,128)(2,1)}), bf16[8,160,2048]{2,1,0:T(8,128)(2,1)}, u32[]{:S(2)}, u32[]{:S(2)}) async-start(bf16[8,160,2048]{2,1,0:T(8,128)(2,1)} %bitcast.100), calls=%async_computation.4 | async-start | bytes 10485760 | tf_op jit(solution)/shard_map/all_to_all | solution.py:36
  208.5 65.0 %all-to-all-start.3 = ((bf16[8,160,2048]{2,1,0:T(8,128)(2,1)}), bf16[8,160,2048]{2,1,0:T(8,128)(2,1)}, u32[]{:S(2)}, u32[]{:S(2)}) async-start(bf16[8,160,2048]{2,1,0:T(8,128)(2,1)} %bitcast.101), calls=%async_computation.3 | async-start | bytes 10485760 | tf_op jit(solution)/shard_map/all_to_all | solution.py:36
  220.4 8.7 %copy-start.10 = (bf16[1,768,2048]{2,1,0:T(8,128)(2,1)S(1)}, bf16[1,768,2048]{2,1,0:T(8,128)(2,1)}, u32[]{:S(2)}) copy-start(bf16[1,768,2048]{2,1,0:T(8,128)(2,1)} %param.15) | copy-start | bytes 9437188
  227.8 1.3 copy-start.14
  273.5 36.7 %all-to-all-start.5 = ((bf16[8,160,1024]{2,1,0:T(8,128)(2,1)}), bf16[8,160,1024]{2,1,0:T(8,128)(2,1)}, u32[]{:S(2)}, u32[]{:S(2)}) async-start(bf16[8,160,1024]{2,1,0:T(8,128)(2,1)} %bitcast.104), calls=%async_computation.5 | async-start | bytes 5242880 | tf_op jit(solution)/shard_map/all_to_all | solution.py:36
  279.5 7.4 %copy-start.3 = (bf16[1280,512]{1,0:T(8,128)(2,1)}, bf16[1280,512]{1,0:T(8,128)(2,1)S(1)}, u32[]{:S(2)}) copy-start(bf16[1280,512]{1,0:T(8,128)(2,1)S(1)} %get-tuple-element.35) | copy-start | bytes 3932164
  282.0 8.0 %copy-start.11 = (bf16[1,768,2048]{2,1,0:T(8,128)(2,1)S(1)}, bf16[1,768,2048]{2,1,0:T(8,128)(2,1)}, u32[]{:S(2)}) copy-start(bf16[1,768,2048]{2,1,0:T(8,128)(2,1)} %param.15) | copy-start | bytes 9437188
  282.0 8.0 %copy-start.15 = (bf16[1280,768]{1,0:T(8,128)(2,1)S(1)}, bf16[1280,768]{1,0:T(8,128)(2,1)}, u32[]{:S(2)}) copy-start(bf16[1280,768]{1,0:T(8,128)(2,1)} %copy-done.14) | copy-start | bytes 5898244
  286.9 1.1 copy-start.6
  310.1 78.0 %all-to-all-start.6 = ((bf16[8,160,1024]{2,1,0:T(8,128)(2,1)}), bf16[8,160,1024]{2,1,0:T(8,128)(2,1)}, u32[]{:S(2)}, u32[]{:S(2)}) async-start(bf16[8,160,1024]{2,1,0:T(8,128)(2,1)} %bitcast.102), calls=%async_computation.6 | async-start | bytes 5242880 | tf_op jit(solution)/shard_map/all_to_all | solution.py:36
  316.1 25.2 %collective-permute-start.11 = (bf16[128,2048]{1,0:T(8,128)(2,1)S(1)}, bf16[128,2048]{1,0:T(8,128)(2,1)S(1)}, u32[]{:S(2)}, u32[]{:S(2)}) collective-permute-start(bf16[128,2048]{1,0:T(8,128)(2,1)S(1)} %get-tuple-element.18), channel_id=1, source_target_pairs={{8,0},{9,1},{10,2},{11,3},{12,4},{13,5},{14,6},{15,7},{16,8},{17,9... | collective-permute-start | bytes 1572872 | tf_op jit(solution)/shard_map/ppermute | solution.py:32
  329.0 46.2 %collective-permute-start.10 = (bf16[128,2048]{1,0:T(8,128)(2,1)S(1)}, bf16[128,2048]{1,0:T(8,128)(2,1)S(1)}, u32[]{:S(2)}, u32[]{:S(2)}) collective-permute-start(bf16[128,2048]{1,0:T(8,128)(2,1)S(1)} %get-tuple-element.19), channel_id=1, source_target_pairs={{16,0},{17,1},{18,2},{19,3},{20,4},{21,5},{22,6},{23,7},{24,8},{25... | collective-permute-start | bytes 1572872 | tf_op jit(solution)/shard_map/ppermute | solution.py:32
  329.3 51.2 %copy-start.1 = (bf16[1280,512]{1,0:T(8,128)(2,1)S(1)}, bf16[1280,512]{1,0:T(8,128)(2,1)}, u32[]{:S(2)}) copy-start(bf16[1280,512]{1,0:T(8,128)(2,1)} %get-tuple-element.34) | copy-start | bytes 3932164
  329.3 45.9 %collective-permute-start.9 = (bf16[128,2048]{1,0:T(8,128)(2,1)S(1)}, bf16[128,2048]{1,0:T(8,128)(2,1)S(1)}, u32[]{:S(2)}, u32[]{:S(2)}) collective-permute-start(bf16[128,2048]{1,0:T(8,128)(2,1)S(1)} %get-tuple-element.17), channel_id=1, source_target_pairs={{24,0},{25,1},{26,2},{27,3},{28,4},{29,5},{30,6},{31,7},{0,8},{1,9... | collective-permute-start | bytes 1572872 | tf_op jit(solution)/shard_map/ppermute | solution.py:32
  378.9 5.5 %copy-start.4 = (bf16[128,2048]{1,0:T(8,128)(2,1)}, bf16[128,2048]{1,0:T(8,128)(2,1)S(1)}, u32[]{:S(2)}) copy-start(bf16[128,2048]{1,0:T(8,128)(2,1)S(1)} %add_convert_fusion) | copy-start | bytes 1572868
  384.3 9.1 %collective-permute-start.14 = (bf16[128,1024]{1,0:T(8,128)(2,1)}, bf16[128,1024]{1,0:T(8,128)(2,1)}, u32[]{:S(2)}, u32[]{:S(2)}) collective-permute-start(bf16[128,1024]{1,0:T(8,128)(2,1)} %get-tuple-element.23), channel_id=1, source_target_pairs={{8,0},{9,1},{10,2},{11,3},{12,4},{13,5},{14,6},{15,7},{16,8},{17,9... | collective-permute-start | bytes 786440 | tf_op jit(solution)/shard_map/ppermute | solution.py:32
  384.3 27.5 %collective-permute-start.13 = (bf16[128,1024]{1,0:T(8,128)(2,1)}, bf16[128,1024]{1,0:T(8,128)(2,1)}, u32[]{:S(2)}, u32[]{:S(2)}) collective-permute-start(bf16[128,1024]{1,0:T(8,128)(2,1)} %get-tuple-element.24), channel_id=1, source_target_pairs={{16,0},{17,1},{18,2},{19,3},{20,4},{21,5},{22,6},{23,7},{24,8},{25... | collective-permute-start | bytes 786440 | tf_op jit(solution)/shard_map/ppermute | solution.py:32
  386.1 25.7 %collective-permute-start.12 = (bf16[128,1024]{1,0:T(8,128)(2,1)S(1)}, bf16[128,1024]{1,0:T(8,128)(2,1)}, u32[]{:S(2)}, u32[]{:S(2)}) collective-permute-start(bf16[128,1024]{1,0:T(8,128)(2,1)S(1)} %get-tuple-element.22), channel_id=1, source_target_pairs={{24,0},{25,1},{26,2},{27,3},{28,4},{29,5},{30,6},{31,7},{0,8},{1,9... | collective-permute-start | bytes 786440 | tf_op jit(solution)/shard_map/ppermute | solution.py:32
  388.2 23.7 %copy-start.2 = (bf16[1280,512]{1,0:T(8,128)(2,1)S(1)}, bf16[1280,512]{1,0:T(8,128)(2,1)}, u32[]{:S(2)}) copy-start(bf16[1280,512]{1,0:T(8,128)(2,1)} %get-tuple-element.34) | copy-start | bytes 3932164
  391.6 22.8 %collective-permute-start.17 = (bf16[128,1024]{1,0:T(8,128)(2,1)S(1)}, bf16[128,1024]{1,0:T(8,128)(2,1)S(1)}, u32[]{:S(2)}, u32[]{:S(2)}) collective-permute-start(bf16[128,1024]{1,0:T(8,128)(2,1)S(1)} %get-tuple-element.26), channel_id=1, source_target_pairs={{8,0},{9,1},{10,2},{11,3},{12,4},{13,5},{14,6},{15,7},{16,8},{17,9... | collective-permute-start | bytes 786440 | tf_op jit(solution)/shard_map/ppermute | solution.py:32
  393.4 38.3 %collective-permute-start.16 = (bf16[128,1024]{1,0:T(8,128)(2,1)S(1)}, bf16[128,1024]{1,0:T(8,128)(2,1)S(1)}, u32[]{:S(2)}, u32[]{:S(2)}) collective-permute-start(bf16[128,1024]{1,0:T(8,128)(2,1)S(1)} %get-tuple-element.27), channel_id=1, source_target_pairs={{16,0},{17,1},{18,2},{19,3},{20,4},{21,5},{22,6},{23,7},{24,8},{25... | collective-permute-start | bytes 786440 | tf_op jit(solution)/shard_map/ppermute | solution.py:32
  393.4 38.3 %collective-permute-start.15 = (bf16[128,1024]{1,0:T(8,128)(2,1)S(1)}, bf16[128,1024]{1,0:T(8,128)(2,1)S(1)}, u32[]{:S(2)}, u32[]{:S(2)}) collective-permute-start(bf16[128,1024]{1,0:T(8,128)(2,1)S(1)} %get-tuple-element.25), channel_id=1, source_target_pairs={{24,0},{25,1},{26,2},{27,3},{28,4},{29,5},{30,6},{31,7},{0,8},{1,9... | collective-permute-start | bytes 786440 | tf_op jit(solution)/shard_map/ppermute | solution.py:32
  414.3 19.8 %copy-start.5 = (bf16[128,2048]{1,0:T(8,128)(2,1)S(1)}, bf16[128,2048]{1,0:T(8,128)(2,1)}, u32[]{:S(2)}) copy-start(bf16[128,2048]{1,0:T(8,128)(2,1)} %copy-done.4) | copy-start | bytes 1572868
